TPU v7x, 32 devices: a whole 2x2x4 slice. The times are simulated.
32 devices in a mesh: dp: 8 (over z, core), seq: 4 (over y, x).
Axes of the slice: x: 2, y: 2, z: 4, core: 2. Of those that a mesh axis runs over, the one named last changes fastest.
Arguments:
- latents: bfloat16 [2, 16, 1024, 1152], P(None, 'dp', 'seq'), may hold values from -6 to 6
- condition: bfloat16 [2, 16, 1152], P(None, 'dp'), may hold values from -6 to 6
- cotangent: bfloat16 [2, 16, 1024, 1152], P(None, 'dp', 'seq'), may hold values from -6 to 6
- modulate_weight: bfloat16 [1152, 6912], P(('dp', 'seq')), may hold values from -0.1875 to 0.1875
- modulate_bias: bfloat16 [6912], P(('dp', 'seq')), may hold values from -1.796875 to 1.796875
- triple_weight: bfloat16 [1152, 3456], P(('dp', 'seq')), may hold values from -0.1875 to 0.1875
- triple_bias: bfloat16 [2304], P(('dp', 'seq')), may hold values from -1.796875 to 1.796875
- output_weight: bfloat16 [1152, 1152], P(('dp', 'seq')), may hold values from -3 to 3
- output_bias: bfloat16 [1152], P(('dp', 'seq')), may hold values from -1.796875 to 1.796875
- expand_weight: bfloat16 [1152, 4608], P(('dp', 'seq')), may hold values from -0.1875 to 0.1875
- expand_bias: bfloat16 [4608], P(('dp', 'seq')), may hold values from -3 to 3
- shrink_weight: bfloat16 [4608, 1152], P(('dp', 'seq')), may hold values from -0.09375 to 0.09375
- shrink_bias: bfloat16 [1152], P(('dp', 'seq')), may hold values from -1.796875 to 1.796875
Outputs:
- output: bfloat16 [2, 16, 1024, 1152], P(None, 'dp', 'seq')
- latents_gradient: float32 [2, 16, 1024, 1152], P(None, 'dp', 'seq')
- condition_gradient: float32 [2, 16, 1152], P(None, 'dp')
- modulate_weight_gradient: float32 [1152, 6912], P(('dp', 'seq'))
- modulate_bias_gradient: float32 [6912], P(('dp', 'seq'))
- triple_weight_gradient: float32 [1152, 3456], P(('dp', 'seq'))
- triple_bias_gradient: float32 [2304], P(('dp', 'seq'))
- output_weight_gradient: float32 [1152, 1152], P(('dp', 'seq'))
- output_bias_gradient: float32 [1152], P(('dp', 'seq'))
- expand_weight_gradient: float32 [1152, 4608], P(('dp', 'seq'))
- expand_bias_gradient: float32 [4608], P(('dp', 'seq'))
- shrink_weight_gradient: float32 [4608, 1152], P(('dp', 'seq'))
- shrink_bias_gradient: float32 [1152], P(('dp', 'seq'))
All inputs are finite; a program needn't handle non-finite values.
Results may differ from a plain program's by a relative error of at most 0.013.
The roundings to bfloat16 on the way count: a program that leaves them out, or rounds other values in their place, can miss the bound.
Values may be sent and summed in bfloat16 or wider, within the bound.
A program may use at most 384 MiB of HBM per device.

v0:
```python
import jax
import jax.numpy as jnp
from jax import lax
from jax.sharding import PartitionSpec as P

HEADS = 16
HD = 72


EPSILON = 1e-06
GELU_COEF = 0.7978845608028654
CUBIC = 0.044715


def gelu_tanh(values):
    return 0.5 * values * (1.0 + jnp.tanh(GELU_COEF * (values + CUBIC * values * values * values)))


def gelu_slope(values):
    tangent = jnp.tanh(GELU_COEF * (values + CUBIC * values * values * values))
    return 0.5 * (1.0 + tangent) + 0.5 * values * (1.0 - tangent * tangent) * GELU_COEF * (
        1.0 + 3.0 * CUBIC * values * values
    )


def norm_parts(values):
    centered = values - jnp.mean(values, axis=-1, keepdims=True)
    variance = jnp.mean(centered * centered, axis=-1, keepdims=True)
    inverse = lax.rsqrt(variance + EPSILON)
    return (centered * inverse, inverse)


def norm_back(incoming, normed, inverse, scaling):
    shift_grad = jnp.sum(incoming, axis=1)
    scale_grad = jnp.sum(incoming * normed, axis=1)
    normed_grad = incoming * (1.0 + scaling)
    mean_first = jnp.mean(normed_grad, axis=-1, keepdims=True)
    mean_second = jnp.mean(normed_grad * normed, axis=-1, keepdims=True)
    return (inverse * (normed_grad - mean_first - normed * mean_second), shift_grad, scale_grad)


def split_heads(values):
    return values.reshape(values.shape[0], HEADS, HD)


def attend_forward(operands):
    queries, keys_all, values_all = operands
    scores = jnp.einsum(
        "qhd,khd->hqk",
        split_heads(queries),
        split_heads(keys_all),
        preferred_element_type=jnp.float32,
    ) * HD ** (-0.5)
    row_peak = jnp.max(scores, axis=-1, keepdims=True)
    log_total = row_peak + jnp.log(jnp.sum(jnp.exp(scores - row_peak), axis=-1, keepdims=True))
    soft_weights = jnp.exp(scores - log_total).astype(jnp.bfloat16)
    mixed_heads = jnp.einsum(
        "hqk,khd->qhd", soft_weights, split_heads(values_all), preferred_element_type=jnp.float32
    )
    return (mixed_heads.reshape(queries.shape).astype(jnp.bfloat16), log_total)


def attend_query_side(operands):
    queries, keys_all, values_all, incoming, log_total = operands
    per_head_keys = split_heads(keys_all)
    scores = jnp.einsum(
        "qhd,khd->hqk", split_heads(queries), per_head_keys, preferred_element_type=jnp.float32
    ) * HD ** (-0.5)
    soft_exact = jnp.exp(scores - log_total)
    prob_grad = jnp.einsum(
        "qhd,khd->hqk",
        split_heads(incoming),
        split_heads(values_all),
        preferred_element_type=jnp.float32,
    )
    centre = jnp.sum(prob_grad * soft_exact, axis=-1, keepdims=True)
    score_grad = (soft_exact * (prob_grad - centre) * HD ** (-0.5)).astype(jnp.bfloat16)
    query_grad = (
        jnp.einsum("hqk,khd->qhd", score_grad, per_head_keys, preferred_element_type=jnp.float32)
        .reshape(queries.shape)
        .astype(jnp.bfloat16)
    )
    return (query_grad, centre)


def attend_key_side(operands):
    queries_all, incoming_all, log_all, centre_all, key_rows, value_rows = operands
    query_heads = split_heads(queries_all)
    incoming_heads = split_heads(incoming_all)
    scores = jnp.einsum(
        "qhd,khd->hqk", query_heads, split_heads(key_rows), preferred_element_type=jnp.float32
    ) * HD ** (-0.5)
    soft_exact = jnp.exp(scores - log_all)
    prob_grad = jnp.einsum(
        "qhd,khd->hqk", incoming_heads, split_heads(value_rows), preferred_element_type=jnp.float32
    )
    score_grad = (soft_exact * (prob_grad - centre_all) * HD ** (-0.5)).astype(jnp.bfloat16)
    key_grad = jnp.einsum(
        "hqk,qhd->khd", score_grad, query_heads, preferred_element_type=jnp.float32
    ).reshape(key_rows.shape)
    value_grad = jnp.einsum(
        "hqk,qhd->khd",
        soft_exact.astype(jnp.bfloat16),
        incoming_heads,
        preferred_element_type=jnp.float32,
    ).reshape(value_rows.shape)
    return (key_grad, value_grad)


def accumulate(running, fresh):
    if running is None:
        return fresh
    return tuple((total_term + new_term for total_term, new_term in zip(running, fresh)))


def on_device(
    latents,
    condition,
    cotangent,
    modulate_weight,
    modulate_bias,
    triple_weight,
    triple_bias,
    output_weight,
    output_bias,
    expand_weight,
    expand_bias,
    shrink_weight,
    shrink_bias,
):
    micro_count = latents.shape[0]
    features = latents.shape[3]
    first_seq = (lax.axis_index("seq") == 0).astype(jnp.bfloat16)
    output_rows = []
    latent_grads = []
    condition_grads = []
    running = None
    for batch_index in range(micro_count):
        gathered = (
            lax.all_gather(modulate_weight, ("dp", "seq"), axis=0, tiled=True),
            lax.all_gather(modulate_bias, ("dp", "seq"), axis=0, tiled=True),
            lax.all_gather(triple_weight, ("dp", "seq"), axis=0, tiled=True),
            lax.all_gather(triple_bias, ("dp", "seq"), axis=0, tiled=True),
            lax.all_gather(output_weight, ("dp", "seq"), axis=0, tiled=True),
            lax.all_gather(output_bias, ("dp", "seq"), axis=0, tiled=True),
            lax.all_gather(expand_weight, ("dp", "seq"), axis=0, tiled=True),
            lax.all_gather(expand_bias, ("dp", "seq"), axis=0, tiled=True),
            lax.all_gather(shrink_weight, ("dp", "seq"), axis=0, tiled=True),
            lax.all_gather(shrink_bias, ("dp", "seq"), axis=0, tiled=True),
        )
        (
            modulate_full,
            modulate_offset,
            triple_full,
            triple_offset,
            output_full,
            output_offset,
            expand_weight_joined,
            expand_offset,
            shrink_weight_joined,
            shrink_offset,
        ) = gathered
        latent_float = latents[batch_index].astype(jnp.float32)
        cond_float = condition[batch_index].astype(jnp.float32)
        cond_act = jax.nn.silu(cond_float).astype(jnp.bfloat16)
        modulation = jnp.dot(
            cond_act, modulate_full, preferred_element_type=jnp.float32
        ) + modulate_offset.astype(jnp.float32)
        shift_one, scale_one, gate_one, shift_two, scale_two, gate_two = jnp.split(
            modulation[:, None, :], 6, axis=-1
        )
        normed_one, inverse_one = norm_parts(latent_float)
        hidden_one = (normed_one * (1.0 + scale_one) + shift_one).astype(jnp.bfloat16)
        projected = jnp.einsum(
            "lsd,de->lse", hidden_one, triple_full, preferred_element_type=jnp.float32
        )
        queries = (projected[..., :features] + triple_offset[:features].astype(jnp.float32)).astype(
            jnp.bfloat16
        )
        key_rows = projected[..., features : 2 * features].astype(jnp.bfloat16)
        value_rows = (
            projected[..., 2 * features :] + triple_offset[features:].astype(jnp.float32)
        ).astype(jnp.bfloat16)
        keys_all, values_all = (
            lax.all_gather(key_rows, "seq", axis=1, tiled=True),
            lax.all_gather(value_rows, "seq", axis=1, tiled=True),
        )
        mixed, log_total = lax.map(attend_forward, (queries, keys_all, values_all))
        branch_one = jnp.einsum(
            "lsd,de->lse", mixed, output_full, preferred_element_type=jnp.float32
        ) + output_offset.astype(jnp.float32)
        middle = latent_float + gate_one * branch_one
        normed_two, inverse_two = norm_parts(middle)
        second_hidden = (normed_two * (1.0 + scale_two) + shift_two).astype(jnp.bfloat16)
        pre_act = jnp.einsum(
            "gin,no->gio", second_hidden, expand_weight_joined, preferred_element_type=jnp.float32
        ) + expand_offset.astype(jnp.float32)
        activated_hidden = gelu_tanh(pre_act).astype(jnp.bfloat16)
        branch_two = jnp.einsum(
            "gyv,vc->gyc",
            activated_hidden,
            shrink_weight_joined,
            preferred_element_type=jnp.float32,
        ) + shrink_offset.astype(jnp.float32)
        output_rows.append((middle + gate_two * branch_two).astype(jnp.bfloat16))
        gathered_again = (
            lax.all_gather(modulate_weight, ("dp", "seq"), axis=0, tiled=True),
            lax.all_gather(modulate_bias, ("dp", "seq"), axis=0, tiled=True),
            lax.all_gather(triple_weight, ("dp", "seq"), axis=0, tiled=True),
            lax.all_gather(triple_bias, ("dp", "seq"), axis=0, tiled=True),
            lax.all_gather(output_weight, ("dp", "seq"), axis=0, tiled=True),
            lax.all_gather(output_bias, ("dp", "seq"), axis=0, tiled=True),
            lax.all_gather(expand_weight, ("dp", "seq"), axis=0, tiled=True),
            lax.all_gather(expand_bias, ("dp", "seq"), axis=0, tiled=True),
            lax.all_gather(shrink_weight, ("dp", "seq"), axis=0, tiled=True),
            lax.all_gather(shrink_bias, ("dp", "seq"), axis=0, tiled=True),
        )
        modulate_full = gathered_again[0]
        triple_full = gathered_again[2]
        output_full = gathered_again[4]
        expand_weight_joined = gathered_again[6]
        shrink_weight_joined = gathered_again[8]
        incoming = cotangent[batch_index].astype(jnp.float32)
        second_branch_gradient = (gate_two * incoming).astype(jnp.bfloat16)
        gate_grad_two = jnp.sum(incoming * branch_two, axis=1)
        shrink_offset_grad = jnp.sum(second_branch_gradient.astype(jnp.float32), axis=(0, 1))
        shrink_full_grad = jnp.einsum(
            "ceh,cea->ha",
            activated_hidden,
            second_branch_gradient,
            preferred_element_type=jnp.float32,
        )
        act_grad = jnp.einsum(
            "net,pt->nep",
            second_branch_gradient,
            shrink_weight_joined,
            preferred_element_type=jnp.float32,
        )
        preactivation_gradient = (act_grad * gelu_slope(pre_act)).astype(jnp.bfloat16)
        expand_offset_grad = jnp.sum(preactivation_gradient.astype(jnp.float32), axis=(0, 1))
        expand_full_grad = jnp.einsum(
            "ztx,ztb->xb", second_hidden, preactivation_gradient, preferred_element_type=jnp.float32
        )
        hidden_grad_two = jnp.einsum(
            "vgc,jc->vgj",
            preactivation_gradient,
            expand_weight_joined,
            preferred_element_type=jnp.float32,
        )
        norm_grad_two, shift_grad_two, scale_grad_two = norm_back(
            hidden_grad_two, normed_two, inverse_two, scale_two
        )
        middle_grad = incoming + norm_grad_two
        branch_grad_one = (gate_one * middle_grad).astype(jnp.bfloat16)
        gate_grad_one = jnp.sum(middle_grad * branch_one, axis=1)
        output_offset_grad = jnp.sum(branch_grad_one.astype(jnp.float32), axis=(0, 1))
        output_full_grad = jnp.einsum(
            "lsd,lse->de", mixed, branch_grad_one, preferred_element_type=jnp.float32
        )
        mixed_grad = jnp.einsum(
            "lse,de->lsd", branch_grad_one, output_full, preferred_element_type=jnp.float32
        ).astype(jnp.bfloat16)
        query_grad, centre = lax.map(
            attend_query_side, (queries, keys_all, values_all, mixed_grad, log_total)
        )
        queries_all, incoming_all = (
            lax.all_gather(queries, "seq", axis=1, tiled=True),
            lax.all_gather(mixed_grad, "seq", axis=1, tiled=True),
        )
        log_all, centre_all = (
            lax.all_gather(log_total, "seq", axis=2, tiled=True),
            lax.all_gather(centre, "seq", axis=2, tiled=True),
        )
        key_grad, value_grad = lax.map(
            attend_key_side, (queries_all, incoming_all, log_all, centre_all, key_rows, value_rows)
        )
        key_grad = key_grad.astype(jnp.bfloat16)
        value_grad = value_grad.astype(jnp.bfloat16)
        triple_grad = jnp.concatenate([query_grad, key_grad, value_grad], axis=-1)
        triple_offset_grad = jnp.concatenate(
            [
                jnp.sum(query_grad.astype(jnp.float32), axis=(0, 1)),
                jnp.sum(value_grad.astype(jnp.float32), axis=(0, 1)),
            ]
        )
        triple_full_grad = jnp.einsum(
            "lsd,lse->de", hidden_one, triple_grad, preferred_element_type=jnp.float32
        )
        hidden_grad_one = jnp.einsum(
            "lse,de->lsd", triple_grad, triple_full, preferred_element_type=jnp.float32
        )
        norm_grad_one, shift_grad_one, scale_grad_one = norm_back(
            hidden_grad_one, normed_one, inverse_one, scale_one
        )
        latent_grads.append(middle_grad + norm_grad_one)
        modulate_partial = jnp.concatenate(
            [
                shift_grad_one,
                scale_grad_one,
                gate_grad_one,
                shift_grad_two,
                scale_grad_two,
                gate_grad_two,
            ],
            axis=-1,
        )
        modulate_total = lax.psum(modulate_partial.astype(jnp.bfloat16), "seq")
        sigmoid_cond = jax.nn.sigmoid(cond_float)
        silu_slope = sigmoid_cond * (1.0 + cond_float * (1.0 - sigmoid_cond))
        cond_back = lax.dot_general(
            modulate_total,
            modulate_full,
            (((1,), (1,)), ((), ())),
            preferred_element_type=jnp.float32,
        )
        condition_grads.append(cond_back * silu_slope)
        owned_total = modulate_total * first_seq
        modulate_full_grad = jnp.einsum(
            "le,lf->ef", cond_act, owned_total, preferred_element_type=jnp.float32
        )
        modulate_offset_grad = jnp.sum(owned_total.astype(jnp.float32), axis=0)
        shard_grads = (
            lax.psum_scatter(modulate_full_grad, ("dp", "seq"), scatter_dimension=0, tiled=True),
            lax.psum_scatter(modulate_offset_grad, ("dp", "seq"), scatter_dimension=0, tiled=True),
            lax.psum_scatter(triple_full_grad, ("dp", "seq"), scatter_dimension=0, tiled=True),
            lax.psum_scatter(triple_offset_grad, ("dp", "seq"), scatter_dimension=0, tiled=True),
            lax.psum_scatter(output_full_grad, ("dp", "seq"), scatter_dimension=0, tiled=True),
            lax.psum_scatter(output_offset_grad, ("dp", "seq"), scatter_dimension=0, tiled=True),
            lax.psum_scatter(expand_full_grad, ("dp", "seq"), scatter_dimension=0, tiled=True),
            lax.psum_scatter(expand_offset_grad, ("dp", "seq"), scatter_dimension=0, tiled=True),
            lax.psum_scatter(shrink_full_grad, ("dp", "seq"), scatter_dimension=0, tiled=True),
            lax.psum_scatter(shrink_offset_grad, ("dp", "seq"), scatter_dimension=0, tiled=True),
        )
        running = accumulate(running, shard_grads)
    return (
        jnp.stack(output_rows),
        jnp.stack(latent_grads),
        jnp.stack(condition_grads),
        running[0],
        running[1],
        running[2],
        running[3],
        running[4],
        running[5],
        running[6],
        running[7],
        running[8],
        running[9],
    )


def solution(mesh):
    placed = (
        P(None, "dp", "seq", None),
        P(None, "dp", None),
        P(None, "dp", "seq", None),
        P(("dp", "seq"), None),
        P(("dp", "seq")),
        P(("dp", "seq"), None),
        P(("dp", "seq")),
        P(("dp", "seq"), None),
        P(("dp", "seq")),
        P(("dp", "seq"), None),
        P(("dp", "seq")),
        P(("dp", "seq"), None),
        P(("dp", "seq")),
    )
    return jax.shard_map(
        on_device,
        mesh=mesh,
        in_specs=placed,
        out_specs=(
            P(None, "dp", "seq", None),
            P(None, "dp", "seq", None),
            P(None, "dp", None),
            P(("dp", "seq"), None),
            P(("dp", "seq")),
            P(("dp", "seq"), None),
            P(("dp", "seq")),
            P(("dp", "seq"), None),
            P(("dp", "seq")),
            P(("dp", "seq"), None),
            P(("dp", "seq")),
            P(("dp", "seq"), None),
            P(("dp", "seq")),
        ),
        check_vma=False,
    )
```

profile of v0, /device:TPU:0, one launch (start us, length us, event | category | flops | bytes accessed | tf_op | source)
XLA Modules:
  0.0 3587.8 jit_solution(14305368099570282794)
XLA Ops:
  14.3 43.4 %all-reduce.19 = (bf16[6912]{0:T(1024)(128)(2,1)S(1)}, bf16[2304]{0:T(1024)(128)(2,1)S(1)}, bf16[1152]{0:T(1024)(128)(2,1)}, bf16[1152]{0:T(1024)(128)(2,1)}, bf16[4608]{0:T(1024)(128)(2,1)}) all-reduce(bf16[6912]{0:T(1024)(128)(2,1)S(1)} %dynamic-update-slice, ...), channel_id=1, replica_groups=mesh['dp'=8,'seq'=4] {'dp','seq'}, use_global_device_ids=true, to_apply=%add | all-reduce | flops 16128 | bytes 64512
  60.6 32.6 all-gather.38.cloned.1.call-done
  105.8 108.3 %all-gather.36.cloned.1.call-done = bf16[32,36,6912]{2,1,0:T(8,128)(2,1)} async-done(((bf16[1,36,6912]{2,1,0:T(8,128)(2,1)}), bf16[32,36,6912]{2,1,0:T(8,128)(2,1)}) %all-gather.36.cloned.1.call-update) | async-done | bytes 15925264 | tf_op jit(solution)/shard_map/all_gather | solution.py:140
  280.3 87.7 %all-gather.42.cloned.1.call-done = bf16[32,36,4608]{2,1,0:T(8,128)(2,1)} async-done(((bf16[1,36,4608]{2,1,0:T(8,128)(2,1)}), bf16[32,36,4608]{2,1,0:T(8,128)(2,1)}) %all-gather.42.cloned.1.call-update) | async-done | bytes 10616848 | tf_op jit(solution)/shard_map/all_gather | solution.py:146
  383.7 41.4 %all-gather.24.cloned.1.call-done = bf16[2,1024,1152]{2,1,0:T(8,128)(2,1)} async-done(((bf16[2,256,1152]{2,1,0:T(8,128)(2,1)}), bf16[2,1024,1152]{2,1,0:T(8,128)(2,1)}) %all-gather.24.cloned.1.call-update) | async-done | bytes 4718608 | tf_op jit(solution)/shard_map/all_gather | solution.py:186
  431.7 52.2 %all-gather.26.cloned.1.call-done = bf16[2,1024,1152]{2,1,0:T(8,128)(2,1)} async-done(((bf16[2,256,1152]{2,1,0:T(8,128)(2,1)}), bf16[2,1024,1152]{2,1,0:T(8,128)(2,1)}) %all-gather.26.cloned.1.call-update) | async-done | bytes 4718608 | tf_op jit(solution)/shard_map/all_gather | solution.py:185
  491.3 28.1 while.73
  519.4 23.5 all-gather.18.cloned.1.call-done
  549.5 52.3 %all-gather.20.cloned.1.call-done = bf16[2,1024,1152]{2,1,0:T(8,128)(2,1)} async-done(((bf16[2,256,1152]{2,1,0:T(8,128)(2,1)}), bf16[2,1024,1152]{2,1,0:T(8,128)(2,1)}) %all-gather.20.cloned.1.call-update) | async-done | bytes 4718608 | tf_op jit(solution)/shard_map/all_gather | solution.py:185
  609.1 36.3 %while.72 = (s32[]{:T(128)}, bf16[2,256,1152]{1,2,0:T(8,128)(2,1)S(1)}, f32[2,16,256,1]{2,1,3,0:T(8,128)}, bf16[2,1024,1152]{1,2,0:T(8,128)(2,1)}, bf16[2,256,11...) while((s32[]{:T(128)}, bf16[2,256,1152]{1,2,0:T(8,128)(2,1)S(1)}, ...), condition=%wide.region_5.6_spmd, body=%wide.region_2.5_spmd.sunk | while | flops 1241804800 | bytes 68157536 | solution.py:188
  666.7 25.3 all-gather.22.cloned.1.call-done
  773.3 83.7 %while.76 = (s32[]{:T(128)}, bf16[2,256,1152]{1,2,0:T(8,128)(2,1)}, f32[2,16,256,1]{2,1,3,0:T(8,128)}, bf16[2,1024,1152]{1,2,0:T(8,128)(2,1)}, bf16[2,256,1152]{...) while((s32[]{:T(128)}, bf16[2,256,1152]{1,2,0:T(8,128)(2,1)}, ...), condition=%wide.region_29.30_spmd, body=%wide.region_27.29_spmd.sunk | while | flops 1854173184 | bytes 121438472 | solution.py:263
  893.7 83.1 %while.74 = (s32[]{:T(128)}, bf16[2,256,1152]{1,2,0:T(8,128)(2,1)}, f32[2,16,256,1]{2,1,3,0:T(8,128)}, bf16[2,1024,1152]{1,2,0:T(8,128)(2,1)}, bf16[2,256,1152]{...) while((s32[]{:T(128)}, bf16[2,256,1152]{1,2,0:T(8,128)(2,1)}, ...), condition=%wide.region_20.21_spmd, body=%wide.region_18.20_spmd.sunk | while | flops 1854173184 | bytes 121438472 | solution.py:263
  1099.6 99.4 %while.77 = (s32[]{:T(128)}, bf16[2,256,1152]{2,1,0:T(8,128)(2,1)}, bf16[2,256,1152]{2,1,0:T(8,128)(2,1)}, bf16[2,1024,1152]{2,1,0:T(8,128)(2,1)}, bf16[2,256,11...) while((s32[]{:T(128)}, bf16[2,256,1152]{2,1,0:T(8,128)(2,1)}, ...), condition=%wide.region_31.32_spmd, body=%wide.region_30.31_spmd.sunk | while | flops 2453667840 | bytes 100335768 | solution.py:274
  1201.2 96.7 %while.75 = (s32[]{:T(128)}, bf16[2,256,1152]{2,1,0:T(8,128)(2,1)}, bf16[2,256,1152]{2,1,0:T(8,128)(2,1)}, bf16[2,1024,1152]{2,1,0:T(8,128)(2,1)}, bf16[2,256,11...) while((s32[]{:T(128)}, bf16[2,256,1152]{2,1,0:T(8,128)(2,1)}, ...), condition=%wide.region_22.23_spmd, body=%wide.region_21.22_spmd.sunk | while | flops 2453667840 | bytes 100335768 | solution.py:274
  1365.1 23.5 convolution_add_fusion
  1388.7 854.5 %fusion.171 = (f32[40,6912]{1,0:T(8,128)}, f32[48,1152]{1,0:T(8,128)}) fusion(f32[1152,6912]{1,0:T(8,128)} %convolution_add_fusion, f32[1152,1152]{1,0:T(8,128)} %fusion.61), kind=kCustom, calls=%all-reduce-scatter.4 | all-reduce-scatter fusion | flops 10616834 | bytes 38486016
  2244.8 33.3 collective-permute-start.18
  2310.2 922.3 %fusion.172 = (f32[48,3456]{1,0:T(8,128)S(1)}, f32[40,4608]{1,0:T(8,128)}) fusion(f32[1152,3456]{1,0:T(8,128)} %fusion.38, f32[1152,4608]{1,0:T(8,128)} %fusion.37), kind=kCustom, calls=%all-reduce-scatter.5 | all-reduce-scatter fusion | flops 11206658 | bytes 38559744
  3233.4 25.2 collective-permute-start.23
  3327.0 30.7 collective-permute-start.6
  3384.3 77.3 %all-reduce.18 = (f32[6912]{0:T(1024)}, f32[2304]{0:T(1024)}, f32[1152]{0:T(1024)}, f32[4608]{0:T(1024)}, f32[1152]{0:T(1024)}) all-reduce(f32[6912]{0:T(1024)} %add.436, f32[2304]{0:T(1024)S(1)} %maximum_add_fusion, f32[1152]{0:T(1024)} %add.440, f32[4608]{0:T(1024)} %add.442, ...), channel_id=13, replica_groups=mesh['dp'=8,'seq'=4] {'dp','seq'}, use_global_device_ids=true, to_apply=%region_51.52.clone | all-reduce | flops 16128 | bytes 129024
  3496.3 36.1 %concatenate.27 = f32[420,3456]{1,0:T(8,128)} concatenate(f32[36,3456]{1,0:T(8,128)} %collective-permute-done.11, f32[48,3456]{1,0:T(8,128)S(1)} %copy-done.54, f32[48,3456]{1,0:T(8,128)} %copy-done.55, f32[48,3456]{1,0:T(8,128)} %copy-done.56, f32[48,3456]{1,0:T(8,128)} %copy-done.57, f32[48,3456]{1,0:T(8,128)} %copy-done.58, f32[48,3456]{1,0:T(8,128)} %collective-permute-done.5, ...), dimensions={0} | concatenate | bytes 11612160
  3556.8 21.7 concatenate.26
  (689 shorter events, 1069.8 us)
Async XLA Ops:
  7.2 86.1 %all-gather.38.cloned.1.call-start = ((), (), s32[]{:S(2)}) async-start(), calls=%async_computation.12 | async-start | bytes 9123840 | tf_op jit(solution)/shard_map/all_gather | solution.py:142
  7.9 206.2 %all-gather.36.cloned.1.call-start = ((), (), s32[]{:S(2)}) async-start(), calls=%async_computation.11 | async-start | bytes 18247680 | tf_op jit(solution)/shard_map/all_gather | solution.py:140
  8.7 266.5 %all-gather.40.cloned.1.call-start = ((), (), s32[]{:S(2)}) async-start(), calls=%async_computation.13 | async-start | bytes 3041280 | tf_op jit(solution)/shard_map/all_gather | solution.py:144
  9.4 358.6 %all-gather.42.cloned.1.call-start = ((), (), s32[]{:S(2)}) async-start(), calls=%async_computation.14 | async-start | bytes 12165120 | tf_op jit(solution)/shard_map/all_gather | solution.py:146
  10.0 415.1 %all-gather.24.cloned.1.call-start = ((), (), s32[]{:S(2)}) async-start(), calls=%async_computation.4 | async-start | bytes 5898240 | tf_op jit(solution)/shard_map/all_gather | solution.py:186
  265.7 218.2 %all-gather.26.cloned.1.call-start = ((), (), s32[]{:S(2)}) async-start(), calls=%async_computation.5 | async-start | bytes 5898240 | tf_op jit(solution)/shard_map/all_gather | solution.py:185
  269.4 273.4 %all-gather.18.cloned.1.call-start = ((), (), s32[]{:S(2)}) async-start(), calls=%async_computation.1 | async-start | bytes 5898240 | tf_op jit(solution)/shard_map/all_gather | solution.py:186
  270.2 331.6 %all-gather.20.cloned.1.call-start = ((), (), s32[]{:S(2)}) async-start(), calls=%async_computation.2 | async-start | bytes 5898240 | tf_op jit(solution)/shard_map/all_gather | solution.py:185
  273.2 418.9 %all-gather.22.cloned.1.call-start = ((), (), s32[]{:S(2)}) async-start(), calls=%async_computation.3 | async-start | bytes 10948608 | tf_op jit(solution)/shard_map/all_gather | solution.py:148
  273.9 823.3 %all-gather.32.cloned.1.call-start = ((), (), s32[]{:S(2)}) async-start(), calls=%async_computation.8 | async-start | bytes 5898240 | tf_op jit(solution)/shard_map/all_gather | solution.py:267
  383.6 713.6 %all-gather.34.cloned.1.call-start = ((), (), s32[]{:S(2)}) async-start(), calls=%async_computation.9 | async-start | bytes 5898240 | tf_op jit(solution)/shard_map/all_gather | solution.py:268
  728.1 470.9 %all-gather.28.cloned.1.call-start = ((), (), s32[]{:S(2)}) async-start(), calls=%async_computation.6 | async-start | bytes 5898240 | tf_op jit(solution)/shard_map/all_gather | solution.py:267
  728.8 470.2 %all-gather.30.cloned.1.call-start = ((), (), s32[]{:S(2)}) async-start(), calls=%async_computation.7 | async-start | bytes 5898240 | tf_op jit(solution)/shard_map/all_gather | solution.py:268
  1024.3 2556.5 %reduce-scatter.10.cloned.1.call-start = ((), (), s32[]{:S(2)}) async-start(), calls=%async_computation.10 | async-start | bytes 21897216 | tf_op jit(solution)/shard_map/reduce_scatter | solution.py:331
  2244.8 1042.9 %collective-permute-start.18 = (f32[48,1152]{1,0:T(8,128)}, f32[48,1152]{1,0:T(8,128)}, u32[]{:S(2)}, u32[]{:S(2)}) collective-permute-start(f32[48,1152]{1,0:T(8,128)} %get-tuple-element.591), channel_id=1, source_target_pairs={{0,7},{1,8},{2,9},{3,10},{4,11},{5,12},{6,13},{7,14},{8,15},{9,16}... | collective-permute-start | bytes 663560
  2278.1 1005.7 %collective-permute-start.19 = (f32[36,1152]{1,0:T(8,128)}, f32[36,1152]{1,0:T(8,128)}, u32[]{:S(2)}, u32[]{:S(2)}) collective-permute-start(f32[36,1152]{1,0:T(8,128)} %slice.70), channel_id=1, source_target_pairs={{0,8},{1,9},{2,10},{3,11},{4,12},{5,13},{6,14},{7,15},{8,16},{9,17... | collective-permute-start | bytes 497672
  3287.7 70.0 %collective-permute-start.10 = (f32[48,3456]{1,0:T(8,128)S(1)}, f32[48,3456]{1,0:T(8,128)S(1)}, u32[]{:S(2)}, u32[]{:S(2)}) collective-permute-start(f32[48,3456]{1,0:T(8,128)S(1)} %get-tuple-element.594), channel_id=1, source_target_pairs={{0,7},{1,8},{2,9},{3,10},{4,11},{5,12},{6,13},{7,14},{8,15},{9,16}... | collective-permute-start | bytes 1990664
  3357.7 132.9 %collective-permute-start.22 = (f32[40,4608]{1,0:T(8,128)}, f32[40,4608]{1,0:T(8,128)}, u32[]{:S(2)}, u32[]{:S(2)}) collective-permute-start(f32[40,4608]{1,0:T(8,128)} %get-tuple-element.595), channel_id=1, source_target_pairs={{0,3},{1,4},{2,5},{3,6},{4,7},{5,8},{6,9},{7,10},{8,11},{9,12},{10... | collective-permute-start | bytes 2211848
  3363.0 119.9 %collective-permute-start.5 = (f32[48,3456]{1,0:T(8,128)S(1)}, f32[48,3456]{1,0:T(8,128)}, u32[]{:S(2)}, u32[]{:S(2)}) collective-permute-start(f32[48,3456]{1,0:T(8,128)S(1)} %get-tuple-element.594), channel_id=1, source_target_pairs={{0,2},{1,3},{2,4},{3,5},{4,6},{5,7},{6,8},{7,9},{8,10},{9,11},{10,... | collective-permute-start | bytes 1990664
  3367.7 120.5 %collective-permute-start.4 = (f32[48,3456]{1,0:T(8,128)S(1)}, f32[48,3456]{1,0:T(8,128)}, u32[]{:S(2)}, u32[]{:S(2)}) collective-permute-start(f32[48,3456]{1,0:T(8,128)S(1)} %get-tuple-element.594), channel_id=1, source_target_pairs={{0,1},{1,2},{2,3},{3,4},{4,5},{5,6},{6,7},{7,8},{8,9},{9,10},{10,1... | collective-permute-start | bytes 1990664
  3372.6 161.8 %collective-permute-start.21 = (f32[40,4608]{1,0:T(8,128)}, f32[40,4608]{1,0:T(8,128)}, u32[]{:S(2)}, u32[]{:S(2)}) collective-permute-start(f32[40,4608]{1,0:T(8,128)} %get-tuple-element.595), channel_id=1, source_target_pairs={{0,2},{1,3},{2,4},{3,5},{4,6},{5,7},{6,8},{7,9},{8,10},{9,11},{10,... | collective-permute-start | bytes 2211848
  3376.0 159.6 %collective-permute-start.20 = (f32[40,4608]{1,0:T(8,128)}, f32[40,4608]{1,0:T(8,128)}, u32[]{:S(2)}, u32[]{:S(2)}) collective-permute-start(f32[40,4608]{1,0:T(8,128)} %get-tuple-element.595), channel_id=1, source_target_pairs={{0,1},{1,2},{2,3},{3,4},{4,5},{5,6},{6,7},{7,8},{8,9},{9,10},{10,1... | collective-permute-start | bytes 2211848
  3482.9 73.8 %collective-permute-start.2 = (f32[40,6912]{1,0:T(8,128)S(1)}, f32[40,6912]{1,0:T(8,128)S(1)}, u32[]{:S(2)}, u32[]{:S(2)}) collective-permute-start(f32[40,6912]{1,0:T(8,128)S(1)} %copy-done.40), channel_id=1, source_target_pairs={{0,3},{1,4},{2,5},{3,6},{4,7},{5,8},{6,9},{7,10},{8,11},{9,12},{10... | collective-permute-start | bytes 3317768
  3488.2 68.5 %collective-permute-start.1 = (f32[40,6912]{1,0:T(8,128)S(1)}, f32[40,6912]{1,0:T(8,128)}, u32[]{:S(2)}, u32[]{:S(2)}) collective-permute-start(f32[40,6912]{1,0:T(8,128)S(1)} %copy-done.40), channel_id=1, source_target_pairs={{0,2},{1,3},{2,4},{3,5},{4,6},{5,7},{6,8},{7,9},{8,10},{9,11},{10,... | collective-permute-start | bytes 3317768
  (185 other events, 6511.2 us)
Sparse Core Ops, SparseCore 0:
  10.9 82.2 all-gather.37
  96.2 117.8 all-gather.35
  217.0 56.9 all-gather.39
  276.8 91.1 all-gather.41
  369.7 55.3 all-gather.23
  426.8 57.0 all-gather.25
  485.8 57.0 all-gather.17
  544.7 57.0 all-gather.19
  604.7 87.3 all-gather.21
  693.8 55.5 all-gather.31
  751.2 57.0 all-gather.33
  810.0 57.0 all-gather.27
  1024.4 55.7 all-gather.29
  1097.3 218.7 reduce-scatter.9
where the time goes:
time: 3600 us; the launch traced here: 3590 us
  blocking collectives  1950 us (54%)
  matrix products  601 us (17%)
  waiting for transfers between devices  443 us (12%)
  local copies, waits for them, and re-layouts  352 us (10%)
  starting transfers between devices  164 us (5%)
  other arithmetic  50 us (1%)
    unnamed x4, blocking collectives  1900 us
    unnamed x335, local copies, waits for them, and re-layouts  177 us
    unnamed x24, starting transfers between devices  164 us
    all_gather x1, waiting for transfers between devices, on_device(): lax.all_gather(modulate_weight, ('dp', 'seq'), axis=0, tiled=True)  108 us
    all_gather x2, waiting for transfers between devices, on_device(): lax.all_gather(key_rows, 'seq', axis=1, tiled=True)  104 us
    dynamic_slice x48, local copies, waits for them, and re-layouts, on_device(): mixed, log_total = lax.map(attend_forward, (queries, keys_all, values_all))  101 us
    all_gather x1, waiting for transfers between devices, on_device(): lax.all_gather(expand_weight, ('dp', 'seq'), axis=0, tiled=True)  87.7 us
  transfers between devices with their start and end apart: 38, of which 10 were waited for; matrix products, arithmetic and copies ran while one was open for 77% of the time, Pallas kernels for 0%

commit v1 on v0

v1 whole, which is shorter than its diff:
```python
import functools

import jax
import jax.numpy as jnp
from jax import lax
from jax.experimental import pallas as pl
from jax.experimental.pallas import tpu as pltpu
from jax.sharding import PartitionSpec as P

HEADS = 16
HD = 72
LANES = 128
WINDOW = 256
QUERY_BLOCK = 256

EPSILON = 1e-06
GELU_COEF = 0.7978845608028654
CUBIC = 0.044715
LOG2E = 1.4426950408889634
AXES = ("dp", "seq")
F32 = jnp.float32
BF16 = jnp.bfloat16


def gelu_parts(values):
    square = values * values
    tangent = jnp.tanh(GELU_COEF * values * (1.0 + CUBIC * square))
    half = 0.5 * (1.0 + tangent)
    slope = half + (0.5 * GELU_COEF) * values * (1.0 - tangent * tangent) * (1.0 + 3.0 * CUBIC * square)
    return (values * half, slope)


def norm_parts(values):
    centered = values - jnp.mean(values, axis=-1, keepdims=True)
    variance = jnp.mean(centered * centered, axis=-1, keepdims=True)
    inverse = lax.rsqrt(variance + EPSILON)
    return (centered * inverse, inverse)


def norm_back(incoming, normed, inverse, scaling):
    shift_grad = jnp.sum(incoming, axis=1)
    scale_grad = jnp.sum(incoming * normed, axis=1)
    normed_grad = incoming * (1.0 + scaling)
    mean_first = jnp.mean(normed_grad, axis=-1, keepdims=True)
    mean_second = jnp.mean(normed_grad * normed, axis=-1, keepdims=True)
    return (inverse * (normed_grad - mean_first - normed * mean_second), shift_grad, scale_grad)


def dot_nt(left, right):
    return lax.dot_general(left, right, (((1,), (1,)), ((), ())), preferred_element_type=F32)


def dot_tn(left, right):
    return lax.dot_general(left, right, (((0,), (0,)), ((), ())), preferred_element_type=F32)


def dot_nn(left, right):
    return jnp.dot(left, right, preferred_element_type=F32)


def head_window(features):
    head = pl.program_id(0)
    last = features // LANES - WINDOW // LANES
    tile = jnp.minimum(head * HD // LANES, last)
    start = pl.multiple_of(tile * LANES, LANES)
    first = head * HD - start
    lane = lax.broadcasted_iota(jnp.int32, (1, WINDOW), 1)
    return start, (lane >= first) & (lane < first + HD)


def attend_forward_kernel(query_ref, key_ref, value_ref, mixed_ref, log_ref):
    features = query_ref.shape[1]
    start, inside = head_window(features)
    window = pl.ds(start, WINDOW)
    keys = jnp.where(inside, key_ref[:, window], 0)
    values = jnp.where(inside, value_ref[:, window], 0)
    factor = HD**-0.5 * LOG2E
    for block in range(query_ref.shape[0] // QUERY_BLOCK):
        rows = pl.ds(block * QUERY_BLOCK, QUERY_BLOCK)
        scores = dot_nt(keys, query_ref[rows, window])
        peak = jnp.max(scores, axis=0, keepdims=True)
        powers = jnp.exp2((scores - peak) * factor)
        total = jnp.sum(powers, axis=0, keepdims=True)
        log_ref[0, :, rows] = peak * factor + jnp.log2(total)
        weights = (powers * (1.0 / total)).astype(BF16)
        mixed = dot_tn(values, weights).T.astype(BF16)
        mixed_ref[rows, window] = jnp.where(inside, mixed, mixed_ref[rows, window])


def attend_backward_kernel(
    query_ref, key_ref, value_ref, incoming_ref, log_ref, grad_ref, key_total, value_total
):
    features = query_ref.shape[1]
    start, inside = head_window(features)
    window = pl.ds(start, WINDOW)
    keys = jnp.where(inside, key_ref[:, window], 0)
    values = jnp.where(inside, value_ref[:, window], 0)
    scale = HD**-0.5
    factor = scale * LOG2E
    for block in range(query_ref.shape[0] // QUERY_BLOCK):
        rows = pl.ds(block * QUERY_BLOCK, QUERY_BLOCK)
        queries = query_ref[rows, window]
        incoming = incoming_ref[rows, window]
        probs = jnp.exp2(dot_nt(keys, queries) * factor - log_ref[0, :, rows])
        prob_grad = dot_nt(values, incoming)
        centre = jnp.sum(probs * prob_grad, axis=0, keepdims=True)
        score_grad = (probs * (prob_grad - centre) * scale).astype(BF16)
        key_part = dot_nn(score_grad, queries)
        value_part = dot_nn(probs.astype(BF16), incoming)
        if block == 0:
            key_total[...] = key_part
            value_total[...] = value_part
        else:
            key_total[...] += key_part
            value_total[...] += value_part
        query_grad = dot_tn(keys, score_grad).T.astype(grad_ref.dtype)
        grad_ref[rows, window] = jnp.where(inside, query_grad, grad_ref[rows, window])
    for part, total in ((1, key_total), (2, value_total)):
        place = pl.ds(pl.multiple_of(start + part * features, LANES), WINDOW)
        grad_ref[:, place] = jnp.where(inside, total[...].astype(grad_ref.dtype), grad_ref[:, place])


def whole_block(shape, column):
    return pl.BlockSpec(shape, lambda head: (0, column), pipeline_mode=pl.Buffered(1))


def attend_forward(projected, everyone):
    rows = projected.shape[0]
    features = projected.shape[1] // 3
    tokens = everyone.shape[0]
    return pl.pallas_call(
        attend_forward_kernel,
        grid=(HEADS,),
        in_specs=[
            whole_block((rows, features), 0),
            whole_block((tokens, features), 1),
            whole_block((tokens, features), 2),
        ],
        out_specs=[
            whole_block((rows, features), 0),
            pl.BlockSpec((1, 1, rows), lambda head: (head, 0, 0)),
        ],
        out_shape=[
            jax.ShapeDtypeStruct((rows, features), BF16),
            jax.ShapeDtypeStruct((HEADS, 1, rows), F32),
        ],
        compiler_params=pltpu.CompilerParams(vmem_limit_bytes=56 * 1024 * 1024),
        cost_estimate=pl.CostEstimate(
            flops=4 * rows * tokens * HEADS * WINDOW,
            bytes_accessed=2 * (rows * 2 + tokens * 2) * features,
            transcendentals=rows * tokens * HEADS,
        ),
    )(projected, everyone, everyone)


def attend_backward(projected, everyone, incoming, log_total):
    rows = projected.shape[0]
    features = projected.shape[1] // 3
    tokens = everyone.shape[0]
    kind = BF16 if rows == tokens else F32
    return pl.pallas_call(
        attend_backward_kernel,
        grid=(HEADS,),
        in_specs=[
            whole_block((rows, features), 0),
            whole_block((tokens, features), 1),
            whole_block((tokens, features), 2),
            whole_block((rows, features), 0),
            pl.BlockSpec((1, 1, rows), lambda head: (head, 0, 0)),
        ],
        out_specs=whole_block((tokens, 3 * features), 0),
        out_shape=jax.ShapeDtypeStruct((tokens, 3 * features), kind),
        scratch_shapes=[pltpu.VMEM((tokens, WINDOW), F32), pltpu.VMEM((tokens, WINDOW), F32)],
        compiler_params=pltpu.CompilerParams(vmem_limit_bytes=56 * 1024 * 1024),
        cost_estimate=pl.CostEstimate(
            flops=10 * rows * tokens * HEADS * WINDOW,
            bytes_accessed=2 * (rows * 2 + tokens * 5) * features,
            transcendentals=rows * tokens * HEADS,
        ),
    )(projected, everyone, everyone, incoming, log_total)


class Layout:
    def __init__(self, micro, local, tokens, seq):
        self.micro, self.local, self.tokens, self.seq = micro, local, tokens, seq
        self.latents = micro * local
        self.sharers = max(1, seq // self.latents)
        self.held = max(1, self.latents // seq)
        self.span = seq // self.sharers

    def gather(self, values):
        values = values.reshape(self.latents, self.tokens, values.shape[-1])
        if self.sharers > 1:
            values = jnp.repeat(values, self.sharers, axis=0)
        moved = lax.all_to_all(values, "seq", split_axis=0, concat_axis=1, tiled=True)
        if self.sharers > 1:
            part = lax.axis_index("seq") % self.sharers
            count = self.span * self.tokens
            moved = lax.dynamic_slice_in_dim(moved, part * count, count, axis=1)
        return moved

    def scatter(self, values):
        if self.sharers > 1:
            values = jnp.concatenate([values] * self.sharers, axis=1)
        moved = lax.all_to_all(values, "seq", split_axis=1, concat_axis=0, tiled=True)
        if self.sharers > 1:
            part = lax.axis_index("seq") // self.span
            moved = moved.reshape(self.latents, self.sharers, self.tokens, values.shape[-1])
            moved = lax.dynamic_index_in_dim(moved, part, axis=1, keepdims=False)
        return moved.reshape(self.micro, self.local, self.tokens, values.shape[-1])

    def own_group(self, values, axis):
        if self.sharers == self.seq:
            return values
        count = values.shape[axis] // self.seq * self.sharers
        return lax.dynamic_slice_in_dim(
            values, lax.axis_index("seq") // self.sharers * count, count, axis=axis
        )


def on_device(
    latents,
    condition,
    cotangent,
    modulate_weight,
    modulate_bias,
    triple_weight,
    triple_bias,
    output_weight,
    output_bias,
    expand_weight,
    expand_bias,
    shrink_weight,
    shrink_bias,
):
    micro, local, tokens, features = latents.shape
    hidden = expand_weight.shape[1]
    groups = lax.axis_size("dp")
    seq = lax.axis_size("seq")
    devices = groups * seq
    place = Layout(micro, local, tokens, seq)
    held = place.held
    me = lax.axis_index("dp") * seq + lax.axis_index("seq")

    everyone_cond = lax.all_gather(condition.reshape(micro * local, features), "dp", axis=0, tiled=True)
    bias_shard = jnp.concatenate([modulate_bias, triple_bias, output_bias, expand_bias, shrink_bias])
    biases = lax.all_gather(bias_shard, AXES, axis=0, tiled=False).astype(F32)
    cuts = []
    offset = 0
    for shard in (modulate_bias, triple_bias, output_bias, expand_bias, shrink_bias):
        cuts.append(biases[:, offset : offset + shard.shape[0]].reshape(-1))
        offset += shard.shape[0]
    modulate_offset, triple_offset, output_offset, expand_offset, shrink_offset = cuts

    latent_rows = place.gather(latents)
    first_shard = jnp.concatenate([triple_weight, output_weight], axis=1)
    first_full = lax.all_gather(first_shard, AXES, axis=0, tiled=True)
    triple_full = first_full[:, : 3 * features]
    output_full = first_full[:, 3 * features :]
    expand_full = lax.all_gather(expand_weight, AXES, axis=0, tiled=True)
    shrink_full = lax.all_gather(shrink_weight, AXES, axis=0, tiled=True)

    owned = modulate_weight.shape[0]
    cond_act = jax.nn.silu(everyone_cond.astype(F32)).astype(BF16)
    act_owned = lax.dynamic_slice_in_dim(cond_act, me * owned, owned, axis=1)
    modulation_part = dot_nn(act_owned, modulate_weight)
    if place.sharers > 1:
        modulation_part = jnp.repeat(modulation_part, place.sharers, axis=0)
    modulation_parts = lax.all_to_all(modulation_part, AXES, split_axis=0, concat_axis=0, tiled=True)
    modulation = jnp.sum(modulation_parts.reshape(devices, held, -1), axis=0) + modulate_offset
    shift_one, scale_one, gate_one, shift_two, scale_two, gate_two = jnp.split(
        modulation[:, None, :], 6, axis=-1
    )

    latent_float = latent_rows.astype(F32)
    normed_one, inverse_one = norm_parts(latent_float)
    hidden_one = (normed_one * (1.0 + scale_one) + shift_one).astype(BF16)
    rows = held * latent_rows.shape[1]

    def flat(values):
        return values.reshape(rows, values.shape[-1])

    def unflat(values):
        return values.reshape(held, rows // held, values.shape[-1])

    zero = jnp.zeros((features,), F32)
    full_bias = jnp.concatenate([triple_offset[:features], zero, triple_offset[features:]])
    projected = unflat((dot_nn(flat(hidden_one), triple_full) + full_bias).astype(BF16))
    if place.sharers > 1:
        everyone = place.own_group(lax.all_gather(projected, "seq", axis=1, tiled=True), 1)
    else:
        everyone = projected
    mixed_parts, log_parts = zip(
        *(attend_forward(projected[index], everyone[index]) for index in range(held))
    )
    mixed = jnp.stack(mixed_parts) if held > 1 else mixed_parts[0][None]
    branch_one = unflat(dot_nn(flat(mixed), output_full)) + output_offset
    middle = latent_float + gate_one * branch_one
    normed_two, inverse_two = norm_parts(middle)
    hidden_two = (normed_two * (1.0 + scale_two) + shift_two).astype(BF16)
    pre_act = dot_nn(flat(hidden_two), expand_full) + expand_offset
    activated = gelu_parts(pre_act)[0].astype(BF16)
    branch_two = unflat(dot_nn(activated, shrink_full)) + shrink_offset
    output = place.scatter((middle + gate_two * branch_two).astype(BF16))

    incoming = place.gather(cotangent).astype(F32)
    branch_two_grad = (gate_two * incoming).astype(BF16)
    gate_two_grad = jnp.sum(incoming * branch_two, axis=1)
    shrink_offset_grad = jnp.sum(branch_two_grad.astype(F32), axis=(0, 1))
    shrink_grad = dot_tn(activated, flat(branch_two_grad)).astype(BF16)
    shrink_total = lax.psum_scatter(shrink_grad, AXES, scatter_dimension=0, tiled=True).astype(F32)
    act_grad = dot_nt(flat(branch_two_grad), shrink_full)
    pre_grad = (act_grad * gelu_parts(pre_act)[1]).astype(BF16)
    expand_offset_grad = jnp.sum(pre_grad.astype(F32), axis=0)
    expand_grad = dot_tn(flat(hidden_two), pre_grad).astype(BF16)
    expand_total = scatter_rows(expand_grad, devices)
    hidden_two_grad = unflat(dot_nt(pre_grad, expand_full))
    norm_grad_two, shift_two_grad, scale_two_grad = norm_back(
        hidden_two_grad, normed_two, inverse_two, scale_two
    )
    middle_grad = incoming + norm_grad_two
    branch_one_grad = (gate_one * middle_grad).astype(BF16)
    gate_one_grad = jnp.sum(middle_grad * branch_one, axis=1)
    output_offset_grad = jnp.sum(branch_one_grad.astype(F32), axis=(0, 1))
    output_grad = dot_tn(flat(mixed), flat(branch_one_grad)).astype(BF16)
    mixed_grad = unflat(dot_nt(flat(branch_one_grad), output_full).astype(BF16))
    grads = []
    for index in range(held):
        grad = attend_backward(projected[index], everyone[index], mixed_grad[index], log_parts[index])
        if place.sharers > 1:
            key_value = grad[:, features:]
            key_value = lax.psum_scatter(
                own_slots(key_value, place), "seq", scatter_dimension=0, tiled=True
            ).astype(BF16)
            grad = jnp.concatenate([grad[: rows // held, :features].astype(BF16), key_value], axis=1)
        grads.append(grad)
    triple_rows = jnp.concatenate(grads) if held > 1 else grads[0]
    column_sums = jnp.sum(triple_rows.astype(F32), axis=0)
    triple_offset_grad = jnp.concatenate([column_sums[:features], column_sums[2 * features :]])
    triple_grad = dot_tn(flat(hidden_one), triple_rows).astype(BF16)
    first_grad = jnp.concatenate([triple_grad, output_grad], axis=1)
    first_total = scatter_rows(first_grad, devices)
    hidden_one_grad = unflat(dot_nt(triple_rows, triple_full))
    norm_grad_one, shift_one_grad, scale_one_grad = norm_back(
        hidden_one_grad, normed_one, inverse_one, scale_one
    )
    latents_gradient = place.scatter((middle_grad + norm_grad_one).astype(BF16)).astype(F32)

    modulation_grad = jnp.concatenate(
        [shift_one_grad, scale_one_grad, gate_one_grad, shift_two_grad, scale_two_grad, gate_two_grad],
        axis=-1,
    )
    if place.sharers > 1:
        parts = lax.all_gather(modulation_grad, "seq", axis=0, tiled=True)
        modulation_grad = jnp.sum(place.own_group(parts, 0), axis=0, keepdims=True)
    all_grads = lax.all_gather(modulation_grad.astype(BF16), AXES, axis=0, tiled=True)
    if place.sharers > 1:
        all_grads = all_grads[:: place.sharers]
    modulate_total = dot_tn(act_owned, all_grads)
    shard = modulate_bias.shape[0]
    modulate_offset_total = jnp.sum(
        lax.dynamic_slice_in_dim(all_grads, me * shard, shard, axis=1).astype(F32), axis=0
    )
    cond_back = dot_nt(all_grads, modulate_weight)
    everyone_back = lax.all_gather(cond_back, AXES, axis=1, tiled=True)
    group_back = lax.dynamic_slice_in_dim(
        everyone_back, lax.axis_index("dp") * micro * local, micro * local, axis=0
    ).reshape(condition.shape)
    cond_float = condition.astype(F32)
    sigmoid_cond = jax.nn.sigmoid(cond_float)
    condition_gradient = group_back * (sigmoid_cond * (1.0 + cond_float * (1.0 - sigmoid_cond)))

    bias_grads = jnp.concatenate(
        [
            values.reshape(devices, -1)
            for values in (triple_offset_grad, output_offset_grad, expand_offset_grad, shrink_offset_grad)
        ],
        axis=1,
    )
    bias_total = jnp.sum(
        lax.all_to_all(bias_grads, AXES, split_axis=0, concat_axis=0, tiled=True), axis=0
    )
    bias_cuts = []
    offset = 0
    for part in (triple_bias, output_bias, expand_bias, shrink_bias):
        bias_cuts.append(bias_total[offset : offset + part.shape[0]])
        offset += part.shape[0]
    return (
        output,
        latents_gradient,
        condition_gradient,
        modulate_total,
        modulate_offset_total,
        first_total[:, : 3 * features],
        bias_cuts[0],
        first_total[:, 3 * features :],
        bias_cuts[1],
        expand_total,
        bias_cuts[2],
        shrink_total,
        bias_cuts[3],
    )


def scatter_rows(values, devices):
    rows, columns = values.shape
    slots = values.reshape(rows * columns // 1152, 1152)
    total = lax.psum_scatter(slots, AXES, scatter_dimension=0, tiled=True)
    return total.reshape(rows // devices, columns).astype(F32)


def own_slots(values, place):
    group = lax.axis_index("seq") // place.sharers
    slots = jnp.zeros((place.seq // place.sharers,) + values.shape, values.dtype)
    slots = lax.dynamic_update_index_in_dim(slots, values, group, axis=0)
    return slots.reshape(-1, values.shape[-1])


def solution(mesh):
    tokens = P(None, "dp", "seq", None)
    conditions = P(None, "dp", None)
    weight = P(AXES, None)
    bias = P(AXES)
    parameters = (weight, bias) * 5
    return jax.shard_map(
        on_device,
        mesh=mesh,
        in_specs=(tokens, conditions, tokens) + parameters,
        out_specs=(tokens, tokens, conditions) + parameters,
        check_vma=False,
    )
```

time: 3600 us -> 1020 us (0.28)
  blocking collectives: 1950 us -> 304 us
  matrix products: 601 us -> 204 us
  waiting for transfers between devices: 443 us -> 154 us
  local copies, waits for them, and re-layouts: 352 us -> 121 us
  starting transfers between devices: 164 us -> 21 us
  Pallas kernels: 0 us -> 126 us
    unnamed x4 -> x1, blocking collectives: 1900 us -> 80.7 us
    all_gather x13 -> x3, waiting for transfers between devices: 423 us -> 21.4 us  [the longest x1 21.4 us: on_device(): expand_full = lax.all_gather(expand_weight, AXES, axis=0, tiled=True)]
    dot_general x62 -> x15, matrix products: 601 us -> 204 us  [the longest x5 72.5 us: dot_nn(): return jnp.dot(left, right, preferred_element_type=F32)]
    unnamed x24 -> x0, starting transfers between devices: 164 us -> none
    all_gather x4 -> x3, blocking collectives: 36.1 us -> 181 us  [the longest x1 96.3 us: on_device(): lax.all_gather(modulation_grad.astype(BF16), AXES, axis=0, tiled=True)]
    pallas_call x0 -> x2, Pallas kernels: none -> 126 us  [the longest x1 76.4 us: attend_backward(): pl.pallas_call(attend_backward_kernel, grid=(HEADS,), in_specs=[whole_blo...]
    unnamed x335 -> x93, local copies, waits for them, and re-layouts: 177 us -> 61.6 us
    dynamic_slice x48 -> x1, local copies, waits for them, and re-layouts: 101 us -> 0.78 us  [on_device(): lax.dynamic_slice_in_dim(everyone_back, lax.axis_index('dp') * micro * lo...]
  transfers between devices with their start and end apart: 38 -> 11, of which waited for: 10 -> 3; matrix products, arithmetic and copies ran while one was open for 77% -> 25% of each run, Pallas kernels for 0% -> 5%
where the time goes in v1:
time: 1020 us; the launch traced here: 1010 us
  blocking collectives  304 us (30%)
  matrix products  204 us (20%)
  waiting for transfers between devices  154 us (15%)
  Pallas kernels  126 us (12%)
  local copies, waits for them, and re-layouts  121 us (12%)
  other arithmetic  65.4 us (6%)
  starting transfers between devices  21 us (2%)
  between operations  14.9 us (1%)
    all_gather x1, blocking collectives, on_device(): lax.all_gather(modulation_grad.astype(BF16), AXES, axis=0, tiled=True)  96.3 us
    reduce_scatter x1, waiting for transfers between devices, on_device(): lax.psum_scatter(shrink_grad, AXES, scatter_dimension=0, tiled=True)  94.8 us
    unnamed x1, blocking collectives  80.7 us
    pallas_call x1, Pallas kernels, attend_backward(): pl.pallas_call(attend_backward_kernel, grid=(HEADS,), in_specs=[whole_blo...  76.4 us
    dot_general x5, matrix products, dot_nn(): return jnp.dot(left, right, preferred_element_type=F32)  72.5 us
    dot_general x5, matrix products, dot_nt(): lax.dot_general(left, right, (((1,), (1,)), ((), ())), preferred_element_...  72 us
    all_gather x1, blocking collectives, on_device(): everyone_back = lax.all_gather(cond_back, AXES, axis=1, tiled=True)  68.6 us
    unnamed x93, local copies, waits for them, and re-layouts  61.6 us
  transfers between devices with their start and end apart: 11, of which 3 were waited for; matrix products, arithmetic and copies ran while one was open for 25% of the time, Pallas kernels for 5%

profile of v1, /device:TPU:0, one launch (start us, length us, event | category | flops | bytes accessed | tf_op | source)
XLA Modules:
  0.0 1011.0 jit_solution(16027296516154906876)
XLA Ops:
  11.3 15.7 %all-gather.1 = bf16[8,4,1152]{2,1,0:T(4,128)(2,1)S(1)} all-gather(bf16[1,4,1152]{2,1,0:T(4,128)(2,1)S(1)} %reshape.538), channel_id=1, replica_groups=mesh['dp'=8,'seq'=4] {'dp'}, dimensions={0}, use_global_device_ids=true | all-gather | bytes 82944 | tf_op jit(solution)/shard_map/all_gather | solution.py:245
  28.3 42.8 %all_to_all.54 = f32[32,1,6912]{2,1,0:T(1,128)} all-to-all(f32[32,1,6912]{2,1,0:T(1,128)S(1)} %copy.34), channel_id=1, replica_groups=mesh['dp'=8,'seq'=4] {'dp','seq'}, dimensions={0} | all-to-all | bytes 1769472 | tf_op jit(solution)/shard_map/all_to_all | solution.py:269
  75.3 80.7 %all-reduce = bf16[16128]{0:T(1024)(128)(2,1)S(1)} all-reduce(bf16[16128]{0:T(1024)(128)(2,1)S(1)} %dynamic-update-slice), channel_id=2, replica_groups=mesh['dp'=8,'seq'=4] {'dp','seq'}, use_global_device_ids=true, to_apply=%add | all-reduce | flops 16128 | bytes 64512
  165.4 36.7 %all-to-all-done.3 = bf16[4,256,1152]{2,1,0:T(8,128)(2,1)} async-done(((bf16[4,256,1152]{2,1,0:T(8,128)(2,1)}), bf16[4,256,1152]{2,1,0:T(8,128)(2,1)}, u32[]{:S(2)}, u32[]{:S(2)}) %all-to-all-start.3) | async-done | bytes 2359328 | tf_op jit(solution)/shard_map/all_to_all | solution.py:195
  208.0 14.1 %reshape.541 = bf16[1152,4608]{1,0:T(8,128)(2,1)} reshape(bf16[32,36,4608]{2,1,0:T(8,128)(2,1)} %all-gather.12.cloned.1.call-done) | data formatting | bytes 21233664
  222.1 21.4 %all-gather.14.cloned.1.call-done = bf16[32,36,4608]{2,1,0:T(8,128)(2,1)} async-done(((bf16[1,36,4608]{2,1,0:T(8,128)(2,1)}), bf16[32,36,4608]{2,1,0:T(8,128)(2,1)}) %all-gather.14.cloned.1.call-update) | async-done | bytes 10616848 | tf_op jit(solution)/shard_map/all_gather | solution.py:260
  243.5 14.1 %reshape.543 = bf16[1152,4608]{1,0:T(8,128)(2,1)} reshape(bf16[32,36,4608]{2,1,0:T(8,128)(2,1)} %all-gather.14.cloned.1.call-done) | data formatting | bytes 21233664
  257.6 15.1 %add_convert_fusion.query_ref.key_ref.value_ref = bf16[1024,3456]{1,0:T(8,128)(2,1)} fusion(bf16[1024,1152]{1,0:T(8,128)(2,1)} %add_convert_fusion.4, f32[3456]{0:T(1024)S(1)} %pad_maximum_fusion.2, bf16[1152,4608]{1,0:T(8,128)(2,1)} %reshape.541), kind=kOutput, calls=%fused_computation.9 | convolution fusion | flops 8160804864 | bytes 17413632 | tf_op jit(solution)/shard_map/dot_general | solution.py:58
  272.7 49.6 %shard_map.228 = (bf16[1024,1152]{1,0:T(8,128)(2,1)}, f32[16,1,1024]{2,1,0:T(1,128)}) custom-call(bf16[1024,3456]{1,0:T(8,128)(2,1)} %add_convert_fusion.query_ref.key_ref.value_ref, bf16[1024,3456]{1,0:T(8,128)(2,1)} %add_convert_fusion.query_ref.key_ref.value_ref, bf16[1024,3456]{1,0:T(8,128)(2,1)} %add_convert_fusion.query_ref.key_ref.value_ref), custom_call_target="tpu_custom_call" | custom-call | flops 17179869184 | bytes 9437184 | tf_op jit(solution)/shard_map/pallas_call | solution.py:131
  333.6 17.7 %fusion.25 = f32[1024,4608]{1,0:T(8,128)} fusion(bf16[1152,4608]{1,0:T(8,128)(2,1)S(1)} %bitcast.91, f32[1024,1152]{1,0:T(8,128)} %copy-done.3, f32[1152]{0:T(1024)S(1)} %get-tuple-element.26, f32[1152]{0:T(1024)S(1)} %get-tuple-element.27, f32[1024]{0:T(1024)S(1)} %add_rsqrt_fusion, f32[1024]{0:T(1024)S(1)} %broadcast_multiply_fusion.4), kind=kOutput, calls=%fused_computation.95 | convolution fusion | flops 10877534208 | bytes 34227200 | tf_op jit(solution)/shard_map/dot_general | solution.py:58
  351.3 26.7 %convert_reduce_fusion = (f32[4608]{0:T(1024)}, bf16[1024,4608]{1,0:T(8,128)(2,1)}) fusion(f32[1024,4608]{1,0:T(8,128)} %fusion.25, f32[4608]{0:T(1024)S(1)} %add.178, bf16[1024,1152]{1,0:T(8,128)(2,1)S(1)} %copy-done.5, bf16[4608,1152]{1,0:T(8,128)(2,1)} %all-gather.10.cloned.1.call-done), kind=kOutput, calls=%fused_computation.2 | convolution fusion | flops 10966003712 | bytes 41324544 | tf_op jit(solution)/shard_map/dot_general | solution.py:50
  378.0 21.4 %multiply_reduce_fusion = (bf16[1152]{0:T(1024)(128)(2,1)}, f32[1024]{0:T(1024)S(1)}, f32[1024]{0:T(1024)S(1)}, bf16[1152]{0:T(1024)(128)(2,1)}, f32[1024,1152]{1,0:T(8,128)}) fusion(f32[1024,1152]{1,0:T(8,128)} %copy-done.3, f32[1024]{0:T(1024)S(1)} %add_rsqrt_fusion, f32[1024]{0:T(1024)S(1)} %broadcast_multiply_fusion.4, f32[1152]{0:T(1024)S(1)} %get-tuple-element.27, ...), kind=kOutput, calls=%fused_computation.32 | convolution fusion | flops 10882248704 | bytes 29516800 | tf_op jit(solution)/shard_map/dot_general | solution.py:50
  399.4 30.8 %fusion.5 = (bf16[1152]{0:T(1024)(128)(2,1)}, bf16[1,1024,1152]{2,1,0:T(8,128)(2,1)}, f32[1152]{0:T(1024)}, bf16[1024,1152]{1,0:T(8,128)(2,1)}, f32[1024,1152]{1,0:T(8,128)}) fusion(bf16[4,256,1152]{2,1,0:T(8,128)(2,1)} %all-to-all-done.3, f32[1024,1152]{1,0:T(8,128)} %copy-done.3, f32[1152]{0:T(1024)S(1)} %copy-done.12, f32[1024]{0:T(1024)S(1)} %get-tuple-element.56, ...), kind=kOutput, calls=%fused_computation.23 | convolution fusion | flops 10941233152 | bytes 50785024 | tf_op jit(solution)/shard_map/dot_general | solution.py:58
  441.1 76.4 %shard_map.229 = bf16[1024,3456]{1,0:T(8,128)(2,1)} custom-call(bf16[1024,3456]{1,0:T(8,128)(2,1)} %add_convert_fusion.query_ref.key_ref.value_ref, bf16[1024,3456]{1,0:T(8,128)(2,1)} %add_convert_fusion.query_ref.key_ref.value_ref, bf16[1024,3456]{1,0:T(8,128)(2,1)} %add_convert_fusion.query_ref.key_ref.value_ref, ...), custom_call_target="tpu_custom_call" | custom-call | flops 42949672960 | bytes 16515072 | tf_op jit(solution)/shard_map/pallas_call | solution.py:161
  534.6 16.3 %reshape.523 = bf16[4608,1152]{1,0:T(8,128)(2,1)} reshape(bf16[1152,4608]{1,0:T(8,128)(2,1)} %pad_maximum_fusion) | data formatting | bytes 21233664 | tf_op jit(solution)/shard_map/reshape | solution.py:407
  551.6 18.2 %convolution_convert_fusion.1 = bf16[1152,4608]{1,0:T(8,128)(2,1)} fusion(bf16[1024,4608]{1,0:T(8,128)(2,1)} %get-tuple-element.55, f32[1024,1152]{1,0:T(8,128)} %copy-done.3, f32[1152]{0:T(1024)S(1)} %copy-done.21, f32[1152]{0:T(1024)S(1)} %get-tuple-element.27, f32[1024]{0:T(1024)S(1)} %add_rsqrt_fusion, f32[1024]{0:T(1024)S(1)} %broadcast_multiply_fusion.4), kind=kOutput, calls=%fused_computation.1 | convolution fusion | flops 10882842624 | bytes 24790016 | tf_op jit(solution)/shard_map/dot_general | solution.py:54
  569.8 16.8 %reshape.527 = bf16[4608,1152]{1,0:T(8,128)(2,1)} reshape(bf16[1152,4608]{1,0:T(8,128)(2,1)} %convolution_convert_fusion.1) | data formatting | bytes 21233664 | tf_op jit(solution)/shard_map/reshape | solution.py:407
  588.4 23.2 %convolution_convert_fusion = bf16[4608,1152]{1,0:T(8,128)(2,1)} fusion(bf16[1024,1152]{1,0:T(8,128)(2,1)S(1)} %copy-done.6, f32[1024,4608]{1,0:T(8,128)} %fusion.25, f32[4608]{0:T(1024)S(1)} %add.178), kind=kOutput, calls=%fused_computation | convolution fusion | flops 10924130304 | bytes 31868928 | tf_op jit(solution)/shard_map/dot_general | solution.py:54
  623.5 16.1 %multiply_reduce_fusion.2 = (bf16[1152]{0:T(1024)(128)(2,1)S(1)}, f32[1024]{0:T(1024)S(1)}, f32[1024]{0:T(1024)S(1)}, bf16[1152]{0:T(1024)(128)(2,1)S(1)}, f32[1024,1152]{1,0:T(8,128)}) fusion(bf16[4,256,1152]{2,1,0:T(8,128)(2,1)S(1)} %copy-done.2, f32[1024]{0:T(1024)S(1)} %copy-done.18, f32[1024]{0:T(1024)S(1)} %bitcast.100, f32[1152]{0:T(1024)S(1)} %copy-done.10, ...), kind=kOutput, calls=%fused_computation.34 | convolution fusion | flops 8165519360 | bytes 22144000 | tf_op jit(solution)/shard_map/dot_general | solution.py:50
  647.8 16.5 %reduce.51 = bf16[1024,1152]{1,0:T(8,128)(2,1)} reduce(bf16[1024,1,1152]{2,1,0:T(2,128)(2,1)} %bitcast.85, bf16[]{:T(256)} %broadcast.226), dimensions={1}, to_apply=%bitcast.83.reduce_sub_computation | reduce | bytes 4718594
  687.9 15.1 %reduce.52 = bf16[1024,1152]{1,0:T(8,128)(2,1)S(1)} reduce(bf16[1024,1,1152]{2,1,0:T(2,128)(2,1)} %bitcast.86, bf16[]{:T(256)} %broadcast.226), dimensions={1}, to_apply=%bitcast.82.reduce_sub_computation | reduce | bytes 4718594
  709.5 96.3 %all-gather.4 = bf16[32,1,6912]{2,1,0:T(2,128)(2,1)S(1)} all-gather(bf16[1,1,6912]{2,1,0:T(2,128)(2,1)S(1)} %bitcast.102), channel_id=1, replica_groups=mesh['dp'=8,'seq'=4] {'dp','seq'}, dimensions={0}, use_global_device_ids=true | all-gather | bytes 456192 | tf_op jit(solution)/shard_map/all_gather | solution.py:356
  807.0 68.6 %all-gather.5 = f32[32,36,32]{1,2,0:T(8,128)S(1)} all-gather(f32[1,36,32]{1,2,0:T(8,128)S(1)} %convolution_bitcast_fusion.1), channel_id=1, replica_groups=mesh['dp'=8,'seq'=4] {'dp','seq'}, dimensions={0}, use_global_device_ids=true | all-gather | bytes 152064 | tf_op jit(solution)/shard_map/all_gather | solution.py:365
  907.3 94.8 %reduce-scatter.8.cloned.1.call-done = bf16[144,1152]{1,0:T(8,128)(2,1)} async-done(((bf16[4608,1152]{1,0:T(8,128)(2,1)}), bf16[144,1152]{1,0:T(8,128)(2,1)}) %reduce-scatter.8.cloned.1.call-update) | async-done | bytes 331792 | tf_op jit(solution)/shard_map/reduce_scatter | solution.py:311
  (186 shorter events, 151.0 us)
Async XLA Ops:
  7.2 200.8 %all-gather.12.cloned.1.call-start = ((), (), s32[]{:S(2)}) async-start(), calls=%async_computation.13 | async-start | bytes 12165120 | tf_op jit(solution)/shard_map/all_gather | solution.py:257
  9.1 234.4 %all-gather.14.cloned.1.call-start = ((), (), s32[]{:S(2)}) async-start(), calls=%async_computation.14 | async-start | bytes 12165120 | tf_op jit(solution)/shard_map/all_gather | solution.py:260
  9.8 341.5 %all-gather.10.cloned.1.call-start = ((), (), s32[]{:S(2)}) async-start(), calls=%async_computation.9 | async-start | bytes 10948608 | tf_op jit(solution)/shard_map/all_gather | solution.py:261
  27.0 44.2 %copy-start.8 = (f32[32,1152]{1,0:T(8,128)}, f32[32,1152]{1,0:T(8,128)S(1)}, u32[]{:S(2)}) copy-start(f32[32,1152]{1,0:T(8,128)S(1)} %reshape.548) | copy-start | bytes 442372
  27.0 47.9 %copy-start.27 = (bf16[216]{0:T(256)(128)(2,1)S(1)}, bf16[216]{0:T(256)(128)(2,1)}, u32[]{:S(2)}) copy-start(bf16[216]{0:T(256)(128)(2,1)} %param.17) | copy-start | bytes 1300
  27.0 47.9 %copy-start.28 = (bf16[72]{0:T(256)(128)(2,1)S(1)}, bf16[72]{0:T(256)(128)(2,1)}, u32[]{:S(2)}) copy-start(bf16[72]{0:T(256)(128)(2,1)} %param.19) | copy-start | bytes 436
  27.1 47.9 %copy-start.29 = (bf16[36]{0:T(256)(128)(2,1)S(1)}, bf16[36]{0:T(256)(128)(2,1)}, u32[]{:S(2)}) copy-start(bf16[36]{0:T(256)(128)(2,1)} %param.21) | copy-start | bytes 220
  27.1 47.9 %copy-start.30 = (bf16[144]{0:T(256)(128)(2,1)S(1)}, bf16[144]{0:T(256)(128)(2,1)}, u32[]{:S(2)}) copy-start(bf16[144]{0:T(256)(128)(2,1)} %param.23) | copy-start | bytes 868
  27.1 47.9 %copy-start.31 = (bf16[36]{0:T(256)(128)(2,1)S(1)}, bf16[36]{0:T(256)(128)(2,1)}, u32[]{:S(2)}) copy-start(bf16[36]{0:T(256)(128)(2,1)} %param.25) | copy-start | bytes 220
  71.2 88.1 %all-to-all-start = ((bf16[4,256,1152]{2,1,0:T(8,128)(2,1)}), bf16[4,256,1152]{2,1,0:T(8,128)(2,1)S(1)}, u32[]{:S(2)}, u32[]{:S(2)}) async-start(bf16[4,256,1152]{2,1,0:T(8,128)(2,1)} %bitcast.95), calls=%async_computation | async-start | bytes 4718592 | tf_op jit(solution)/shard_map/all_to_all | solution.py:195
  159.3 163.0 %copy-start.1 = (bf16[4,256,1152]{2,1,0:T(8,128)(2,1)}, bf16[4,256,1152]{2,1,0:T(8,128)(2,1)S(1)}, u32[]{:S(2)}) copy-start(bf16[4,256,1152]{2,1,0:T(8,128)(2,1)S(1)} %all-to-all-done) | copy-start | bytes 7077892
  159.3 42.8 %all-to-all-start.3 = ((bf16[4,256,1152]{2,1,0:T(8,128)(2,1)}), bf16[4,256,1152]{2,1,0:T(8,128)(2,1)}, u32[]{:S(2)}, u32[]{:S(2)}) async-start(bf16[4,256,1152]{2,1,0:T(8,128)(2,1)} %bitcast.96), calls=%async_computation.3 | async-start | bytes 4718592 | tf_op jit(solution)/shard_map/all_to_all | solution.py:195
  163.8 738.7 %reduce-scatter.4.cloned.1.call-start = ((), (), s32[]{:S(2)}) async-start(), calls=%async_computation.10 | async-start | bytes 10948608 | tf_op jit(solution)/shard_map/reduce_scatter | solution.py:408
  164.0 41.6 %copy-start.9 = (f32[1152]{0:T(1024)}, f32[1152]{0:T(1024)S(1)}, u32[]{:S(2)}) copy-start(f32[1152]{0:T(1024)S(1)} %get-tuple-element.29) | copy-start | bytes 13828
  164.0 169.5 %copy-start.20 = (f32[1152]{0:T(1024)}, f32[1152]{0:T(1024)S(1)}, u32[]{:S(2)}) copy-start(f32[1152]{0:T(1024)S(1)} %get-tuple-element.26) | copy-start | bytes 13828
  164.4 41.2 %copy-start.14 = (f32[1,2,4,128]{3,1,2,0:T(2,128)}, f32[1,2,4,128]{3,1,2,0:T(2,128)S(1)}, u32[]{:S(2)}) copy-start(f32[1,2,4,128]{3,1,2,0:T(2,128)S(1)} %copy.43) | copy-start | bytes 12292
  165.4 42.6 %copy-start.17 = (f32[1024]{0:T(1024)}, f32[1024]{0:T(1024)S(1)}, u32[]{:S(2)}) copy-start(f32[1024]{0:T(1024)S(1)} %add_rsqrt_fusion.1) | copy-start | bytes 12292
  441.1 76.4 %copy-start.7 = (bf16[1024,1152]{1,0:T(8,128)(2,1)S(1)}, bf16[1024,1152]{1,0:T(8,128)(2,1)}, u32[]{:S(2)}) copy-start(bf16[1024,1152]{1,0:T(8,128)(2,1)} %add_convert_fusion.4) | copy-start | bytes 7077892
  550.9 354.3 %reduce-scatter.6.cloned.1.call-start = ((), (), s32[]{:S(2)}) async-start(), calls=%async_computation.11 | async-start | bytes 10948608 | tf_op jit(solution)/shard_map/reduce_scatter | solution.py:408
  586.6 415.4 %reduce-scatter.8.cloned.1.call-start = ((), (), s32[]{:S(2)}) async-start(), calls=%async_computation.12 | async-start | bytes 10948608 | tf_op jit(solution)/shard_map/reduce_scatter | solution.py:311
  620.0 48.4 %all-to-all-start.5 = ((f32[32,1,288]{2,1,0:T(1,128)}), f32[32,1,288]{2,1,0:T(1,128)S(1)}, u32[]{:S(2)}, u32[]{:S(2)}) async-start(f32[32,1,288]{2,1,0:T(1,128)} %all_to_all.46), calls=%async_computation.6 | async-start | bytes 98304 | tf_op jit(solution)/shard_map/all_to_all | solution.py:381
  668.4 36.9 %all-to-all-start.2 = ((bf16[4,2,147456]{2,1,0:T(2,128)(2,1)}), bf16[4,2,147456]{2,1,0:T(2,128)(2,1)}, u32[]{:S(2)}, u32[]{:S(2)}) async-start(bf16[4,2,147456]{2,1,0:T(2,128)(2,1)} %reshape.558), calls=%async_computation.2 | async-start | bytes 4718592 | tf_op jit(solution)/shard_map/all_to_all | solution.py:205
  705.3 176.5 %copy-start.16 = (bf16[2,2,1152]{2,1,0:T(2,128)(2,1)S(1)}, bf16[2,2,1152]{2,1,0:T(2,128)(2,1)}, u32[]{:S(2)}) copy-start(bf16[2,2,1152]{2,1,0:T(2,128)(2,1)} %param.14) | copy-start | bytes 27652
  705.3 188.6 %all-to-all-start.4 = ((bf16[4,2,147456]{2,1,0:T(2,128)(2,1)}), bf16[4,2,147456]{2,1,0:T(2,128)(2,1)S(1)}, u32[]{:S(2)}, u32[]{:S(2)}) async-start(bf16[4,2,147456]{2,1,0:T(2,128)(2,1)} %reshape.560), calls=%async_computation.4 | async-start | bytes 4718592 | tf_op jit(solution)/shard_map/all_to_all | solution.py:205
  (24 other events, 266.2 us)
Sparse Core Ops, SparseCore 0:
  11.5 125.3 all-gather.11
  139.8 103.6 all-gather.13
  246.4 85.6 all-gather.9
  551.1 153.2 reduce-scatter.3
  710.3 144.9 reduce-scatter.5
  861.2 140.8 reduce-scatter.7

commit v2 on v1

--- a/solution.py
+++ b/solution.py
@@ -416,14 +416,906 @@
     return slots.reshape(-1, values.shape[-1])
 
 
+MESH = pl.DeviceIdType.MESH
+ANY = pl.BlockSpec(memory_space=pl.ANY)
+ROWS = 144
+
+
+class Here:
+    def __init__(self):
+        dp, self.member = lax.axis_index("dp"), lax.axis_index("seq")
+        self.group = dp
+        self.z, self.core = dp // 2, dp % 2
+        self.index = dp * 4 + self.member
+        y, x = self.member // 2, self.member % 2
+        self.across_x = y * 2 + (1 - x)
+        self.across_y = (1 - y) * 2 + x
+        self.across = (1 - y) * 2 + (1 - x)
+
+    def at_x(self):
+        return (self.group, self.across_x)
+
+    def at_y(self):
+        return (self.group, self.across_y)
+
+    def at_core(self):
+        return (self.z * 2 + (1 - self.core), self.member)
+
+    def at_z(self, step):
+        return (lax.rem(self.z + step, 4) * 2 + self.core, self.member)
+
+    def at_member(self, step):
+        return (self.group, lax.rem(self.member + step, 4))
+
+    def at_index(self, step):
+        place = lax.rem(self.index + step, 32)
+        return (place // 4, lax.rem(place, 4))
+
+
+def greet(partners):
+    barrier = pltpu.get_barrier_semaphore()
+    for partner in partners:
+        pl.semaphore_signal(barrier, inc=1, device_id=partner, device_id_type=MESH)
+    pl.semaphore_wait(barrier, len(partners))
+
+
+def greet_all(here):
+    barrier = pltpu.get_barrier_semaphore()
+
+    def signal(step, carry):
+        pl.semaphore_signal(barrier, inc=1, device_id=here.at_index(step), device_id_type=MESH)
+        return carry
+
+    lax.fori_loop(1, 32, signal, 0)
+    pl.semaphore_wait(barrier, 31)
+
+
+class Wires:
+    def __init__(self, sent, landed):
+        self.sent, self.landed = sent, landed
+
+    def copy(self, number, source, target, partner):
+        return pltpu.make_async_remote_copy(
+            src_ref=source,
+            dst_ref=target,
+            send_sem=self.sent.at[number],
+            recv_sem=self.landed.at[number],
+            device_id=partner,
+            device_id_type=MESH,
+        )
+
+
+def everyone(here, source_of, target, sent, landed):
+    def copy_of(step):
+        place = lax.rem(here.index + step, 32)
+        return pltpu.make_async_remote_copy(
+            src_ref=source_of(place),
+            dst_ref=target.at[here.index],
+            send_sem=sent.at[step],
+            recv_sem=landed.at[step],
+            device_id=here.at_index(step),
+            device_id_type=MESH,
+        )
+
+    def start(step, carry):
+        copy_of(step).start()
+        return carry
+
+    def wait(step, carry):
+        copy_of(step).wait()
+        return carry
+
+    lax.fori_loop(1, 32, start, 0)
+    return lambda: lax.fori_loop(1, 32, wait, 0)
+
+
+def same_core(here, source, target, sent, landed):
+    mine = here.z * 4 + here.member
+
+    def copy_of(step):
+        place = lax.rem(mine + step, 16)
+        return pltpu.make_async_remote_copy(
+            src_ref=source.at[place],
+            dst_ref=target.at[mine],
+            send_sem=sent.at[step],
+            recv_sem=landed.at[step],
+            device_id=(place // 4 * 2 + here.core, lax.rem(place, 4)),
+            device_id_type=MESH,
+        )
+
+    def start(step, carry):
+        copy_of(step).start()
+        return carry
+
+    def wait(step, carry):
+        copy_of(step).wait()
+        return carry
+
+    lax.fori_loop(1, 16, start, 0)
+    return lambda: lax.fori_loop(1, 16, wait, 0)
+
+
+def introduce_kernel(note_ref, shard_ref, notes_ref, blocks_ref, landing, wide, note_sent, note_landed, sent, landed, local):
+    here = Here()
+    greet_all(here)
+    wires = Wires(sent, landed)
+
+    def columns(place):
+        return shard_ref.at[:, :, pl.ds(pl.multiple_of(place * 1152, LANES), 1152)]
+
+    quads = []
+    for step in range(1, 4):
+        place = lax.rem(here.member + step, 4)
+        quads.append(wires.copy(step - 1, columns(place), landing.at[here.member], here.at_member(step)))
+    for copy in quads:
+        copy.start()
+    done = everyone(here, lambda place: note_ref.at[0], notes_ref, note_sent, note_landed)
+    own = pltpu.make_async_copy(columns(here.member), landing.at[here.member], local.at[0])
+    own.start()
+    mine = pltpu.make_async_copy(note_ref.at[0], notes_ref.at[here.index], local.at[1])
+    mine.start()
+    own.wait()
+    for copy in quads:
+        copy.wait_recv()
+    for part in range(2):
+        for member in range(4):
+            wide[member * 36 : member * 36 + 36, :] = landing[member, part].astype(F32)[:36]
+        blocks_ref[part] = wide[...].astype(BF16)
+    for copy in quads:
+        copy.wait_send()
+    mine.wait()
+    done()
+
+
+def introduce(note, shard):
+    return pl.pallas_call(
+        introduce_kernel,
+        in_specs=[ANY, ANY],
+        out_specs=[ANY, pl.BlockSpec(memory_space=pltpu.VMEM)],
+        out_shape=[
+            jax.ShapeDtypeStruct((32,) + note.shape[1:], note.dtype),
+            jax.ShapeDtypeStruct((2, ROWS, 1152), BF16),
+        ],
+        scratch_shapes=[
+            pltpu.VMEM((4,) + shard.shape[:2] + (1152,), BF16),
+            pltpu.VMEM((ROWS, 1152), F32),
+            pltpu.SemaphoreType.DMA((32,)),
+            pltpu.SemaphoreType.DMA((32,)),
+            pltpu.SemaphoreType.DMA((3,)),
+            pltpu.SemaphoreType.DMA((3,)),
+            pltpu.SemaphoreType.DMA((2,)),
+        ],
+        compiler_params=pltpu.CompilerParams(collective_id=1, has_side_effects=True),
+    )(note, shard)
+
+
+ARRIVALS = (0, 1, 3, 2)
+
+
+class Gather:
+    COPIES = 31
+
+    def __init__(self, here, place, own, sent, landed):
+        self.here, self.place, self.own = here, place, own
+        self.wires = Wires(sent, landed)
+
+    def z_of(self, order):
+        return lax.rem(self.here.z + 4 - ARRIVALS[order], 4)
+
+    def along(self, step, block):
+        here = self.here
+        return self.wires.copy(step - 1, block, self.own(here.z), here.at_z(step))
+
+    def begin(self, block):
+        for step in (1, 3, 2):
+            self.along(step, block).start()
+
+    def sideways(self, kind, order):
+        here = self.here
+        z = self.z_of(order)
+        partner = (here.at_x, here.at_y, here.at_core)[kind]()
+        return self.wires.copy(
+            3 + kind * 4 + order, self.own(z), self.place(here.member, z, here.core), partner
+        )
+
+    def passed(self, kind, order):
+        here = self.here
+        z = self.z_of(order)
+        if kind == 3:
+            member = here.across_x if order >= 2 else here.across_y
+            partner = here.at_y() if order >= 2 else here.at_x()
+        else:
+            member = (here.across_x, here.across_y, here.across)[kind]
+            partner = here.at_core()
+        ref = self.place(member, z, here.core)
+        return self.wires.copy(15 + kind * 4 + order, ref, ref, partner)
+
+    def spread(self, order):
+        for kind in range(3):
+            self.sideways(kind, order).start()
+
+    def relay(self, order):
+        self.sideways(0, order).wait_recv()
+        if order >= 2:
+            self.passed(3, order).start()
+        self.passed(0, order).start()
+        self.sideways(1, order).wait_recv()
+        if order < 2:
+            self.passed(3, order).start()
+        self.passed(1, order).start()
+
+    def close(self, order):
+        self.passed(3, order).wait_recv()
+        self.passed(2, order).start()
+
+    def end(self):
+        for order in range(4):
+            self.sideways(2, order).wait_recv()
+            for kind in range(3):
+                self.passed(kind, order).wait_recv()
+        for order in range(4):
+            for kind in range(3):
+                self.sideways(kind, order).wait_send()
+            for kind in range(4):
+                self.passed(kind, order).wait_send()
+
+
+def open_kernel(
+    block_ref, shrink_ref, part_ref, token_ref, full_ref, expand_ref, shrinks_ref, parts_ref, tokens_ref,
+    part_mine, part_half, part_sent, part_landed, sent, landed, more_sent, more_landed, local,
+):
+    here = Here()
+    greet_all(here)
+    more = Wires(more_sent, more_landed)
+    half = more.copy(0, part_ref.at[1 - here.core], part_half, here.at_core())
+    half.start()
+    load = pltpu.make_async_copy(part_ref.at[here.core], part_mine, local.at[0])
+    load.start()
+    first = Gather(
+        here,
+        lambda member, z, core: full_ref.at[member, z, core],
+        lambda z: full_ref.at[here.member, z, here.core],
+        sent.at[0],
+        landed.at[0],
+    )
+    second = Gather(here, None, lambda z: expand_ref.at[z], sent.at[1], landed.at[1])
+    third = Gather(here, None, lambda z: shrinks_ref.at[z], sent.at[2], landed.at[2])
+    first.begin(block_ref.at[0])
+    mine = here.z * 4 + here.member
+    own = [
+        pltpu.make_async_copy(block_ref.at[0], first.own(here.z), local.at[1]),
+        pltpu.make_async_copy(block_ref.at[1], second.own(here.z), local.at[2]),
+        pltpu.make_async_copy(shrink_ref, third.own(here.z), local.at[3]),
+        pltpu.make_async_copy(token_ref.at[here.member], tokens_ref.at[here.member], local.at[4]),
+    ]
+    for copy in own:
+        copy.start()
+    moved = []
+    for step in range(1, 4):
+        place = lax.rem(here.member + step, 4)
+        moved.append(more.copy(step, token_ref.at[place], tokens_ref.at[here.member], here.at_member(step)))
+    for copy in moved:
+        copy.start()
+    load.wait()
+    half.wait()
+
+    def add(place, carry):
+        part_mine[place] += part_half[place]
+        return carry
+
+    lax.fori_loop(0, 16, add, 0)
+    done = same_core(here, part_mine, parts_ref, part_sent, part_landed)
+    keep = pltpu.make_async_copy(part_mine.at[mine], parts_ref.at[mine], local.at[5])
+    keep.start()
+    own[0].wait()
+    first.spread(0)
+    for order in range(1, 4):
+        first.along(ARRIVALS[order], block_ref.at[0]).wait_recv()
+        first.spread(order)
+    second.begin(block_ref.at[1])
+    third.begin(shrink_ref)
+    for order in range(4):
+        first.relay(order)
+    for order in range(4):
+        first.close(order)
+    first.end()
+    for step in (1, 3, 2):
+        first.along(step, block_ref.at[0]).wait_send()
+        second.along(step, block_ref.at[1]).wait()
+        third.along(step, shrink_ref).wait()
+    for copy in moved:
+        copy.wait()
+    for copy in own[1:]:
+        copy.wait()
+    keep.wait()
+    done()
+
+
+def open_up(blocks, shrink, parts, tokens):
+    column = jax.ShapeDtypeStruct((4, ROWS, 1152), BF16)
+    return pl.pallas_call(
+        open_kernel,
+        in_specs=[ANY] * 4,
+        out_specs=[ANY] * 5,
+        out_shape=[
+            jax.ShapeDtypeStruct((4, 4, 2, ROWS, 1152), BF16),
+            column,
+            column,
+            jax.ShapeDtypeStruct(parts.shape[1:], parts.dtype),
+            jax.ShapeDtypeStruct(tokens.shape, tokens.dtype),
+        ],
+        scratch_shapes=[
+            pltpu.VMEM(parts.shape[1:], F32),
+            pltpu.VMEM(parts.shape[1:], F32),
+            pltpu.SemaphoreType.DMA((16,)),
+            pltpu.SemaphoreType.DMA((16,)),
+            pltpu.SemaphoreType.DMA((3, 31)),
+            pltpu.SemaphoreType.DMA((3, 31)),
+            pltpu.SemaphoreType.DMA((4,)),
+            pltpu.SemaphoreType.DMA((4,)),
+            pltpu.SemaphoreType.DMA((6,)),
+        ],
+        compiler_params=pltpu.CompilerParams(collective_id=2, has_side_effects=True),
+    )(blocks, shrink, parts, tokens)
+
+
+def forward_gather_kernel(
+    query_ref, key_ref, value_ref, expand_column, shrink_column, mixed_ref, log_ref, expand_full, shrink_full,
+    sent, landed, local,
+):
+    head = pl.program_id(0)
+    here = Here()
+    second = Gather(
+        here,
+        lambda member, z, core: expand_full.at[member, z, core],
+        lambda z: expand_column.at[z],
+        sent.at[0],
+        landed.at[0],
+    )
+    third = Gather(
+        here,
+        lambda member, z, core: shrink_full.at[z, core, member],
+        lambda z: shrink_column.at[z],
+        sent.at[1],
+        landed.at[1],
+    )
+    own = (
+        pltpu.make_async_copy(expand_column, expand_full.at[here.member, :, here.core], local.at[0]),
+        pltpu.make_async_copy(shrink_column, shrink_full.at[:, here.core, here.member], local.at[1]),
+    )
+
+    @pl.when(head == 0)
+    def _():
+        greet((here.at_x(), here.at_y(), here.at_core()))
+        for gather in (second, third):
+            for order in range(4):
+                gather.spread(order)
+        for copy in own:
+            copy.start()
+
+    for order, turn in enumerate((6, 8, 10, 12)):
+
+        @pl.when(head == turn)
+        def _():
+            second.relay(order)
+
+    attend_forward_kernel(query_ref, key_ref, value_ref, mixed_ref, log_ref)
+
+    @pl.when(head == HEADS - 1)
+    def _():
+        for order in range(4):
+            third.relay(order)
+        for gather in (second, third):
+            for order in range(4):
+                gather.close(order)
+        for gather in (second, third):
+            gather.end()
+        for copy in own:
+            copy.wait()
+
+
+def attend_forward_gather(projected, expand_column, shrink_column):
+    rows = projected.shape[0]
+    features = projected.shape[1] // 3
+    return pl.pallas_call(
+        forward_gather_kernel,
+        grid=(HEADS,),
+        in_specs=[whole_block((rows, features), part) for part in range(3)] + [ANY] * 2,
+        out_specs=[
+            whole_block((rows, features), 0),
+            pl.BlockSpec((1, 1, rows), lambda head: (head, 0, 0)),
+            ANY,
+            ANY,
+        ],
+        out_shape=[
+            jax.ShapeDtypeStruct((rows, features), BF16),
+            jax.ShapeDtypeStruct((HEADS, 1, rows), F32),
+            jax.ShapeDtypeStruct((4, 4, 2, ROWS, 1152), BF16),
+            jax.ShapeDtypeStruct((4, 2, 4, ROWS, 1152), BF16),
+        ],
+        scratch_shapes=[
+            pltpu.SemaphoreType.DMA((2, 31)),
+            pltpu.SemaphoreType.DMA((2, 31)),
+            pltpu.SemaphoreType.DMA((2,)),
+        ],
+        compiler_params=pltpu.CompilerParams(
+            collective_id=5, has_side_effects=True, vmem_limit_bytes=56 * 1024 * 1024
+        ),
+    )(projected, projected, projected, expand_column, shrink_column)
+
+
+class Reduce:
+    SCRATCH = (
+        pltpu.VMEM((4, 4, ROWS, 1152), BF16),
+        pltpu.VMEM((4, 4, ROWS, 1152), BF16),
+        pltpu.VMEM((2, 2, ROWS, 1152), BF16),
+        pltpu.VMEM((2, 4, ROWS, 1152), BF16),
+        pltpu.VMEM((3, ROWS, 1152), BF16),
+        pltpu.SemaphoreType.DMA((13,)),
+        pltpu.SemaphoreType.DMA((13,)),
+        pltpu.SemaphoreType.DMA((4,)),
+    )
+
+    def __init__(self, here, source, total, kept, crossed, relayed, beside, along, sent, landed, local):
+        self.here, self.source, self.total, self.local = here, source, total, local
+        self.kept, self.crossed, self.relayed, self.beside, self.pieces = kept, crossed, relayed, beside, along
+        self.wires = Wires(sent, landed)
+        self.order = (here.across, here.across_x, here.across_y, here.member)
+
+    def load(self, turn):
+        return pltpu.make_async_copy(
+            self.source.at[self.order[turn], :, self.here.core], self.kept.at[turn], self.local.at[turn]
+        )
+
+    def cross(self, turn):
+        here = self.here
+        return self.wires.copy(
+            turn, self.source.at[self.order[turn], :, 1 - here.core], self.crossed.at[turn], here.at_core()
+        )
+
+    def relay(self, way):
+        partner = (self.here.at_x, self.here.at_y)[way]()
+        half = pl.ds(2 - 2 * way, 2)
+        return self.wires.copy(4 + way, self.kept.at[0, half], self.relayed.at[way], partner)
+
+    def side(self, way, part):
+        partner = (self.here.at_x, self.here.at_y)[way]()
+        half = pl.ds(2 * part, 2)
+        return self.wires.copy(
+            6 + 2 * way + part, self.kept.at[1 + way, half], self.beside.at[way, half], partner
+        )
+
+    def along(self, step):
+        z = lax.rem(self.here.z + step, 4)
+        return self.wires.copy(9 + step, self.kept.at[3, z], self.pieces.at[step - 1], self.here.at_z(step))
+
+    def begin(self):
+        for turn in range(4):
+            self.cross(turn).start()
+            self.load(turn).start()
+
+    def add_crossed(self, turn):
+        self.load(turn).wait()
+        self.cross(turn).wait_recv()
+
+        def add(z, carry):
+            self.kept[turn, z] = (self.kept[turn, z].astype(F32) + self.crossed[turn, z].astype(F32)).astype(BF16)
+            return carry
+
+        lax.fori_loop(0, 4, add, 0)
+
+    def add_relayed(self, turn, way, first):
+        def add(z, carry):
+            self.kept[turn, first + z] = (
+                self.kept[turn, first + z].astype(F32) + self.relayed[way, z].astype(F32)
+            ).astype(BF16)
+            return carry
+
+        lax.fori_loop(0, 2, add, 0)
+
+    def diagonal(self):
+        self.add_crossed(0)
+        self.relay(1).start()
+        self.relay(0).start()
+
+    def direct_x(self):
+        self.add_crossed(1)
+        self.side(0, 1).start()
+
+    def direct_y(self):
+        self.add_crossed(2)
+        self.side(1, 0).start()
+
+    def relay_x(self):
+        self.relay(1).wait_recv()
+        self.add_relayed(1, 1, 0)
+        self.side(0, 0).start()
+
+    def relay_y(self):
+        self.relay(0).wait_recv()
+        self.add_relayed(2, 0, 2)
+        self.side(1, 1).start()
+
+    def keep_own(self):
+        self.add_crossed(3)
+
+    def three(self, z):
+        return (
+            self.kept[3, z].astype(F32) + self.beside[0, z].astype(F32) + self.beside[1, z].astype(F32)
+        )
+
+    def along_z(self):
+        here = self.here
+        for way in range(2):
+            for part in range(2):
+                self.side(way, part).wait_recv()
+        for step in (2, 1, 3):
+            z = lax.rem(here.z + step, 4)
+            self.kept[3, z] = self.three(z).astype(BF16)
+            self.along(step).start()
+        self.total[...] = self.three(here.z)
+
+    def finish(self):
+        for step in (1, 3, 2):
+            self.along(step).wait_recv()
+        self.total[...] += self.pieces[0].astype(F32) + self.pieces[1].astype(F32) + self.pieces[2].astype(F32)
+        for turn in range(4):
+            self.cross(turn).wait_send()
+        for way in range(2):
+            self.relay(way).wait_send()
+            for part in range(2):
+                self.side(way, part).wait_send()
+        for step in range(1, 4):
+            self.along(step).wait_send()
+
+    def steps(self):
+        return (
+            self.begin,
+            self.diagonal,
+            self.direct_x,
+            self.direct_y,
+            self.keep_own,
+            self.relay_x,
+            self.relay_y,
+            self.along_z,
+            self.finish,
+        )
+
+
+def backward_reduce_kernel(
+    query_ref, key_ref, value_ref, incoming_ref, log_ref, source_ref, grad_ref, total_ref,
+    key_total, value_total, *scratch
+):
+    head = pl.program_id(0)
+    here = Here()
+    reduce = Reduce(here, source_ref, total_ref, *scratch)
+
+    @pl.when(head == 0)
+    def _():
+        greet((here.at_x(), here.at_y(), here.at_core(), here.at_z(1), here.at_z(2), here.at_z(3)))
+
+    steps = reduce.steps()
+    for step, turn in zip(steps[:-1], (0, 1, 1, 2, 2, 4, 4, 10)):
+        pl.when(head == turn)(step)
+    attend_backward_kernel(
+        query_ref, key_ref, value_ref, incoming_ref, log_ref, grad_ref, key_total, value_total
+    )
+    pl.when(head == HEADS - 1)(steps[-1])
+
+
+def attend_backward_reduce(projected, incoming, log_total, source):
+    rows = projected.shape[0]
+    features = projected.shape[1] // 3
+    return pl.pallas_call(
+        backward_reduce_kernel,
+        grid=(HEADS,),
+        in_specs=[whole_block((rows, features), part) for part in (0, 1, 2, 0)]
+        + [pl.BlockSpec((1, 1, rows), lambda head: (head, 0, 0)), ANY],
+        out_specs=[whole_block((rows, 3 * features), 0), whole_block((ROWS, features), 0)],
+        out_shape=[
+            jax.ShapeDtypeStruct((rows, 3 * features), BF16),
+            jax.ShapeDtypeStruct((ROWS, features), F32),
+        ],
+        scratch_shapes=[pltpu.VMEM((rows, WINDOW), F32), pltpu.VMEM((rows, WINDOW), F32), *Reduce.SCRATCH],
+        compiler_params=pltpu.CompilerParams(
+            collective_id=6, has_side_effects=True, vmem_limit_bytes=58 * 1024 * 1024
+        ),
+    )(projected, projected, projected, incoming, log_total, source)
+
+
+def close_kernel(
+    grad_ref, token_ref, row_ref, bias_ref, block_ref, share_ref, tokens_ref, rows_ref, biases_ref,
+    total, pieces, row_sent, row_landed, bias_sent, bias_landed, more_sent, more_landed, more_local, *scratch
+):
+    here = Here()
+    greet_all(here)
+    reduce = Reduce(here, grad_ref, total, *scratch)
+    reduce.begin()
+    rows_done = everyone(here, lambda place: row_ref.at[0], rows_ref, row_sent, row_landed)
+    bias_done = everyone(here, lambda place: bias_ref.at[place], biases_ref, bias_sent, bias_landed)
+    wires = Wires(more_sent, more_landed)
+
+    def move(step):
+        place = lax.rem(here.member + step, 4)
+        return wires.copy(step - 1, token_ref.at[place], tokens_ref.at[here.member], here.at_member(step))
+
+    def cut(part, source):
+        for member in range(4):
+            pieces[part, member, :36] = source[member * 36 : member * 36 + 36, :]
+
+    def share(part, step):
+        place = lax.rem(here.member + step, 4)
+        return wires.copy(
+            3 * part + 2 + step, pieces.at[part, place], share_ref.at[part, here.member], here.at_member(step)
+        )
+
+    def keep(part):
+        return pltpu.make_async_copy(
+            pieces.at[part, here.member], share_ref.at[part, here.member], more_local.at[3 + part]
+        )
+
+    own = [
+        pltpu.make_async_copy(token_ref.at[here.member], tokens_ref.at[here.member], more_local.at[0]),
+        pltpu.make_async_copy(row_ref.at[0], rows_ref.at[here.index], more_local.at[1]),
+        pltpu.make_async_copy(bias_ref.at[here.index], biases_ref.at[here.index], more_local.at[2]),
+    ]
+    for copy in own:
+        copy.start()
+    cut(1, block_ref)
+    for step in range(1, 4):
+        share(1, step).start()
+    keep(1).start()
+    move(2).start()
+    for step in reduce.steps()[1:-1]:
+        step()
+    move(1).start()
+    move(3).start()
+    reduce.finish()
+    cut(0, total)
+    for step in range(1, 4):
+        share(0, step).start()
+    keep(0).start()
+    for step in range(1, 4):
+        move(step).wait()
+        share(0, step).wait()
+        share(1, step).wait()
+    for copy in own:
+        copy.wait()
+    keep(0).wait()
+    keep(1).wait()
+    rows_done()
+    bias_done()
+
+
+def close_down(grad, tokens, row, bias, block):
+    return pl.pallas_call(
+        close_kernel,
+        in_specs=[ANY] * 4 + [pl.BlockSpec(memory_space=pltpu.VMEM)],
+        out_specs=[ANY] * 4,
+        out_shape=[
+            jax.ShapeDtypeStruct((2, 4, 40, 1152), F32),
+            jax.ShapeDtypeStruct(tokens.shape, tokens.dtype),
+            jax.ShapeDtypeStruct((32,) + row.shape[1:], row.dtype),
+            jax.ShapeDtypeStruct(bias.shape, bias.dtype),
+        ],
+        scratch_shapes=[pltpu.VMEM((ROWS, 1152), F32), pltpu.VMEM((2, 4, 40, 1152), F32)]
+        + [pltpu.SemaphoreType.DMA((32,))] * 4
+        + [pltpu.SemaphoreType.DMA((9,))] * 2
+        + [pltpu.SemaphoreType.DMA((5,))]
+        + list(Reduce.SCRATCH),
+        compiler_params=pltpu.CompilerParams(
+            collective_id=3, has_side_effects=True, vmem_limit_bytes=48 * 1024 * 1024
+        ),
+    )(grad, tokens, row, bias, block)
+
+
+def swap_kernel(part_ref, parts_ref, sent, landed, local):
+    here = Here()
+    greet_all(here)
+    done = everyone(here, lambda place: part_ref.at[place // 4], parts_ref, sent, landed)
+    own = pltpu.make_async_copy(part_ref.at[here.group], parts_ref.at[here.index], local.at[0])
+    own.start()
+    own.wait()
+    done()
+
+
+def swap(parts):
+    return pl.pallas_call(
+        swap_kernel,
+        in_specs=[ANY],
+        out_specs=ANY,
+        out_shape=jax.ShapeDtypeStruct((32,) + parts.shape[1:], parts.dtype),
+        scratch_shapes=[
+            pltpu.SemaphoreType.DMA((32,)),
+            pltpu.SemaphoreType.DMA((32,)),
+            pltpu.SemaphoreType.DMA((1,)),
+        ],
+        compiler_params=pltpu.CompilerParams(collective_id=4, has_side_effects=True),
+    )(parts)
+
+
+def pad_lanes(values, width):
+    return jnp.pad(values, ((0, 0), (0, width - values.shape[1])))
+
+
+def on_device_fast(
+    latents,
+    condition,
+    cotangent,
+    modulate_weight,
+    modulate_bias,
+    triple_weight,
+    triple_bias,
+    output_weight,
+    output_bias,
+    expand_weight,
+    expand_bias,
+    shrink_weight,
+    shrink_bias,
+):
+    micro, local, tokens, features = latents.shape
+    devices = 32
+    me = lax.axis_index("dp") * 4 + lax.axis_index("seq")
+    hidden = expand_weight.shape[1]
+    shard = jnp.stack([jnp.concatenate([triple_weight, output_weight], axis=1), expand_weight])
+    shard = jnp.pad(shard, ((0, 0), (0, 12), (0, 0)))
+    own_cond = lax.dynamic_index_in_dim(condition.reshape(4, features), lax.axis_index("seq"), axis=0, keepdims=False)
+    biases = (modulate_bias, triple_bias, output_bias, expand_bias, shrink_bias)
+    note = jnp.concatenate([own_cond, *biases]).astype(F32)
+    note = jnp.pad(note, (0, 1664 - note.shape[0])).reshape(1, 1, 1664)
+    notes, blocks = introduce(note, shard)
+    notes = notes.reshape(32, 1664)
+    cond_act = jax.nn.silu(notes[:, :features]).astype(BF16)
+    cuts = []
+    offset = features
+    for bias in biases:
+        cuts.append(notes[:, offset : offset + bias.shape[0]].reshape(-1))
+        offset += bias.shape[0]
+    modulate_offset, triple_offset, output_offset, expand_offset, shrink_offset = cuts
+    owned = modulate_weight.shape[0]
+    act_owned = lax.dynamic_slice_in_dim(cond_act, me * owned, owned, axis=1)
+    parts = pad_lanes(dot_nn(act_owned, modulate_weight), 56 * LANES).reshape(4, 2, 4, 56, LANES)
+    parts = jnp.swapaxes(parts, 0, 1).reshape(2, 16, 56, LANES)
+    first_full, expand_column, shrink_column, parts, token_rows = open_up(
+        blocks, shrink_weight, parts, latents.reshape(4, tokens, features)
+    )
+    first_full = first_full.reshape(4, features, features)
+    modulation = jnp.sum(parts, axis=0).reshape(-1)[: 6 * features] + modulate_offset
+    shift_one, scale_one, gate_one, shift_two, scale_two, gate_two = jnp.split(modulation[None, :], 6, axis=-1)
+
+    latent_float = token_rows.reshape(4 * tokens, features).astype(F32)
+    normed_one, inverse_one = norm_parts(latent_float)
+    hidden_one = (normed_one * (1.0 + scale_one) + shift_one).astype(BF16)
+    zero = jnp.zeros((features,), F32)
+    full_bias = jnp.concatenate([triple_offset[:features], zero, triple_offset[features:]])
+    triple_full = first_full[:3]
+    output_full = first_full[3]
+    projected = (
+        jnp.concatenate([dot_nn(hidden_one, first_full[part]) for part in range(3)], axis=1) + full_bias
+    ).astype(BF16)
+    mixed, log_total, expand_full, shrink_full = attend_forward_gather(projected, expand_column, shrink_column)
+    mixed, cotangent = lax.optimization_barrier((mixed, cotangent))
+    expand_full = expand_full.reshape(4, features, features)
+    shrink_full = shrink_full.reshape(hidden, features)
+    branch_one = dot_nn(mixed, output_full) + output_offset
+    middle = latent_float + gate_one * branch_one
+    normed_two, inverse_two = norm_parts(middle)
+    hidden_two = (normed_two * (1.0 + scale_two) + shift_two).astype(BF16)
+    pre_act = jnp.concatenate([dot_nn(hidden_two, expand_full[part]) for part in range(4)], axis=1) + expand_offset
+    activated = gelu_parts(pre_act)[0].astype(BF16)
+    branch_two = dot_nn(activated, shrink_full) + shrink_offset
+
+    def exchange(values):
+        return lax.all_to_all(values.reshape(4, tokens, features), "seq", split_axis=0, concat_axis=0, tiled=True)
+
+    output = exchange((middle + gate_two * branch_two).astype(BF16))
+    incoming = exchange(cotangent).reshape(4 * tokens, features).astype(F32)
+    branch_two_grad = (gate_two * incoming).astype(BF16)
+    gate_two_grad = jnp.sum(incoming * branch_two, axis=0)
+    shrink_offset_grad = jnp.sum(branch_two_grad.astype(F32), axis=0)
+    shrink_grad = dot_tn(activated, branch_two_grad).astype(BF16)
+    shrink_total = lax.psum_scatter(shrink_grad, AXES, scatter_dimension=0, tiled=True).astype(F32)
+    act_grad = dot_nt(branch_two_grad, shrink_full)
+    pre_grad = (act_grad * gelu_parts(pre_act)[1]).astype(BF16)
+    expand_offset_grad = jnp.sum(pre_grad.astype(F32), axis=0)
+    expand_grad = jnp.stack(
+        [dot_tn(hidden_two, pre_grad[:, part * features : (part + 1) * features]).astype(BF16) for part in range(4)]
+    ).reshape(4, 4, 2, ROWS, features)
+    hidden_two_grad = sum(
+        dot_nt(pre_grad[:, part * features : (part + 1) * features], expand_full[part]) for part in range(4)
+    )
+    norm_grad_two, shift_two_grad, scale_two_grad = norm_back(
+        hidden_two_grad[None], normed_two[None], inverse_two[None], scale_two[None]
+    )
+    middle_grad = incoming + norm_grad_two[0]
+    branch_one_grad = (gate_one * middle_grad).astype(BF16)
+    gate_one_grad = jnp.sum(middle_grad * branch_one, axis=0)
+    output_offset_grad = jnp.sum(branch_one_grad.astype(F32), axis=0)
+    output_grad = dot_tn(mixed, branch_one_grad).astype(BF16)
+    mixed_grad = dot_nt(branch_one_grad, output_full).astype(BF16)
+    triple_rows, expand_block = attend_backward_reduce(projected, mixed_grad, log_total, expand_grad)
+    column_sums = jnp.sum(triple_rows.astype(F32), axis=0)
+    triple_offset_grad = jnp.concatenate([column_sums[:features], column_sums[2 * features :]])
+    first_grad = jnp.stack(
+        [dot_tn(hidden_one, triple_rows[:, part * features : (part + 1) * features]).astype(BF16) for part in range(3)]
+        + [output_grad]
+    ).reshape(4, 4, 2, ROWS, features)
+    hidden_one_grad = sum(
+        dot_nt(triple_rows[:, part * features : (part + 1) * features], first_full[part]) for part in range(3)
+    )
+    norm_grad_one, shift_one_grad, scale_one_grad = norm_back(
+        hidden_one_grad[None], normed_one[None], inverse_one[None], scale_one[None]
+    )
+    token_grad = (middle_grad + norm_grad_one[0]).astype(BF16).reshape(4, tokens, features)
+    modulation_grad = jnp.concatenate(
+        [
+            shift_one_grad[0],
+            scale_one_grad[0],
+            gate_one_grad,
+            shift_two_grad[0],
+            scale_two_grad[0],
+            gate_two_grad,
+        ]
+    ).astype(BF16)
+    row = jnp.pad(modulation_grad, (0, 8192 - 6 * features)).reshape(1, 64, LANES)
+    bias_grads = jnp.concatenate(
+        [
+            values.reshape(devices, -1)
+            for values in (triple_offset_grad, output_offset_grad, expand_offset_grad, shrink_offset_grad)
+        ],
+        axis=1,
+    )
+    bias_grads = pad_lanes(bias_grads, 1024).reshape(32, 8, LANES)
+    shares, token_grad, all_grads, bias_parts = close_down(
+        first_grad, token_grad, row, bias_grads, expand_block
+    )
+    all_grads = all_grads.reshape(32, 8192)[:, : 6 * features]
+    modulate_total = dot_tn(act_owned, all_grads)
+    width = modulate_bias.shape[0]
+    modulate_offset_total = jnp.sum(
+        lax.dynamic_slice_in_dim(all_grads, me * width, width, axis=1).astype(F32), axis=0
+    )
+    cond_back = dot_nt(all_grads, modulate_weight)
+    cond_back = jnp.pad(cond_back.reshape(8, 4, owned), ((0, 0), (0, 4), (0, LANES - owned)))
+    cond_back = swap(cond_back)[:, :4, :owned]
+    cond_back = jnp.swapaxes(cond_back, 0, 1).reshape(condition.shape)
+    cond_float = condition.astype(F32)
+    sigmoid_cond = jax.nn.sigmoid(cond_float)
+    condition_gradient = cond_back * (sigmoid_cond * (1.0 + cond_float * (1.0 - sigmoid_cond)))
+    bias_total = jnp.sum(bias_parts.reshape(32, 1024), axis=0)
+    bias_cuts = []
+    offset = 0
+    for bias in biases[1:]:
+        bias_cuts.append(bias_total[offset : offset + bias.shape[0]])
+        offset += bias.shape[0]
+    first_share = shares[0, :, :owned]
+    expand_total = jnp.swapaxes(shares[1, :, :owned], 0, 1).reshape(expand_weight.shape)
+    return (
+        output.reshape(latents.shape),
+        token_grad.reshape(latents.shape).astype(F32),
+        condition_gradient,
+        modulate_total,
+        modulate_offset_total,
+        jnp.concatenate([first_share[0], first_share[1], first_share[2]], axis=1),
+        bias_cuts[0],
+        first_share[3],
+        bias_cuts[1],
+        expand_total,
+        bias_cuts[2],
+        shrink_total,
+        bias_cuts[3],
+    )
+
+
 def solution(mesh):
     tokens = P(None, "dp", "seq", None)
     conditions = P(None, "dp", None)
     weight = P(AXES, None)
     bias = P(AXES)
     parameters = (weight, bias) * 5
+    fast = mesh.shape["dp"] == 8 and mesh.shape["seq"] == 4
     return jax.shard_map(
-        on_device,
+        on_device_fast if fast else on_device,
         mesh=mesh,
         in_specs=(tokens, conditions, tokens) + parameters,
         out_specs=(tokens, tokens, conditions) + parameters,

time: 1020 us -> 808 us (0.79)
  Pallas kernels: 126 us -> 454 us
  blocking collectives: 304 us -> 0 us
  waiting for transfers between devices: 154 us -> 0.02 us
  local copies, waits for them, and re-layouts: 121 us -> 37.7 us
  other arithmetic: 65.4 us -> 78 us
  starting transfers between devices: 21 us -> 9.05 us
    pallas_call x2 -> x6, Pallas kernels: 126 us -> 454 us  [the longest x1 120 us: close_down(): pl.pallas_call(close_kernel, in_specs=[ANY] * 4 + [pl.BlockSpec(memory_sp...]
    all_gather x3 -> x0, blocking collectives: 181 us -> none  [the longest x1 96.3 us: on_device(): lax.all_gather(modulation_grad.astype(BF16), AXES, axis=0, tiled=True)]
    reduce_scatter x3 -> x1, waiting for transfers between devices: 94.8 us -> 0.01 us  [on_device_fast(): lax.psum_scatter(shrink_grad, AXES, scatter_dimension=0, tiled=True)]
    unnamed x1 -> x0, blocking collectives: 80.7 us -> none
    unnamed x93 -> x112, local copies, waits for them, and re-layouts: 61.6 us -> 12.5 us
    all_to_all x1 -> x0, blocking collectives: 42.8 us -> none  [on_device(): lax.all_to_all(modulation_part, AXES, split_axis=0, concat_axis=0, tiled=...]
    all_to_all x5 -> x2, waiting for transfers between devices: 36.7 us -> 0.01 us  [exchange(): lax.all_to_all(values.reshape(4, tokens, features), 'seq', split_axis=0,...]
    unnamed x5 -> x9, other arithmetic: 33.4 us -> 0.11 us
  transfers between devices with their start and end apart: 11 -> 3, of which waited for: 3 -> 0; matrix products, arithmetic and copies ran while one was open for 25% -> 20% of each run, Pallas kernels for 5% -> 29%
where the time goes in v2:
time: 808 us; the launch traced here: 800 us
  Pallas kernels  454 us (56%)
  matrix products  206 us (25%)
  other arithmetic  78 us (10%)
  local copies, waits for them, and re-layouts  37.7 us (5%)
  between operations  15.4 us (2%)
  starting transfers between devices  9.05 us (1%)
    pallas_call x1, Pallas kernels, close_down(): pl.pallas_call(close_kernel, in_specs=[ANY] * 4 + [pl.BlockSpec(memory_sp...  120 us
    pallas_call x1, Pallas kernels, open_up(): pl.pallas_call(open_kernel, in_specs=[ANY] * 4, out_specs=[ANY] * 5, out_...  104 us
    pallas_call x1, Pallas kernels, attend_backward_reduce(): pl.pallas_call(backward_reduce_kernel, grid=(HEADS,), in_specs=[whole_blo...  100 us
    pallas_call x1, Pallas kernels, attend_forward_gather(): pl.pallas_call(forward_gather_kernel, grid=(HEADS,), in_specs=[whole_bloc...  96.4 us
    dot_general x10, matrix products, dot_nt(): lax.dot_general(left, right, (((1,), (1,)), ((), ())), preferred_element_...  77.1 us
    dot_general x10, matrix products, dot_nn(): return jnp.dot(left, right, preferred_element_type=F32)  67.9 us
    dot_general x10, matrix products, dot_tn(): lax.dot_general(left, right, (((0,), (0,)), ((), ())), preferred_element_...  61.1 us
    pallas_call x1, Pallas kernels, introduce(): pl.pallas_call(introduce_kernel, in_specs=[ANY, ANY], out_specs=[ANY, pl....  22.2 us
  transfers between devices with their start and end apart: 3, of which 0 were waited for; matrix products, arithmetic and copies ran while one was open for 20% of the time, Pallas kernels for 29%

profile of v2, /device:TPU:0, one launch (start us, length us, event | category | flops | bytes accessed | tf_op | source)
XLA Modules:
  0.0 799.9 jit_solution(17512413803455642074)
XLA Ops:
  15.1 22.2 %shard_map.228 = (f32[32,1,1664]{2,1,0:T(1,128)}, bf16[2,144,1152]{2,1,0:T(8,128)(2,1)}) custom-call(f32[1,1,1664]{2,1,0:T(1,128)} %reshape.443.note_ref, bf16[2,48,4608]{2,1,0:T(8,128)(2,1)} %fusion.44.shard_ref), custom_call_target="tpu_custom_call" | custom-call | tf_op jit(solution)/shard_map/pallas_call | solution.py:571
  40.1 103.7 %shard_map.229 = (bf16[4,4,2,144,1152]{4,3,2,1,0:T(8,128)(2,1)}, bf16[4,144,1152]{2,1,0:T(8,128)(2,1)}, bf16[4,144,1152]{2,1,0:T(8,128)(2,1)}, f32[16,56,128]{2,1,0:T(8,128)}, bf16[4,256,1152]{2,1,0:T(8,128)(2,1)}) custom-call(bf16[2,144,1152]{2,1,0:T(8,128)(2,1)} %get-tuple-element.32.block_ref, bf16[144,1152]{1,0:T(8,128)(2,1)} %shrink_ref.1, ...), custom_call_target="tpu_custom_call" | custom-call | tf_op jit(solution)/shard_map/pallas_call | solution.py:736
  149.6 6.0 fusion.64
  166.8 5.2 fusion.69
  172.2 8.0 %fusion.query_ref.key_ref.value_ref = bf16[1024,3456]{1,0:T(8,128)(2,1)} fusion(f32[1024,1152]{1,0:T(8,128)} %fusion.71, f32[1024,1152]{1,0:T(8,128)} %fusion.70, f32[1024,1152]{1,0:T(8,128)} %fusion.69, f32[3456]{0:T(1024)S(1)} %pad_maximum_fusion.3), kind=kLoop, calls=%fused_computation.8 | loop fusion | flops 14155776 | bytes 21247488 | tf_op jit(solution)/shard_map/convert_element_type | solution.py:1195
  180.2 96.4 %shard_map.230 = (bf16[1024,1152]{1,0:T(8,128)(2,1)}, f32[16,1,1024]{2,1,0:T(1,128)}, bf16[4,4,2,144,1152]{4,3,2,1,0:T(8,128)(2,1)}, bf16[4,2,4,144,1152]{4,3,2,1,0:T(8,128)(2,1)}) custom-call(bf16[1024,3456]{1,0:T(8,128)(2,1)} %fusion.query_ref.key_ref.value_ref, bf16[1024,3456]{1,0:T(8,128)(2,1)} %fusion.query_ref.key_ref.value_ref, ...), custom_call_target="tpu_custom_call" | custom-call | tf_op jit(solution)/shard_map/pallas_call | solution.py:820
  281.4 8.4 %fusion.62 = (f32[1024]{0:T(1024)S(1)}, f32[1024,1152]{1,0:T(8,128)S(1)}, f32[1024,1152]{1,0:T(8,128)}) fusion(f32[1152]{0:T(1024)S(1)} %get-tuple-element.66, bf16[4,256,1152]{2,1,0:T(8,128)(2,1)S(1)} %copy-done.5, f32[1152]{0:T(1024)S(1)} %add.217, bf16[1024,1152]{1,0:T(8,128)(2,1)} %get-tuple-element.40, bf16[1152,1152]{1,0:T(8,128)(2,1)} %bitcast.189), kind=kOutput, calls=%fused_computation.148 | convolution fusion | flops 2723806208 | bytes 16823296 | tf_op jit(solution)/shard_map/dot_general | solution.py:58
  321.0 14.6 %multiply_convert_fusion.1 = bf16[1024,4608]{1,0:T(8,128)(2,1)} fusion(f32[1024,1152]{1,0:T(8,128)} %fusion.75, f32[1024,1152]{1,0:T(8,128)} %fusion.74, f32[1024,1152]{1,0:T(8,128)} %fusion.73, f32[1024,1152]{1,0:T(8,128)} %fusion.72, f32[4608]{0:T(1024)S(1)} %add.226), kind=kLoop, calls=%fused_computation.4 | loop fusion | flops 61341696 | bytes 28329984 | tf_op jit(solution)/shard_map/convert_element_type | solution.py:1205
  339.9 29.9 %convert_reduce_fusion = (f32[4608]{0:T(1024)S(1)}, bf16[1024,4608]{1,0:T(8,128)(2,1)}) fusion(f32[4608]{0:T(1024)S(1)} %add.226, f32[1024,1152]{1,0:T(8,128)} %fusion.75, f32[1024,1152]{1,0:T(8,128)} %fusion.74, f32[1024,1152]{1,0:T(8,128)} %fusion.73, f32[1024,1152]{1,0:T(8,128)} %fusion.72, bf16[1024,1152]{1,0:T(8,128)(2,1)} %bitcast.207, ...), kind=kOutput, calls=%fused_computation.2 | convolution fusion | flops 10980159488 | bytes 41324544 | tf_op jit(solution)/shard_map/dot_general | solution.py:50
  369.9 6.2 fusion.26
  376.0 5.2 fusion.32
  381.3 5.3 fusion.29
  406.2 8.1 %multiply_reduce_fusion = (bf16[1152]{0:T(1024)(128)(2,1)S(1)}, f32[1024]{0:T(1024)S(1)}, f32[1024]{0:T(1024)S(1)}, bf16[1152]{0:T(1024)(128)(2,1)S(1)}, f32[1024,1152]{1,0:T(8,128)S(1)}) fusion(f32[1024,1152]{1,0:T(8,128)S(1)} %bitcast.164, f32[1024]{0:T(1024)S(1)} %add_rsqrt_fusion, f32[1024]{0:T(1024)S(1)} %broadcast_multiply_fusion.4, ...), kind=kOutput, calls=%fused_computation.54 | convolution fusion | flops 2732060672 | bytes 28632064 | tf_op jit(solution)/shard_map/dot_general | solution.py:50
  414.3 5.3 convert_reduce_fusion.4
  419.6 23.2 %fusion.4 = (bf16[1152]{0:T(1024)(128)(2,1)S(1)}, bf16[1152]{0:T(1024)(128)(2,1)S(1)}, bf16[1024,1152]{1,0:T(8,128)(2,1)}, bf16[1024,1152]{1,0:T(8,128)(2,1)S(1)}) fusion(bf16[4,256,1152]{2,1,0:T(8,128)(2,1)} %all-to-all-done.1, f32[1024,1152]{1,0:T(8,128)} %get-tuple-element.102, f32[1024,1152]{1,0:T(8,128)} %get-tuple-element.69, ...), kind=kOutput, calls=%fused_computation.29 | convolution fusion | flops 10885789696 | bytes 41301504 | tf_op jit(solution)/shard_map/dot_general | solution.py:58
  447.4 18.7 %convolution_convert_fusion = bf16[4608,1152]{1,0:T(8,128)(2,1)} fusion(bf16[1024,4608]{1,0:T(8,128)(2,1)} %multiply_convert_fusion.1, bf16[1024,1152]{1,0:T(8,128)(2,1)S(1)} %get-tuple-element.85), kind=kOutput, calls=%fused_computation | convolution fusion | flops 10876944384 | bytes 22413312 | tf_op jit(solution)/shard_map/dot_general | solution.py:54
  466.2 9.8 %pad_maximum_fusion.source_ref = bf16[4,4,2,144,1152]{4,3,2,1,0:T(8,128)(2,1)} fusion(bf16[1,4,2,144,1152]{4,3,2,1,0:T(8,128)(2,1)} %bitcast.191, bf16[1,4,2,144,1152]{4,3,2,1,0:T(8,128)(2,1)} %bitcast.192, bf16[1,4,2,144,1152]{4,3,2,1,0:T(8,128)(2,1)} %bitcast.193, bf16[1,4,2,144,1152]{4,3,2,1,0:T(8,128)(2,1)} %bitcast.194), kind=kLoop, calls=%fused_computation.10 | loop fusion | flops 15925248 | bytes 21233664 | tf_op jit(solution)/shard_map/stack | solution.py:1221
  476.3 6.7 convolution_convert_fusion.9.incoming_ref
  483.1 100.0 %shard_map.231 = (bf16[1024,3456]{1,0:T(8,128)(2,1)}, f32[144,1152]{1,0:T(8,128)}) custom-call(bf16[1024,3456]{1,0:T(8,128)(2,1)} %fusion.query_ref.key_ref.value_ref, bf16[1024,3456]{1,0:T(8,128)(2,1)} %fusion.query_ref.key_ref.value_ref, bf16[1024,3456]{1,0:T(8,128)(2,1)} %fusion.query_ref.key_ref.value_ref, ...), custom_call_target="tpu_custom_call" | custom-call | tf_op jit(solution)/shard_map/pallas_call | solution.py:1009
  587.8 5.3 fusion.39
  596.8 6.5 fusion.22
  604.9 5.9 convolution_convert_fusion.1
  637.1 119.5 %shard_map.232 = (f32[2,4,40,1152]{3,2,1,0:T(8,128)S(1)}, bf16[4,256,1152]{2,1,0:T(8,128)(2,1)S(1)}, bf16[32,64,128]{2,1,0:T(8,128)(2,1)S(1)}, f32[32,8,128]{2,1,0:T(8,128)S(1)}) custom-call(bf16[4,4,2,144,1152]{4,3,2,1,0:T(8,128)(2,1)} %pad_maximum_fusion.1.grad_ref, bf16[4,256,1152]{2,1,0:T(8,128)(2,1)} %fusion.3.token_ref, ...), custom_call_target="tpu_custom_call" | custom-call | tf_op jit(solution)/shard_map/pallas_call | solution.py:1091
  759.8 11.8 %shard_map.233 = f32[32,8,128]{2,1,0:T(8,128)} custom-call(f32[8,8,128]{2,1,0:T(8,128)} %pad.30.part_ref), custom_call_target="tpu_custom_call" | custom-call | tf_op jit(solution)/shard_map/pallas_call | solution.py:1123
  (210 shorter events, 152.3 us)
Async XLA Ops:
  7.2 31.2 %copy-start = (bf16[36,6912]{1,0:T(8,128)(2,1)S(1)}, bf16[36,6912]{1,0:T(8,128)(2,1)}, u32[]{:S(2)}) copy-start(bf16[36,6912]{1,0:T(8,128)(2,1)} %param.16) | copy-start | bytes 1492996
  38.3 105.5 %copy-start.27 = (f32[32,1152]{1,0:T(8,128)}, f32[32,1152]{1,0:T(8,128)S(1)}, u32[]{:S(2)}) copy-start(f32[32,1152]{1,0:T(8,128)S(1)} %slice.204) | copy-start | bytes 442372
  145.0 10.6 %copy-start.28 = (f32[1152]{0:T(1024)}, f32[1152]{0:T(1024)S(1)}, u32[]{:S(2)}) copy-start(f32[1152]{0:T(1024)S(1)} %get-tuple-element.64) | copy-start | bytes 13828
  145.0 10.6 %copy-start.30 = (f32[1152]{0:T(1024)}, f32[1152]{0:T(1024)S(1)}, u32[]{:S(2)}) copy-start(f32[1152]{0:T(1024)S(1)} %get-tuple-element.65) | copy-start | bytes 13828
  149.5 6.1 copy-start.5
  155.6 6.1 copy-start.10
  155.6 6.1 copy-start.12
  155.6 11.3 %copy-start.14 = (bf16[1,4,2,144,1152]{4,3,2,1,0:T(8,128)(2,1)}, bf16[1,4,2,144,1152]{4,3,2,1,0:T(8,128)(2,1)S(1)}, u32[]{:S(2)}) copy-start(bf16[1,4,2,144,1152]{4,3,2,1,0:T(8,128)(2,1)S(1)} %get-tuple-element.81) | copy-start | bytes 7962628
  276.6 59.0 %all-to-all-start.1 = ((bf16[4,256,1152]{2,1,0:T(8,128)(2,1)}), bf16[4,256,1152]{2,1,0:T(8,128)(2,1)}, u32[]{:S(2)}, u32[]{:S(2)}) async-start(bf16[4,256,1152]{2,1,0:T(8,128)(2,1)} %bitcast.206), calls=%async_computation.1 | async-start | bytes 4718592 | tf_op jit(solution)/shard_map/all_to_all | solution.py:1209
  281.4 11.2 %slice-start.4 = ((s8[10616832]{0:T(1024)(128)(4,1)}), s8[4194304]{0:T(1024)(128)(4,1)S(1)}, s32[]{:S(2)}) async-start(s8[10616832]{0:T(1024)(128)(4,1)} %bitcast.169), calls=%async_computation.8 | async-start | bytes 8388608
  281.4 11.2 %slice-start.5 = ((s8[10616832]{0:T(1024)(128)(4,1)}), s8[4194304]{0:T(1024)(128)(4,1)S(1)}, s32[]{:S(2)}) async-start(s8[10616832]{0:T(1024)(128)(4,1)} %bitcast.169), calls=%async_computation.9 | async-start | bytes 8388608
  281.4 11.2 %slice-start.6 = ((s8[10616832]{0:T(1024)(128)(4,1)}), s8[2228224]{0:T(1024)(128)(4,1)S(1)}, s32[]{:S(2)}) async-start(s8[10616832]{0:T(1024)(128)(4,1)} %bitcast.169), calls=%async_computation.10 | async-start | bytes 4456448
  299.1 15.4 %copy-start.24 = (bf16[1024,1152]{1,0:T(8,128)(2,1)}, bf16[1024,1152]{1,0:T(8,128)(2,1)S(1)}, u32[]{:S(2)}) copy-start(bf16[1024,1152]{1,0:T(8,128)(2,1)S(1)} %add_convert_fusion.1) | copy-start | bytes 7077892
  369.8 6.2 copy-start.20
  369.9 6.2 copy-start.26
  396.2 9.9 %slice-start = ((s8[4718592]{0:T(1024)(128)(4,1)}), s8[4194304]{0:T(1024)(128)(4,1)S(1)}, s32[]{:S(2)}) async-start(s8[4718592]{0:T(1024)(128)(4,1)} %bitcast.163), calls=%async_computation.4 | async-start | bytes 8388608
  442.8 344.7 %all-to-all-start = ((bf16[4,256,1152]{2,1,0:T(8,128)(2,1)}), bf16[4,256,1152]{2,1,0:T(8,128)(2,1)}, u32[]{:S(2)}, u32[]{:S(2)}) async-start(bf16[4,256,1152]{2,1,0:T(8,128)(2,1)} %bitcast.16), calls=%async_computation | async-start | bytes 4718592 | tf_op jit(solution)/shard_map/all_to_all | solution.py:1209
  447.3 340.2 %reduce-scatter.2.cloned.1.call-start = ((), (), s32[]{:S(2)}) async-start(), calls=%async_computation.3 | async-start | bytes 10948608 | tf_op jit(solution)/shard_map/reduce_scatter | solution.py:1217
  466.1 9.9 %copy-start.33 = (f32[1152]{0:T(1024)S(1)}, f32[1152]{0:T(1024)}, u32[]{:S(2)}) copy-start(f32[1152]{0:T(1024)} %get-tuple-element.70) | copy-start | bytes 13828
  466.1 10.2 %copy-start.16 = (bf16[1,4,2,144,1152]{4,3,2,1,0:T(8,128)(2,1)S(1)}, bf16[1,4,2,144,1152]{4,3,2,1,0:T(8,128)(2,1)}, u32[]{:S(2)}) copy-start(bf16[1,4,2,144,1152]{4,3,2,1,0:T(8,128)(2,1)} %get-tuple-element.78) | copy-start | bytes 7962628
  596.8 6.5 copy-start.36
  610.8 7.3 slice-start.9
  618.1 9.7 %slice-start.2 = ((s8[4718592]{0:T(1024)(128)(4,1)}), s8[4194304]{0:T(1024)(128)(4,1)S(1)}, s32[]{:S(2)}) async-start(s8[4718592]{0:T(1024)(128)(4,1)} %bitcast.166), calls=%async_computation.6 | async-start | bytes 8388608
  779.8 6.1 copy-start.2
  (27 other events, 118.2 us)
Sparse Core Ops, SparseCore 0:
  466.3 165.7 reduce-scatter.1

commit v3 on v2

--- a/solution.py
+++ b/solution.py
@@ -88,7 +88,7 @@
 
 
 def attend_backward_kernel(
-    query_ref, key_ref, value_ref, incoming_ref, log_ref, grad_ref, key_total, value_total
+    query_ref, key_ref, value_ref, incoming_ref, log_ref, grad_ref, score_grads, weights
 ):
     features = query_ref.shape[1]
     start, inside = head_window(features)
@@ -97,27 +97,30 @@
     values = jnp.where(inside, value_ref[:, window], 0)
     scale = HD**-0.5
     factor = scale * LOG2E
-    for block in range(query_ref.shape[0] // QUERY_BLOCK):
+    count = query_ref.shape[0] // QUERY_BLOCK
+    turned = keys.T
+
+    def begin(block):
         rows = pl.ds(block * QUERY_BLOCK, QUERY_BLOCK)
-        queries = query_ref[rows, window]
-        incoming = incoming_ref[rows, window]
-        probs = jnp.exp2(dot_nt(keys, queries) * factor - log_ref[0, :, rows])
-        prob_grad = dot_nt(values, incoming)
+        return dot_nt(keys, query_ref[rows, window]), dot_nt(values, incoming_ref[rows, window])
+
+    following = begin(0)
+    for block in range(count):
+        rows = pl.ds(block * QUERY_BLOCK, QUERY_BLOCK)
+        scores, prob_grad = following
+        if block + 1 < count:
+            following = begin(block + 1)
+        probs = jnp.exp2(scores * factor - log_ref[0, :, rows])
         centre = jnp.sum(probs * prob_grad, axis=0, keepdims=True)
-        score_grad = (probs * (prob_grad - centre) * scale).astype(BF16)
-        key_part = dot_nn(score_grad, queries)
-        value_part = dot_nn(probs.astype(BF16), incoming)
-        if block == 0:
-            key_total[...] = key_part
-            value_total[...] = value_part
-        else:
-            key_total[...] += key_part
-            value_total[...] += value_part
-        query_grad = dot_tn(keys, score_grad).T.astype(grad_ref.dtype)
+        score_grads[:, rows] = (probs * (prob_grad - centre) * scale).astype(BF16)
+        weights[:, rows] = probs.astype(BF16)
+        query_grad = dot_nn(turned, score_grads[:, rows]).T.astype(grad_ref.dtype)
         grad_ref[rows, window] = jnp.where(inside, query_grad, grad_ref[rows, window])
+    key_total = dot_nn(score_grads[...], query_ref[:, window])
+    value_total = dot_nn(weights[...], incoming_ref[:, window])
     for part, total in ((1, key_total), (2, value_total)):
         place = pl.ds(pl.multiple_of(start + part * features, LANES), WINDOW)
-        grad_ref[:, place] = jnp.where(inside, total[...].astype(grad_ref.dtype), grad_ref[:, place])
+        grad_ref[:, place] = jnp.where(inside, total.astype(grad_ref.dtype), grad_ref[:, place])
 
 
 def whole_block(shape, column):
@@ -170,7 +173,7 @@
         ],
         out_specs=whole_block((tokens, 3 * features), 0),
         out_shape=jax.ShapeDtypeStruct((tokens, 3 * features), kind),
-        scratch_shapes=[pltpu.VMEM((tokens, WINDOW), F32), pltpu.VMEM((tokens, WINDOW), F32)],
+        scratch_shapes=[pltpu.VMEM((tokens, rows), BF16), pltpu.VMEM((tokens, rows), BF16)],
         compiler_params=pltpu.CompilerParams(vmem_limit_bytes=56 * 1024 * 1024),
         cost_estimate=pl.CostEstimate(
             flops=10 * rows * tokens * HEADS * WINDOW,
@@ -419,6 +422,7 @@
 MESH = pl.DeviceIdType.MESH
 ANY = pl.BlockSpec(memory_space=pl.ANY)
 ROWS = 144
+MATMUL_ROWS = 1024
 
 
 class Here:
@@ -535,7 +539,10 @@
     return lambda: lax.fori_loop(1, 16, wait, 0)
 
 
-def introduce_kernel(note_ref, shard_ref, notes_ref, blocks_ref, landing, wide, note_sent, note_landed, sent, landed, local):
+def introduce_kernel(
+    note_ref, shard_ref, shrink_ref, notes_ref, blocks_ref, quad_ref, landing, wide, buffer,
+    note_sent, note_landed, sent, landed, local,
+):
     here = Here()
     greet_all(here)
     wires = Wires(sent, landed)
@@ -547,14 +554,22 @@
     for step in range(1, 4):
         place = lax.rem(here.member + step, 4)
         quads.append(wires.copy(step - 1, columns(place), landing.at[here.member], here.at_member(step)))
+    shrinks = [
+        wires.copy(2 + step, shrink_ref, quad_ref.at[here.member], here.at_member(step)) for step in range(1, 4)
+    ]
     for copy in quads:
         copy.start()
+    keep = Bounce(shrink_ref, buffer, quad_ref.at[here.member], local.at[2])
+    keep.start()
     done = everyone(here, lambda place: note_ref.at[0], notes_ref, note_sent, note_landed)
     own = pltpu.make_async_copy(columns(here.member), landing.at[here.member], local.at[0])
     own.start()
     mine = pltpu.make_async_copy(note_ref.at[0], notes_ref.at[here.index], local.at[1])
     mine.start()
+    for copy in shrinks:
+        copy.start()
     own.wait()
+    keep.go_on()
     for copy in quads:
         copy.wait_recv()
     for part in range(2):
@@ -563,30 +578,51 @@
         blocks_ref[part] = wide[...].astype(BF16)
     for copy in quads:
         copy.wait_send()
+    for copy in shrinks:
+        copy.wait()
+    keep.wait()
     mine.wait()
     done()
 
 
-def introduce(note, shard):
+def introduce(note, shard, shrink):
     return pl.pallas_call(
         introduce_kernel,
-        in_specs=[ANY, ANY],
-        out_specs=[ANY, pl.BlockSpec(memory_space=pltpu.VMEM)],
+        in_specs=[ANY, ANY, ANY],
+        out_specs=[ANY, pl.BlockSpec(memory_space=pltpu.VMEM), ANY],
         out_shape=[
             jax.ShapeDtypeStruct((32,) + note.shape[1:], note.dtype),
             jax.ShapeDtypeStruct((2, ROWS, 1152), BF16),
+            jax.ShapeDtypeStruct((4, ROWS, 1152), BF16),
         ],
         scratch_shapes=[
             pltpu.VMEM((4,) + shard.shape[:2] + (1152,), BF16),
             pltpu.VMEM((ROWS, 1152), F32),
+            pltpu.VMEM((ROWS, 1152), BF16),
             pltpu.SemaphoreType.DMA((32,)),
             pltpu.SemaphoreType.DMA((32,)),
+            pltpu.SemaphoreType.DMA((6,)),
+            pltpu.SemaphoreType.DMA((6,)),
             pltpu.SemaphoreType.DMA((3,)),
-            pltpu.SemaphoreType.DMA((3,)),
-            pltpu.SemaphoreType.DMA((2,)),
         ],
         compiler_params=pltpu.CompilerParams(collective_id=1, has_side_effects=True),
-    )(note, shard)
+    )(note, shard, shrink)
+
+
+class Bounce:
+    def __init__(self, source, buffer, target, semaphore):
+        self.first = pltpu.make_async_copy(source, buffer, semaphore)
+        self.second = pltpu.make_async_copy(buffer, target, semaphore)
+
+    def start(self):
+        self.first.start()
+
+    def go_on(self):
+        self.first.wait()
+        self.second.start()
+
+    def wait(self):
+        self.second.wait()
 
 
 ARRIVALS = (0, 1, 3, 2)
@@ -661,8 +697,8 @@
 
 
 def open_kernel(
-    block_ref, shrink_ref, part_ref, token_ref, full_ref, expand_ref, shrinks_ref, parts_ref, tokens_ref,
-    part_mine, part_half, part_sent, part_landed, sent, landed, more_sent, more_landed, local,
+    block_ref, part_ref, token_ref, full_ref, expand_ref, parts_ref, tokens_ref,
+    part_mine, part_half, block_buffer, token_buffer, part_sent, part_landed, sent, landed, more_sent, more_landed, local,
 ):
     here = Here()
     greet_all(here)
@@ -679,14 +715,12 @@
         landed.at[0],
     )
     second = Gather(here, None, lambda z: expand_ref.at[z], sent.at[1], landed.at[1])
-    third = Gather(here, None, lambda z: shrinks_ref.at[z], sent.at[2], landed.at[2])
     first.begin(block_ref.at[0])
     mine = here.z * 4 + here.member
     own = [
-        pltpu.make_async_copy(block_ref.at[0], first.own(here.z), local.at[1]),
-        pltpu.make_async_copy(block_ref.at[1], second.own(here.z), local.at[2]),
-        pltpu.make_async_copy(shrink_ref, third.own(here.z), local.at[3]),
-        pltpu.make_async_copy(token_ref.at[here.member], tokens_ref.at[here.member], local.at[4]),
+        Bounce(block_ref.at[0], block_buffer.at[0], first.own(here.z), local.at[1]),
+        Bounce(block_ref.at[1], block_buffer.at[1], second.own(here.z), local.at[2]),
+        Bounce(token_ref.at[here.member], token_buffer, tokens_ref.at[here.member], local.at[3]),
     ]
     for copy in own:
         copy.start()
@@ -696,6 +730,8 @@
         moved.append(more.copy(step, token_ref.at[place], tokens_ref.at[here.member], here.at_member(step)))
     for copy in moved:
         copy.start()
+    for copy in own:
+        copy.go_on()
     load.wait()
     half.wait()
 
@@ -705,7 +741,7 @@
 
     lax.fori_loop(0, 16, add, 0)
     done = same_core(here, part_mine, parts_ref, part_sent, part_landed)
-    keep = pltpu.make_async_copy(part_mine.at[mine], parts_ref.at[mine], local.at[5])
+    keep = pltpu.make_async_copy(part_mine.at[mine], parts_ref.at[mine], local.at[4])
     keep.start()
     own[0].wait()
     first.spread(0)
@@ -713,7 +749,6 @@
         first.along(ARRIVALS[order], block_ref.at[0]).wait_recv()
         first.spread(order)
     second.begin(block_ref.at[1])
-    third.begin(shrink_ref)
     for order in range(4):
         first.relay(order)
     for order in range(4):
@@ -722,7 +757,6 @@
     for step in (1, 3, 2):
         first.along(step, block_ref.at[0]).wait_send()
         second.along(step, block_ref.at[1]).wait()
-        third.along(step, shrink_ref).wait()
     for copy in moved:
         copy.wait()
     for copy in own[1:]:
@@ -731,117 +765,346 @@
     done()
 
 
-def open_up(blocks, shrink, parts, tokens):
+def open_up(blocks, parts, tokens):
     column = jax.ShapeDtypeStruct((4, ROWS, 1152), BF16)
     return pl.pallas_call(
         open_kernel,
-        in_specs=[ANY] * 4,
-        out_specs=[ANY] * 5,
+        in_specs=[ANY] * 3,
+        out_specs=[ANY] * 4,
         out_shape=[
             jax.ShapeDtypeStruct((4, 4, 2, ROWS, 1152), BF16),
             column,
-            column,
             jax.ShapeDtypeStruct(parts.shape[1:], parts.dtype),
             jax.ShapeDtypeStruct(tokens.shape, tokens.dtype),
         ],
         scratch_shapes=[
             pltpu.VMEM(parts.shape[1:], F32),
             pltpu.VMEM(parts.shape[1:], F32),
+            pltpu.VMEM((2, ROWS, 1152), BF16),
+            pltpu.VMEM(tokens.shape[1:], BF16),
             pltpu.SemaphoreType.DMA((16,)),
             pltpu.SemaphoreType.DMA((16,)),
-            pltpu.SemaphoreType.DMA((3, 31)),
-            pltpu.SemaphoreType.DMA((3, 31)),
-            pltpu.SemaphoreType.DMA((4,)),
-            pltpu.SemaphoreType.DMA((4,)),
+            pltpu.SemaphoreType.DMA((2, 31)),
+            pltpu.SemaphoreType.DMA((2, 31)),
+            pltpu.SemaphoreType.DMA((7,)),
+            pltpu.SemaphoreType.DMA((7,)),
             pltpu.SemaphoreType.DMA((6,)),
         ],
         compiler_params=pltpu.CompilerParams(collective_id=2, has_side_effects=True),
-    )(blocks, shrink, parts, tokens)
-
-
-def forward_gather_kernel(
-    query_ref, key_ref, value_ref, expand_column, shrink_column, mixed_ref, log_ref, expand_full, shrink_full,
-    sent, landed, local,
+    )(blocks, parts, tokens)
+
+
+class Column:
+    COPIES = 13
+
+    def __init__(self, here, full, quad, sent, landed):
+        self.here, self.full, self.quad = here, full, quad
+        self.wires = Wires(sent, landed)
+
+    def pass_on(self, way, turn):
+        here = self.here
+        source = self.quad if turn == 0 else self.full.at[here.z - way * turn, here.core]
+        target = self.full.at[here.z - way * turn, here.core]
+        partner = ((here.z + way) * 2 + here.core, here.member)
+        return self.wires.copy(turn + (3 if way < 0 else 0), source, target, partner)
+
+    def arrival(self, way, turn):
+        here = self.here
+        ref = self.full.at[here.z - way * (turn + 1), here.core]
+        return self.wires.copy(turn + (3 if way < 0 else 0), ref, ref, here.at_core())
+
+    def across(self, way, turn):
+        here = self.here
+        ref = self.full.at[here.z - way * (turn + 1), here.core]
+        return self.wires.copy(6 + turn + (3 if way < 0 else 0), ref, ref, here.at_core())
+
+    def own_across(self):
+        here = self.here
+        return self.wires.copy(12, self.quad, self.full.at[here.z, here.core], here.at_core())
+
+    def sends(self, way, turn):
+        z = self.here.z
+        return (z < 3) & (z >= turn) if way > 0 else (z > 0) & (z <= 3 - turn)
+
+    def comes(self, way, turn):
+        z = self.here.z
+        return z >= turn + 1 if way > 0 else z <= 2 - turn
+
+    def start(self, turn):
+        for way in (1, -1):
+            pl.when(self.sends(way, turn))(lambda way=way: self.pass_on(way, turn).start())
+        if turn == 0:
+            self.own_across().start()
+
+    def take(self, turn):
+        for way in (1, -1):
+
+            @pl.when(self.comes(way, turn))
+            def _():
+                self.arrival(way, turn).wait_recv()
+                self.across(way, turn).start()
+
+    def step(self, turn):
+        for way in (1, -1):
+
+            @pl.when(self.comes(way, turn - 1))
+            def _():
+                self.arrival(way, turn - 1).wait_recv()
+            if turn < 3:
+                pl.when(self.sends(way, turn))(lambda way=way: self.pass_on(way, turn).start())
+            pl.when(self.comes(way, turn - 1))(lambda way=way: self.across(way, turn - 1).start())
+
+    def end(self):
+        self.own_across().wait()
+        for way in (1, -1):
+            for turn in range(3):
+                pl.when(self.comes(way, turn))(lambda way=way, turn=turn: self.across(way, turn).wait())
+                pl.when(self.sends(way, turn))(lambda way=way, turn=turn: self.pass_on(way, turn).wait_send())
+
+
+MIX_AT = 19
+EXPAND_AT = MIX_AT + 4
+FORWARD_STEPS = EXPAND_AT + 4
+
+
+def forward_kernel(
+    hidden_ref, weight_ref, bias_ref, latent_ref, scaling_ref, expand_bias_ref, expand_column, shrink_quad, incoming_ref,
+    projected_ref, mixed_ref, log_ref, branch_ref, middle_ref, second_ref, pre_ref, active_ref,
+    expand_full, shrink_full, incomings_ref,
+    chunk, token_buffer, sent, landed, more_sent, more_landed, local, fetch,
 ):
-    head = pl.program_id(0)
+    step = pl.program_id(0)
     here = Here()
+    features = hidden_ref.shape[1]
     second = Gather(
         here,
         lambda member, z, core: expand_full.at[member, z, core],
         lambda z: expand_column.at[z],
-        sent.at[0],
-        landed.at[0],
-    )
-    third = Gather(
-        here,
-        lambda member, z, core: shrink_full.at[z, core, member],
-        lambda z: shrink_column.at[z],
-        sent.at[1],
-        landed.at[1],
-    )
+        sent,
+        landed,
+    )
+    third = Column(here, shrink_full, shrink_quad, more_sent.at[pl.ds(0, 13)], more_landed.at[pl.ds(0, 13)])
+    more = Wires(more_sent, more_landed)
     own = (
-        pltpu.make_async_copy(expand_column, expand_full.at[here.member, :, here.core], local.at[0]),
-        pltpu.make_async_copy(shrink_column, shrink_full.at[:, here.core, here.member], local.at[1]),
-    )
-
-    @pl.when(head == 0)
+        Bounce(expand_column, chunk.at[0, :, 0], expand_full.at[here.member, :, here.core], local.at[0]),
+        Bounce(shrink_quad, chunk.at[1, :, 0], shrink_full.at[here.z, here.core], local.at[1]),
+        Bounce(incoming_ref.at[here.member], token_buffer, incomings_ref.at[here.member], local.at[2]),
+    )
+
+    def fetch_chunk(part):
+        return pltpu.make_async_copy(expand_full.at[part], chunk.at[part % 2], fetch.at[part % 2])
+
+    def move(number):
+        place = lax.rem(here.member + number, 4)
+        return more.copy(
+            12 + number, incoming_ref.at[place], incomings_ref.at[here.member], here.at_member(number)
+        )
+
+    @pl.when(step == 0)
     def _():
-        greet((here.at_x(), here.at_y(), here.at_core()))
-        for gather in (second, third):
-            for order in range(4):
-                gather.spread(order)
+        greet_near(here)
+        for order in range(4):
+            second.spread(order)
+        third.start(0)
         for copy in own:
             copy.start()
 
-    for order, turn in enumerate((6, 8, 10, 12)):
-
-        @pl.when(head == turn)
-        def _():
+    @pl.when(step == 1)
+    def _():
+        for copy in own:
+            copy.go_on()
+
+    def relay_expand():
+        for order in range(4):
             second.relay(order)
-
-    attend_forward_kernel(query_ref, key_ref, value_ref, mixed_ref, log_ref)
-
-    @pl.when(head == HEADS - 1)
-    def _():
+        for number in (2, 1, 3):
+            move(number).start()
+
+    def close_expand():
         for order in range(4):
-            third.relay(order)
-        for gather in (second, third):
-            for order in range(4):
-                gather.close(order)
-        for gather in (second, third):
-            gather.end()
+            second.close(order)
+
+    def finish_expand():
+        second.end()
         for copy in own:
             copy.wait()
-
-
-def attend_forward_gather(projected, expand_column, shrink_column):
-    rows = projected.shape[0]
-    features = projected.shape[1] // 3
+        fetch_chunk(0).start()
+        fetch_chunk(1).start()
+
+    def finish():
+        third.step(3)
+        third.end()
+        for number in (1, 2, 3):
+            move(number).wait()
+
+    for turn, action in (
+        (12, relay_expand),
+        (12, functools.partial(third.step, 1)),
+        (19, close_expand),
+        (EXPAND_AT + 1, functools.partial(third.step, 2)),
+        (EXPAND_AT - 1, finish_expand),
+    ):
+        pl.when(step == turn)(action)
+
+    def row_blocks(body):
+        def one(block, carry):
+            body(pl.ds(pl.multiple_of(block * MATMUL_ROWS, MATMUL_ROWS), MATMUL_ROWS))
+            return carry
+
+        lax.fori_loop(0, hidden_ref.shape[0] // MATMUL_ROWS, one, 0)
+
+    for part in range(3):
+
+        @pl.when(step == part)
+        def _():
+            def project(rows):
+                values = dot_nn(hidden_ref[rows, :], weight_ref[0]) + bias_ref[part]
+                projected_ref[rows, part * features : (part + 1) * features] = values.astype(BF16)
+
+            row_blocks(project)
+
+    @pl.when((step >= 3) & (step < MIX_AT))
+    def _():
+        forward_head(step - 3, features, projected_ref, mixed_ref, log_ref)
+
+    @pl.when((step >= MIX_AT) & (step < EXPAND_AT))
+    def _():
+        rows = pl.ds(pl.multiple_of((step - MIX_AT) * 256, 256), 256)
+        branch = dot_nn(mixed_ref[rows, :], weight_ref[0]) + bias_ref[3]
+        branch_ref[...] = branch
+        middle = latent_ref[...].astype(F32) + scaling_ref[0] * branch
+        middle_ref[...] = middle
+        normed, _ = norm_parts(middle)
+        second_ref[rows, :] = (normed * (1.0 + scaling_ref[2]) + scaling_ref[1]).astype(BF16)
+
+    for part in range(4):
+
+        @pl.when(step == EXPAND_AT + part)
+        def _():
+            fetch_chunk(part).wait()
+
+            def expand(rows):
+                weight = chunk[part % 2].reshape(features, features)
+                values = dot_nn(second_ref[rows, :], weight) + expand_bias_ref[part]
+                pre_ref[rows, :] = values
+                active_ref[rows, :] = gelu_parts(values)[0].astype(BF16)
+
+            row_blocks(expand)
+            if part + 2 < 4:
+                fetch_chunk(part + 2).start()
+
+    pl.when(step == FORWARD_STEPS - 1)(finish)
+
+
+def forward_head(head, features, projected_ref, mixed_ref, log_ref):
+    last = features // LANES - WINDOW // LANES
+    start = jnp.minimum(head * HD // LANES, last) * LANES
+    first = head * HD - start
+    lane = lax.broadcasted_iota(jnp.int32, (1, WINDOW), 1)
+    inside = (lane >= first) & (lane < first + HD)
+
+    def window(part):
+        return pl.ds(pl.multiple_of(start + part * features, LANES), WINDOW)
+
+    keys = jnp.where(inside, projected_ref[:, window(1)], 0)
+    values = jnp.where(inside, projected_ref[:, window(2)], 0)
+    turned = values.T
+    factor = HD**-0.5 * LOG2E
+    count = projected_ref.shape[0] // QUERY_BLOCK
+
+    def score(block):
+        return dot_nt(keys, projected_ref[pl.ds(block * QUERY_BLOCK, QUERY_BLOCK), window(0)])
+
+    following = score(0)
+    for block in range(count):
+        rows = pl.ds(block * QUERY_BLOCK, QUERY_BLOCK)
+        scores = following
+        if block + 1 < count:
+            following = score(block + 1)
+        peak = jnp.max(scores, axis=0, keepdims=True)
+        powers = jnp.exp2(scores * factor - peak * factor)
+        total = jnp.sum(powers, axis=0, keepdims=True)
+        log_ref[0, :, rows] = peak * factor + jnp.log2(total)
+        weights = (powers * (1.0 / total)).astype(BF16)
+        mixed = dot_nn(turned, weights).T.astype(BF16)
+        mixed_ref[rows, window(0)] = jnp.where(inside, mixed, mixed_ref[rows, window(0)])
+
+
+def greet_near(here):
+    greet(
+        [here.at_member(step) for step in range(1, 4)]
+        + [here.at_z(step) for step in range(1, 4)]
+        + [here.at_core()]
+    )
+
+
+def forward(hidden, weights, biases, latents, scalings, expand_bias, expand_column, shrink_quad, incoming):
+    rows, features = hidden.shape
+
+    def clip(step, low, high):
+        return jnp.minimum(jnp.maximum(step - low, 0), high)
+
+    def everything(shape):
+        return pl.BlockSpec(shape, lambda step: (0,) * len(shape), pipeline_mode=pl.Buffered(1))
+
+    by_rows = pl.BlockSpec((256, features), lambda step: (clip(step, MIX_AT, 3), 0))
+    by_part = pl.BlockSpec((rows, features), lambda step: (0, clip(step, EXPAND_AT, 3)))
+    tokens = jax.ShapeDtypeStruct((rows, features), BF16)
+    wide = jax.ShapeDtypeStruct((rows, features), F32)
     return pl.pallas_call(
-        forward_gather_kernel,
-        grid=(HEADS,),
-        in_specs=[whole_block((rows, features), part) for part in range(3)] + [ANY] * 2,
-        out_specs=[
-            whole_block((rows, features), 0),
-            pl.BlockSpec((1, 1, rows), lambda head: (head, 0, 0)),
+        forward_kernel,
+        grid=(FORWARD_STEPS,),
+        in_specs=[
+            everything((rows, features)),
+            pl.BlockSpec((1, features, features), lambda step: (jnp.minimum(step, 3), 0, 0)),
+            everything((4, 1, features)),
+            by_rows,
+            everything((3, 1, features)),
+            everything((4, 1, features)),
             ANY,
             ANY,
+            ANY,
+        ],
+        out_specs=[
+            everything((rows, 3 * features)),
+            everything((rows, features)),
+            pl.BlockSpec((1, 1, rows), lambda step: (clip(step, 3, HEADS - 1), 0, 0)),
+            by_rows,
+            by_rows,
+            everything((rows, features)),
+            by_part,
+            by_part,
+            ANY,
+            ANY,
+            ANY,
         ],
         out_shape=[
-            jax.ShapeDtypeStruct((rows, features), BF16),
+            jax.ShapeDtypeStruct((rows, 3 * features), BF16),
+            tokens,
             jax.ShapeDtypeStruct((HEADS, 1, rows), F32),
+            wide,
+            wide,
+            tokens,
+            jax.ShapeDtypeStruct((rows, 4 * features), F32),
+            jax.ShapeDtypeStruct((rows, 4 * features), BF16),
             jax.ShapeDtypeStruct((4, 4, 2, ROWS, 1152), BF16),
             jax.ShapeDtypeStruct((4, 2, 4, ROWS, 1152), BF16),
+            jax.ShapeDtypeStruct(incoming.shape, BF16),
         ],
         scratch_shapes=[
-            pltpu.SemaphoreType.DMA((2, 31)),
-            pltpu.SemaphoreType.DMA((2, 31)),
+            pltpu.VMEM((2, 4, 2, ROWS, 1152), BF16),
+            pltpu.VMEM(incoming.shape[1:], BF16),
+            pltpu.SemaphoreType.DMA((31,)),
+            pltpu.SemaphoreType.DMA((31,)),
+            pltpu.SemaphoreType.DMA((16,)),
+            pltpu.SemaphoreType.DMA((16,)),
+            pltpu.SemaphoreType.DMA((3,)),
             pltpu.SemaphoreType.DMA((2,)),
         ],
         compiler_params=pltpu.CompilerParams(
-            collective_id=5, has_side_effects=True, vmem_limit_bytes=56 * 1024 * 1024
+            collective_id=5, has_side_effects=True, vmem_limit_bytes=60 * 1024 * 1024
         ),
-    )(projected, projected, projected, expand_column, shrink_column)
+    )(hidden, weights, biases, latents, scalings, expand_bias, expand_column, shrink_quad, incoming)
 
 
 class Reduce:
@@ -864,13 +1127,13 @@
 
     def load(self, turn):
         return pltpu.make_async_copy(
-            self.source.at[self.order[turn], :, self.here.core], self.kept.at[turn], self.local.at[turn]
+            self.source(self.order[turn], self.here.core), self.kept.at[turn], self.local.at[turn]
         )
 
     def cross(self, turn):
         here = self.here
         return self.wires.copy(
-            turn, self.source.at[self.order[turn], :, 1 - here.core], self.crossed.at[turn], here.at_core()
+            turn, self.source(self.order[turn], 1 - here.core), self.crossed.at[turn], here.at_core()
         )
 
     def relay(self, way):
@@ -988,14 +1251,14 @@
 ):
     head = pl.program_id(0)
     here = Here()
-    reduce = Reduce(here, source_ref, total_ref, *scratch)
+    reduce = Reduce(here, lambda member, core: source_ref.at[member, :, core], total_ref, *scratch)
 
     @pl.when(head == 0)
     def _():
         greet((here.at_x(), here.at_y(), here.at_core(), here.at_z(1), here.at_z(2), here.at_z(3)))
 
     steps = reduce.steps()
-    for step, turn in zip(steps[:-1], (0, 1, 1, 2, 2, 4, 4, 10)):
+    for step, turn in zip(steps[:-1], (0, 2, 6, 6, 6, 6, 6, 13)):
         pl.when(head == turn)(step)
     attend_backward_kernel(
         query_ref, key_ref, value_ref, incoming_ref, log_ref, grad_ref, key_total, value_total
@@ -1016,122 +1279,431 @@
             jax.ShapeDtypeStruct((rows, 3 * features), BF16),
             jax.ShapeDtypeStruct((ROWS, features), F32),
         ],
-        scratch_shapes=[pltpu.VMEM((rows, WINDOW), F32), pltpu.VMEM((rows, WINDOW), F32), *Reduce.SCRATCH],
+        scratch_shapes=[pltpu.VMEM((rows, rows), BF16), pltpu.VMEM((rows, rows), BF16), *Reduce.SCRATCH],
         compiler_params=pltpu.CompilerParams(
             collective_id=6, has_side_effects=True, vmem_limit_bytes=58 * 1024 * 1024
         ),
     )(projected, projected, projected, incoming, log_total, source)
 
 
+def clipped(step, low, high):
+    return jnp.minimum(jnp.maximum(step - low, 0), high)
+
+
+def everything(shape):
+    return pl.BlockSpec(shape, lambda step: (0,) * len(shape), pipeline_mode=pl.Buffered(1))
+
+
+def turn_kernel(
+    active_ref, shrink_ref, middle_ref, incoming_ref, gate_ref, bias_ref,
+    tokens_ref, back_ref, grads_ref, sums_ref, total, token, sent, landed, local,
+):
+    step = pl.program_id(0)
+    here = Here()
+    wires = Wires(sent, landed)
+
+    def move(number):
+        place = lax.rem(here.member + number, 4)
+        return wires.copy(number - 1, token.at[place], tokens_ref.at[here.member], here.at_member(number))
+
+    own = pltpu.make_async_copy(token.at[here.member], tokens_ref.at[here.member], local.at[0])
+
+    @pl.when(step == 0)
+    def _():
+        greet([here.at_member(number) for number in range(1, 4)])
+        sums_ref[...] = jnp.zeros_like(sums_ref)
+
+    def blocks(body):
+        def one(block, carry):
+            body(pl.ds(pl.multiple_of(block * MATMUL_ROWS, MATMUL_ROWS), MATMUL_ROWS))
+            return carry
+
+        lax.fori_loop(0, total.shape[0] // MATMUL_ROWS, one, 0)
+
+    @pl.when(step == 0)
+    def _():
+        def first(rows):
+            total[rows, :] = dot_nn(active_ref[rows, :], shrink_ref[...])
+
+        blocks(first)
+
+    @pl.when((step > 0) & (step < 4))
+    def _():
+        def more(rows):
+            total[rows, :] += dot_nn(active_ref[rows, :], shrink_ref[...])
+
+        blocks(more)
+
+    @pl.when((step >= 4) & (step < 8))
+    def _():
+        rows = pl.ds(pl.multiple_of((step - 4) * 256, 256), 256)
+        branch = total[rows, :] + bias_ref[...]
+        incoming = incoming_ref[0].astype(F32)
+        token[step - 4] = (middle_ref[...] + gate_ref[...] * branch).astype(BF16)
+        back = (gate_ref[...] * incoming).astype(BF16)
+        back_ref[rows, :] = back
+        sums_ref[0:1, :] += jnp.sum(incoming * branch, axis=0, keepdims=True)
+        sums_ref[1:2, :] += jnp.sum(back.astype(F32), axis=0, keepdims=True)
+
+    for number in range(1, 4):
+
+        @pl.when(step - 4 == lax.rem(here.member + number, 4))
+        def _():
+            move(number).start()
+
+    @pl.when(step - 4 == here.member)
+    def _():
+        own.start()
+
+    @pl.when(step >= 8)
+    def _():
+        width = active_ref.shape[1] // 3
+        for part in range(3):
+            columns = slice(part * width, (part + 1) * width)
+            grads_ref[0, columns, :] = dot_tn(active_ref[:, columns], back_ref[...]).astype(BF16)
+
+    @pl.when(step == 11)
+    def _():
+        for number in range(1, 4):
+            move(number).wait()
+        own.wait()
+
+
+def turn(active, shrink, middle, incoming, gate, bias):
+    rows, features = middle.shape
+    return pl.pallas_call(
+        turn_kernel,
+        grid=(12,),
+        in_specs=[
+            pl.BlockSpec((rows, features), lambda step: (0, jnp.where(step < 8, jnp.minimum(step, 3), step - 8))),
+            pl.BlockSpec((features, features), lambda step: (jnp.minimum(step, 3), 0)),
+            pl.BlockSpec((256, features), lambda step: (clipped(step, 4, 3), 0)),
+            pl.BlockSpec((1, 256, features), lambda step: (clipped(step, 4, 3), 0, 0)),
+            everything((1, features)),
+            everything((1, features)),
+        ],
+        out_specs=[
+            ANY,
+            everything((rows, features)),
+            pl.BlockSpec((1, features, features), lambda step: (clipped(step, 8, 3), 0, 0)),
+            everything((8, features)),
+        ],
+        out_shape=[
+            jax.ShapeDtypeStruct(incoming.shape, BF16),
+            jax.ShapeDtypeStruct((rows, features), BF16),
+            jax.ShapeDtypeStruct((4, features, features), BF16),
+            jax.ShapeDtypeStruct((8, features), F32),
+        ],
+        scratch_shapes=[
+            pltpu.VMEM((rows, features), F32),
+            pltpu.VMEM(incoming.shape, BF16),
+            pltpu.SemaphoreType.DMA((3,)),
+            pltpu.SemaphoreType.DMA((3,)),
+            pltpu.SemaphoreType.DMA((1,)),
+        ],
+        compiler_params=pltpu.CompilerParams(
+            collective_id=7, has_side_effects=True, vmem_limit_bytes=56 * 1024 * 1024
+        ),
+    )(active, shrink, middle, incoming, gate, bias)
+
+
+NORM_AT = 12
+BACK_STEPS = NORM_AT + 5
+
+
+def back_kernel(
+    back_ref, second_ref, pre_ref, shrink_ref, expand_ref, middle_ref, branch_ref, incoming_ref, mixed_ref, weight_ref,
+    scaling_ref, source_ref, expand_grad_ref, expand_sum_ref, middle_grad_ref, mixed_grad_ref, output_grad_ref, sums_ref,
+    block_ref, total, slope, branch_back, *scratch
+):
+    step = pl.program_id(0)
+    here = Here()
+    reduce = Reduce(here, lambda member, core: source_ref.at[:, core, member], block_ref, *scratch)
+
+    @pl.when(step == 0)
+    def _():
+        greet((here.at_x(), here.at_y(), here.at_core(), here.at_z(1), here.at_z(2), here.at_z(3)))
+        sums_ref[...] = jnp.zeros_like(sums_ref)
+        total[...] = jnp.zeros_like(total)
+
+    steps = reduce.steps()
+    for action, turn in zip(steps[:-1], (0, 2, 5, 5, 5, 5, 5, 11)):
+        pl.when(step == turn)(action)
+
+    @pl.when(step < NORM_AT)
+    def _():
+        def one(block, carry):
+            rows = pl.ds(pl.multiple_of(block * MATMUL_ROWS, MATMUL_ROWS), MATMUL_ROWS)
+            active_grad = dot_nt(back_ref[rows, :], shrink_ref[...])
+            grad = (active_grad * gelu_parts(pre_ref[rows, :])[1]).astype(BF16)
+            slope[rows, :] = grad
+            total[rows, :] += dot_nt(grad, expand_ref[0])
+            return carry
+
+        lax.fori_loop(0, total.shape[0] // MATMUL_ROWS, one, 0)
+        expand_sum_ref[0] = jnp.sum(slope[...].astype(F32), axis=0, keepdims=True)
+        expand_grad_ref[0] = dot_tn(second_ref[...], slope[...]).astype(BF16)
+
+    @pl.when((step >= NORM_AT) & (step < NORM_AT + 4))
+    def _():
+        rows = pl.ds(pl.multiple_of((step - NORM_AT) * 256, 256), 256)
+        grad = total[rows, :]
+        normed, inverse = norm_parts(middle_ref[...])
+        sums_ref[1:2, :] += jnp.sum(grad, axis=0, keepdims=True)
+        sums_ref[2:3, :] += jnp.sum(grad * normed, axis=0, keepdims=True)
+        normed_grad = grad * (1.0 + scaling_ref[1])
+        mean_first = jnp.mean(normed_grad, axis=-1, keepdims=True)
+        mean_second = jnp.mean(normed_grad * normed, axis=-1, keepdims=True)
+        middle_grad = incoming_ref[0].astype(F32) + inverse * (normed_grad - mean_first - normed * mean_second)
+        middle_grad_ref[...] = middle_grad
+        sums_ref[0:1, :] += jnp.sum(middle_grad * branch_ref[...], axis=0, keepdims=True)
+        branch_grad = (scaling_ref[0] * middle_grad).astype(BF16)
+        branch_back[rows, :] = branch_grad
+        sums_ref[3:4, :] += jnp.sum(branch_grad.astype(F32), axis=0, keepdims=True)
+        mixed_grad_ref[...] = dot_nt(branch_grad, weight_ref[0]).astype(BF16)
+
+    @pl.when(step == BACK_STEPS - 1)
+    def _():
+        width = mixed_ref.shape[1] // 3
+        for part in range(3):
+            columns = slice(part * width, (part + 1) * width)
+            output_grad_ref[columns, :] = dot_tn(mixed_ref[:, columns], branch_back[...]).astype(BF16)
+
+    pl.when(step == BACK_STEPS - 1)(steps[-1])
+
+
+def back(back_rows, second, pre, shrink, expand, middle, branch, incoming, mixed, weights, scalings, source):
+    rows, features = middle.shape
+    third = features // 3
+    by_rows = pl.BlockSpec((256, features), lambda step: (clipped(step, NORM_AT, 3), 0))
+
+    def piece(step):
+        return jnp.minimum(step, NORM_AT - 1)
+
+    wide = jax.ShapeDtypeStruct((rows, features), F32)
+    return pl.pallas_call(
+        back_kernel,
+        grid=(BACK_STEPS,),
+        in_specs=[
+            everything((rows, features)),
+            everything((rows, features)),
+            pl.BlockSpec((rows, third), lambda step: (0, piece(step))),
+            pl.BlockSpec((third, features), lambda step: (piece(step), 0)),
+            pl.BlockSpec((1, features, third), lambda step: (piece(step) // 3, 0, piece(step) % 3)),
+            by_rows,
+            by_rows,
+            pl.BlockSpec((1, 256, features), lambda step: (clipped(step, NORM_AT, 3), 0, 0)),
+            everything((rows, features)),
+            pl.BlockSpec((1, features, features), lambda step: (3, 0, 0), pipeline_mode=pl.Buffered(1)),
+            everything((2, 1, features)),
+            ANY,
+        ],
+        out_specs=[
+            pl.BlockSpec((1, features, third), lambda step: (piece(step) // 3, 0, piece(step) % 3)),
+            pl.BlockSpec((1, 1, third), lambda step: (piece(step), 0, 0)),
+            by_rows,
+            by_rows,
+            everything((features, features)),
+            everything((8, features)),
+            everything((ROWS, features)),
+        ],
+        out_shape=[
+            jax.ShapeDtypeStruct((4, features, features), BF16),
+            jax.ShapeDtypeStruct((NORM_AT, 1, third), F32),
+            wide,
+            jax.ShapeDtypeStruct((rows, features), BF16),
+            jax.ShapeDtypeStruct((features, features), BF16),
+            jax.ShapeDtypeStruct((8, features), F32),
+            jax.ShapeDtypeStruct((ROWS, features), F32),
+        ],
+        scratch_shapes=[
+            pltpu.VMEM((rows, features), F32),
+            pltpu.VMEM((rows, third), BF16),
+            pltpu.VMEM((rows, features), BF16),
+            *Reduce.SCRATCH,
+        ],
+        compiler_params=pltpu.CompilerParams(
+            collective_id=8, has_side_effects=True, vmem_limit_bytes=60 * 1024 * 1024
+        ),
+    )(back_rows, second, pre, shrink, expand, middle, branch, incoming, mixed, weights, scalings, source)
+
+
+class Shares:
+    def __init__(self, here, block, pieces, target, wires, local):
+        self.block, self.pieces = block, pieces
+        self.copies = [
+            wires.copy(
+                step - 1,
+                pieces.at[lax.rem(here.member + step, 4)],
+                target.at[here.member],
+                here.at_member(step),
+            )
+            for step in range(1, 4)
+        ]
+        self.copies.append(pltpu.make_async_copy(pieces.at[here.member], target.at[here.member], local))
+
+    def start(self):
+        for member in range(4):
+            self.pieces[member, :36] = self.block[member * 36 : member * 36 + 36, :]
+        for copy in self.copies:
+            copy.start()
+
+    def wait(self):
+        for copy in self.copies:
+            copy.wait()
+
+
 def close_kernel(
-    grad_ref, token_ref, row_ref, bias_ref, block_ref, share_ref, tokens_ref, rows_ref, biases_ref,
-    total, pieces, row_sent, row_landed, bias_sent, bias_landed, more_sent, more_landed, more_local, *scratch
+    grad_ref, triple_ref, weight_ref, latent_ref, middle_ref, scale_ref, vector_ref, bias_ref, block_ref,
+    total, tokens_ref, rows_ref, biases_ref, share_ref,
+    pieces, triple, weight, latent, middle, token, wide, row, row_sent, row_landed, bias_sent, bias_landed,
+    more_sent, more_landed, local, *scratch
 ):
     here = Here()
+    features = latent_ref.shape[1]
     greet_all(here)
-    reduce = Reduce(here, grad_ref, total, *scratch)
+    reduce = Reduce(here, lambda member, core: grad_ref.at[member, :, core], total, *scratch)
+    loads = [
+        pltpu.make_async_copy(weight_ref.at[pl.ds(0, 3)], weight, local.at[0]),
+        pltpu.make_async_copy(triple_ref, triple, local.at[1]),
+        pltpu.make_async_copy(latent_ref, latent, local.at[2]),
+        pltpu.make_async_copy(middle_ref, middle, local.at[3]),
+    ]
+    for copy in loads:
+        copy.start()
     reduce.begin()
-    rows_done = everyone(here, lambda place: row_ref.at[0], rows_ref, row_sent, row_landed)
     bias_done = everyone(here, lambda place: bias_ref.at[place], biases_ref, bias_sent, bias_landed)
+    own_bias = pltpu.make_async_copy(bias_ref.at[here.index], biases_ref.at[here.index], local.at[4])
+    own_bias.start()
     wires = Wires(more_sent, more_landed)
+
+    shares = Shares(here, block_ref, pieces, share_ref, Wires(more_sent.at[pl.ds(3, 3)], more_landed.at[pl.ds(3, 3)]), local.at[7])
+    shares.start()
 
     def move(step):
         place = lax.rem(here.member + step, 4)
-        return wires.copy(step - 1, token_ref.at[place], tokens_ref.at[here.member], here.at_member(step))
-
-    def cut(part, source):
-        for member in range(4):
-            pieces[part, member, :36] = source[member * 36 : member * 36 + 36, :]
-
-    def share(part, step):
+        return wires.copy(step - 1, token.at[place], tokens_ref.at[here.member], here.at_member(step))
+
+    def compute(step):
         place = lax.rem(here.member + step, 4)
-        return wires.copy(
-            3 * part + 2 + step, pieces.at[part, place], share_ref.at[part, here.member], here.at_member(step)
-        )
-
-    def keep(part):
-        return pltpu.make_async_copy(
-            pieces.at[part, here.member], share_ref.at[part, here.member], more_local.at[3 + part]
-        )
-
-    own = [
-        pltpu.make_async_copy(token_ref.at[here.member], tokens_ref.at[here.member], more_local.at[0]),
-        pltpu.make_async_copy(row_ref.at[0], rows_ref.at[here.index], more_local.at[1]),
-        pltpu.make_async_copy(bias_ref.at[here.index], biases_ref.at[here.index], more_local.at[2]),
-    ]
-    for copy in own:
-        copy.start()
-    cut(1, block_ref)
-    for step in range(1, 4):
-        share(1, step).start()
-    keep(1).start()
-    move(2).start()
-    for step in reduce.steps()[1:-1]:
-        step()
-    move(1).start()
-    move(3).start()
+        rows = pl.ds(pl.multiple_of(place * 256, 256), 256)
+        hidden_grad = dot_nt(triple[rows, :features], weight[0])
+        hidden_grad += dot_nt(triple[rows, features : 2 * features], weight[1])
+        hidden_grad += dot_nt(triple[rows, 2 * features :], weight[2])
+        normed, inverse = norm_parts(latent[rows, :].astype(F32))
+        shift = jnp.sum(hidden_grad, axis=0, keepdims=True)
+        scale = jnp.sum(hidden_grad * normed, axis=0, keepdims=True)
+        normed_grad = hidden_grad * (1.0 + scale_ref[...])
+        mean_first = jnp.mean(normed_grad, axis=-1, keepdims=True)
+        mean_second = jnp.mean(normed_grad * normed, axis=-1, keepdims=True)
+        result = middle[rows, :] + inverse * (normed_grad - mean_first - normed * mean_second)
+        token[place] = result.astype(BF16)
+        return shift, scale
+
+    for copy in loads:
+        copy.wait()
+    sums = [compute(2)]
+    reduce.diagonal()
+    sums.append(compute(1))
+    reduce.direct_x()
+    reduce.direct_y()
+    reduce.keep_own()
+    reduce.relay_x()
+    reduce.relay_y()
+    sums.append(compute(3))
+    sums.append(compute(0))
+    own = pltpu.make_async_copy(token.at[here.member], tokens_ref.at[here.member], local.at[5])
+    own.start()
+    wide[...] = vector_ref[...]
+    for part in range(2):
+        vector = sums[0][part] + sums[1][part] + sums[2][part] + sums[3][part]
+        for tile in range(features // LANES):
+            place = part * (features // LANES) + tile
+            wide[place : place + 1, :] = vector[:, tile * LANES : (tile + 1) * LANES]
+    row[...] = wide[...].astype(BF16)
+    rows_done = everyone(here, lambda place: row, rows_ref, row_sent, row_landed)
+    own_row = pltpu.make_async_copy(row, rows_ref.at[here.index], local.at[6])
+    own_row.start()
+    reduce.along_z()
+    for step in (2, 1, 3):
+        move(step).start()
     reduce.finish()
-    cut(0, total)
-    for step in range(1, 4):
-        share(0, step).start()
-    keep(0).start()
+    shares.wait()
     for step in range(1, 4):
         move(step).wait()
-        share(0, step).wait()
-        share(1, step).wait()
-    for copy in own:
-        copy.wait()
-    keep(0).wait()
-    keep(1).wait()
+    own.wait()
+    own_bias.wait()
+    own_row.wait()
     rows_done()
     bias_done()
 
 
-def close_down(grad, tokens, row, bias, block):
+def close_down(grad, triple, weight, latents, middle_grad, scale, vectors, bias, block):
+    rows, features = latents.shape
+    whole = pl.BlockSpec(memory_space=pltpu.VMEM)
     return pl.pallas_call(
         close_kernel,
-        in_specs=[ANY] * 4 + [pl.BlockSpec(memory_space=pltpu.VMEM)],
-        out_specs=[ANY] * 4,
+        in_specs=[ANY] * 5 + [whole, whole, ANY, whole],
+        out_specs=[whole, ANY, ANY, ANY, ANY],
         out_shape=[
-            jax.ShapeDtypeStruct((2, 4, 40, 1152), F32),
-            jax.ShapeDtypeStruct(tokens.shape, tokens.dtype),
-            jax.ShapeDtypeStruct((32,) + row.shape[1:], row.dtype),
+            jax.ShapeDtypeStruct((ROWS, 1152), F32),
+            jax.ShapeDtypeStruct((4, rows // 4, features), BF16),
+            jax.ShapeDtypeStruct((32,) + vectors.shape, BF16),
             jax.ShapeDtypeStruct(bias.shape, bias.dtype),
-        ],
-        scratch_shapes=[pltpu.VMEM((ROWS, 1152), F32), pltpu.VMEM((2, 4, 40, 1152), F32)]
+            jax.ShapeDtypeStruct((4, 40, 1152), F32),
+        ],
+        scratch_shapes=[
+            pltpu.VMEM((4, 40, 1152), F32),
+            pltpu.VMEM(triple.shape, BF16),
+            pltpu.VMEM((3, features, features), BF16),
+            pltpu.VMEM(latents.shape, BF16),
+            pltpu.VMEM(latents.shape, F32),
+            pltpu.VMEM((4, rows // 4, features), BF16),
+            pltpu.VMEM(vectors.shape, F32),
+            pltpu.VMEM(vectors.shape, BF16),
+        ]
         + [pltpu.SemaphoreType.DMA((32,))] * 4
-        + [pltpu.SemaphoreType.DMA((9,))] * 2
-        + [pltpu.SemaphoreType.DMA((5,))]
+        + [pltpu.SemaphoreType.DMA((6,))] * 2
+        + [pltpu.SemaphoreType.DMA((8,))]
         + list(Reduce.SCRATCH),
         compiler_params=pltpu.CompilerParams(
-            collective_id=3, has_side_effects=True, vmem_limit_bytes=48 * 1024 * 1024
+            collective_id=3, has_side_effects=True, vmem_limit_bytes=60 * 1024 * 1024
         ),
-    )(grad, tokens, row, bias, block)
-
-
-def swap_kernel(part_ref, parts_ref, sent, landed, local):
+    )(grad, triple, weight, latents, middle_grad, scale, vectors, bias, block)
+
+
+def swap_kernel(part_ref, block_ref, parts_ref, share_ref, pieces, sent, landed, more_sent, more_landed, local):
     here = Here()
     greet_all(here)
+    shares = Shares(here, block_ref, pieces, share_ref, Wires(more_sent, more_landed), local.at[1])
     done = everyone(here, lambda place: part_ref.at[place // 4], parts_ref, sent, landed)
     own = pltpu.make_async_copy(part_ref.at[here.group], parts_ref.at[here.index], local.at[0])
     own.start()
+    shares.start()
+    shares.wait()
     own.wait()
     done()
 
 
-def swap(parts):
+def swap(parts, block):
     return pl.pallas_call(
         swap_kernel,
-        in_specs=[ANY],
-        out_specs=ANY,
-        out_shape=jax.ShapeDtypeStruct((32,) + parts.shape[1:], parts.dtype),
+        in_specs=[ANY, pl.BlockSpec(memory_space=pltpu.VMEM)],
+        out_specs=[ANY, ANY],
+        out_shape=[
+            jax.ShapeDtypeStruct((32,) + parts.shape[1:], parts.dtype),
+            jax.ShapeDtypeStruct((4, 40, 1152), F32),
+        ],
         scratch_shapes=[
+            pltpu.VMEM((4, 40, 1152), F32),
             pltpu.SemaphoreType.DMA((32,)),
             pltpu.SemaphoreType.DMA((32,)),
-            pltpu.SemaphoreType.DMA((1,)),
+            pltpu.SemaphoreType.DMA((3,)),
+            pltpu.SemaphoreType.DMA((3,)),
+            pltpu.SemaphoreType.DMA((2,)),
         ],
         compiler_params=pltpu.CompilerParams(collective_id=4, has_side_effects=True),
-    )(parts)
+    )(parts, block)
 
 
 def pad_lanes(values, width):
@@ -1163,7 +1735,7 @@
     biases = (modulate_bias, triple_bias, output_bias, expand_bias, shrink_bias)
     note = jnp.concatenate([own_cond, *biases]).astype(F32)
     note = jnp.pad(note, (0, 1664 - note.shape[0])).reshape(1, 1, 1664)
-    notes, blocks = introduce(note, shard)
+    notes, blocks, shrink_quad = introduce(note, shard, shrink_weight)
     notes = notes.reshape(32, 1664)
     cond_act = jax.nn.silu(notes[:, :features]).astype(BF16)
     cuts = []
@@ -1176,63 +1748,67 @@
     act_owned = lax.dynamic_slice_in_dim(cond_act, me * owned, owned, axis=1)
     parts = pad_lanes(dot_nn(act_owned, modulate_weight), 56 * LANES).reshape(4, 2, 4, 56, LANES)
     parts = jnp.swapaxes(parts, 0, 1).reshape(2, 16, 56, LANES)
-    first_full, expand_column, shrink_column, parts, token_rows = open_up(
-        blocks, shrink_weight, parts, latents.reshape(4, tokens, features)
+    first_full, expand_column, parts, token_rows = open_up(
+        blocks, parts, latents.reshape(4, tokens, features)
     )
     first_full = first_full.reshape(4, features, features)
     modulation = jnp.sum(parts, axis=0).reshape(-1)[: 6 * features] + modulate_offset
     shift_one, scale_one, gate_one, shift_two, scale_two, gate_two = jnp.split(modulation[None, :], 6, axis=-1)
 
-    latent_float = token_rows.reshape(4 * tokens, features).astype(F32)
+    token_rows = token_rows.reshape(4 * tokens, features)
+    latent_float = token_rows.astype(F32)
     normed_one, inverse_one = norm_parts(latent_float)
     hidden_one = (normed_one * (1.0 + scale_one) + shift_one).astype(BF16)
     zero = jnp.zeros((features,), F32)
-    full_bias = jnp.concatenate([triple_offset[:features], zero, triple_offset[features:]])
-    triple_full = first_full[:3]
+    first_bias = jnp.stack(
+        [triple_offset[:features], zero, triple_offset[features:], output_offset]
+    ).reshape(4, 1, features)
     output_full = first_full[3]
-    projected = (
-        jnp.concatenate([dot_nn(hidden_one, first_full[part]) for part in range(3)], axis=1) + full_bias
-    ).astype(BF16)
-    mixed, log_total, expand_full, shrink_full = attend_forward_gather(projected, expand_column, shrink_column)
-    mixed, cotangent = lax.optimization_barrier((mixed, cotangent))
+    (
+        projected,
+        mixed,
+        log_total,
+        branch_one,
+        middle,
+        hidden_two,
+        pre_act,
+        activated,
+        expand_full,
+        shrink_full,
+        incoming,
+    ) = forward(
+        hidden_one,
+        first_full,
+        first_bias,
+        token_rows,
+        jnp.stack([gate_one, shift_two, scale_two]),
+        expand_offset.reshape(4, 1, features),
+        expand_column,
+        shrink_quad,
+        cotangent.reshape(4, tokens, features),
+    )
     expand_full = expand_full.reshape(4, features, features)
     shrink_full = shrink_full.reshape(hidden, features)
-    branch_one = dot_nn(mixed, output_full) + output_offset
-    middle = latent_float + gate_one * branch_one
-    normed_two, inverse_two = norm_parts(middle)
-    hidden_two = (normed_two * (1.0 + scale_two) + shift_two).astype(BF16)
-    pre_act = jnp.concatenate([dot_nn(hidden_two, expand_full[part]) for part in range(4)], axis=1) + expand_offset
-    activated = gelu_parts(pre_act)[0].astype(BF16)
-    branch_two = dot_nn(activated, shrink_full) + shrink_offset
-
-    def exchange(values):
-        return lax.all_to_all(values.reshape(4, tokens, features), "seq", split_axis=0, concat_axis=0, tiled=True)
-
-    output = exchange((middle + gate_two * branch_two).astype(BF16))
-    incoming = exchange(cotangent).reshape(4 * tokens, features).astype(F32)
-    branch_two_grad = (gate_two * incoming).astype(BF16)
-    gate_two_grad = jnp.sum(incoming * branch_two, axis=0)
-    shrink_offset_grad = jnp.sum(branch_two_grad.astype(F32), axis=0)
-    shrink_grad = dot_tn(activated, branch_two_grad).astype(BF16)
-    shrink_total = lax.psum_scatter(shrink_grad, AXES, scatter_dimension=0, tiled=True).astype(F32)
-    act_grad = dot_nt(branch_two_grad, shrink_full)
-    pre_grad = (act_grad * gelu_parts(pre_act)[1]).astype(BF16)
-    expand_offset_grad = jnp.sum(pre_grad.astype(F32), axis=0)
-    expand_grad = jnp.stack(
-        [dot_tn(hidden_two, pre_grad[:, part * features : (part + 1) * features]).astype(BF16) for part in range(4)]
-    ).reshape(4, 4, 2, ROWS, features)
-    hidden_two_grad = sum(
-        dot_nt(pre_grad[:, part * features : (part + 1) * features], expand_full[part]) for part in range(4)
-    )
-    norm_grad_two, shift_two_grad, scale_two_grad = norm_back(
-        hidden_two_grad[None], normed_two[None], inverse_two[None], scale_two[None]
-    )
-    middle_grad = incoming + norm_grad_two[0]
-    branch_one_grad = (gate_one * middle_grad).astype(BF16)
-    gate_one_grad = jnp.sum(middle_grad * branch_one, axis=0)
-    output_offset_grad = jnp.sum(branch_one_grad.astype(F32), axis=0)
-    output_grad = dot_tn(mixed, branch_one_grad).astype(BF16)
-    mixed_grad = dot_nt(branch_one_grad, output_full).astype(BF16)
+    output, back_rows, shrink_grad, turn_sums = turn(
+        activated, shrink_full, middle, incoming, gate_two, shrink_offset[None]
+    )
+    expand_grad, expand_offset_grad, middle_grad, mixed_grad, output_grad, back_sums, shrink_total = back(
+        back_rows,
+        hidden_two,
+        pre_act,
+        shrink_full,
+        expand_full,
+        middle,
+        branch_one,
+        incoming,
+        mixed,
+        first_full,
+        jnp.stack([gate_one, scale_two]),
+        shrink_grad.reshape(4, 2, 4, ROWS, features),
+    )
+    expand_grad = expand_grad.reshape(4, 4, 2, ROWS, features)
+    gate_two_grad, shrink_offset_grad = turn_sums[0], turn_sums[1]
+    gate_one_grad, output_offset_grad = back_sums[0], back_sums[3]
     triple_rows, expand_block = attend_backward_reduce(projected, mixed_grad, log_total, expand_grad)
     column_sums = jnp.sum(triple_rows.astype(F32), axis=0)
     triple_offset_grad = jnp.concatenate([column_sums[:features], column_sums[2 * features :]])
@@ -1240,24 +1816,16 @@
         [dot_tn(hidden_one, triple_rows[:, part * features : (part + 1) * features]).astype(BF16) for part in range(3)]
         + [output_grad]
     ).reshape(4, 4, 2, ROWS, features)
-    hidden_one_grad = sum(
-        dot_nt(triple_rows[:, part * features : (part + 1) * features], first_full[part]) for part in range(3)
-    )
-    norm_grad_one, shift_one_grad, scale_one_grad = norm_back(
-        hidden_one_grad[None], normed_one[None], inverse_one[None], scale_one[None]
-    )
-    token_grad = (middle_grad + norm_grad_one[0]).astype(BF16).reshape(4, tokens, features)
-    modulation_grad = jnp.concatenate(
+    vectors = jnp.concatenate(
         [
-            shift_one_grad[0],
-            scale_one_grad[0],
+            jnp.zeros((2 * features,), F32),
             gate_one_grad,
-            shift_two_grad[0],
-            scale_two_grad[0],
+            back_sums[1],
+            back_sums[2],
             gate_two_grad,
+            jnp.zeros((64 * LANES - 6 * features,), F32),
         ]
-    ).astype(BF16)
-    row = jnp.pad(modulation_grad, (0, 8192 - 6 * features)).reshape(1, 64, LANES)
+    ).reshape(64, LANES)
     bias_grads = jnp.concatenate(
         [
             values.reshape(devices, -1)
@@ -1266,8 +1834,8 @@
         axis=1,
     )
     bias_grads = pad_lanes(bias_grads, 1024).reshape(32, 8, LANES)
-    shares, token_grad, all_grads, bias_parts = close_down(
-        first_grad, token_grad, row, bias_grads, expand_block
+    first_block, token_grad, all_grads, bias_parts, expand_share = close_down(
+        first_grad, triple_rows, first_full, token_rows, middle_grad, scale_one, vectors, bias_grads, expand_block
     )
     all_grads = all_grads.reshape(32, 8192)[:, : 6 * features]
     modulate_total = dot_tn(act_owned, all_grads)
@@ -1277,7 +1845,8 @@
     )
     cond_back = dot_nt(all_grads, modulate_weight)
     cond_back = jnp.pad(cond_back.reshape(8, 4, owned), ((0, 0), (0, 4), (0, LANES - owned)))
-    cond_back = swap(cond_back)[:, :4, :owned]
+    cond_back, first_share = swap(cond_back, first_block)
+    cond_back = cond_back[:, :4, :owned]
     cond_back = jnp.swapaxes(cond_back, 0, 1).reshape(condition.shape)
     cond_float = condition.astype(F32)
     sigmoid_cond = jax.nn.sigmoid(cond_float)
@@ -1288,8 +1857,8 @@
     for bias in biases[1:]:
         bias_cuts.append(bias_total[offset : offset + bias.shape[0]])
         offset += bias.shape[0]
-    first_share = shares[0, :, :owned]
-    expand_total = jnp.swapaxes(shares[1, :, :owned], 0, 1).reshape(expand_weight.shape)
+    first_share = first_share[:, :owned]
+    expand_total = jnp.swapaxes(expand_share[:, :owned], 0, 1).reshape(expand_weight.shape)
     return (
         output.reshape(latents.shape),
         token_grad.reshape(latents.shape).astype(F32),

time: 808 us -> 671 us (0.83)
  matrix products: 206 us -> 15.2 us
  Pallas kernels: 454 us -> 599 us
  other arithmetic: 78 us -> 27.1 us
  local copies, waits for them, and re-layouts: 37.7 us -> 23.6 us
  between operations: 15.4 us -> 1.34 us
  starting transfers between devices: 9.05 us -> 0 us
    pallas_call x5 -> x7, Pallas kernels: 354 us -> 509 us  [the longest x1 128 us: forward(): pl.pallas_call(forward_kernel, grid=(FORWARD_STEPS,), in_specs=[everythin...]
    dot_general x10 -> x1, matrix products: 77.1 us -> 0.27 us  [dot_nt(): lax.dot_general(left, right, (((1,), (1,)), ((), ())), preferred_element_...]
    dot_general x10 -> x1, matrix products: 67.9 us -> 0.34 us  [dot_nn(): return jnp.dot(left, right, preferred_element_type=F32)]
    dot_general x10 -> x4, matrix products: 61.1 us -> 14.6 us  [dot_tn(): lax.dot_general(left, right, (((0,), (0,)), ((), ())), preferred_element_...]
    convert_element_type x5 -> x0, other arithmetic: 31.9 us -> none  [the longest x1 14.6 us: on_device_fast(): activated = gelu_parts(pre_act)[0].astype(BF16)]
    pallas_call x1, Pallas kernels: 100 us -> 89.1 us  [attend_backward_reduce(): pl.pallas_call(backward_reduce_kernel, grid=(HEADS,), in_specs=[whole_blo...]
    reduce_sum x2 -> x0, other arithmetic: 9.62 us -> none  [the longest x1 5.35 us: on_device_fast(): output_offset_grad = jnp.sum(branch_one_grad.astype(F32), axis=0)]
    all_to_all x2 -> x0, starting transfers between devices: 9.01 us -> none  [exchange(): lax.all_to_all(values.reshape(4, tokens, features), 'seq', split_axis=0,...]
  transfers between devices with their start and end apart: 3 -> 0, of which waited for: 0 -> 0; matrix products, arithmetic and copies ran while one was open for 20% -> 0% of each run, Pallas kernels for 29% -> 0%
where the time goes in v3:
time: 671 us; the launch traced here: 666 us
  Pallas kernels  599 us (89%)
  other arithmetic  27.1 us (4%)
  local copies, waits for them, and re-layouts  23.6 us (4%)
  matrix products  15.2 us (2%)
    pallas_call x1, Pallas kernels, forward(): pl.pallas_call(forward_kernel, grid=(FORWARD_STEPS,), in_specs=[everythin...  128 us
    pallas_call x1, Pallas kernels, close_down(): pl.pallas_call(close_kernel, in_specs=[ANY] * 5 + [whole, whole, ANY, who...  101 us
    pallas_call x1, Pallas kernels, back(): pl.pallas_call(back_kernel, grid=(BACK_STEPS,), in_specs=[everything((row...  92 us
    pallas_call x1, Pallas kernels, attend_backward_reduce(): pl.pallas_call(backward_reduce_kernel, grid=(HEADS,), in_specs=[whole_blo...  89.1 us
    pallas_call x1, Pallas kernels, open_up(): pl.pallas_call(open_kernel, in_specs=[ANY] * 3, out_specs=[ANY] * 4, out_...  81.5 us
    pallas_call x1, Pallas kernels, turn(): pl.pallas_call(turn_kernel, grid=(12,), in_specs=[pl.BlockSpec((rows, fea...  50.7 us
    pallas_call x1, Pallas kernels, introduce(): pl.pallas_call(introduce_kernel, in_specs=[ANY, ANY, ANY], out_specs=[ANY...  36.7 us
    pallas_call x1, Pallas kernels, swap(): pl.pallas_call(swap_kernel, in_specs=[ANY, pl.BlockSpec(memory_space=pltp...  18.9 us

profile of v3, /device:TPU:0, one launch (start us, length us, event | category | flops | bytes accessed | tf_op | source)
XLA Modules:
  0.0 665.9 jit_solution(14674203333195905772)
XLA Ops:
  1.5 3.4 concatenate.24
  6.6 2.0 fusion.7.shard_ref
  8.5 36.7 %shard_map.228 = (f32[32,1,1664]{2,1,0:T(1,128)}, bf16[2,144,1152]{2,1,0:T(8,128)(2,1)}, bf16[4,144,1152]{2,1,0:T(8,128)(2,1)}) custom-call(f32[1,1,1664]{2,1,0:T(1,128)} %reshape.209.note_ref, bf16[2,48,4608]{2,1,0:T(8,128)(2,1)} %fusion.7.shard_ref, bf16[144,1152]{1,0:T(8,128)(2,1)} %shrink_ref.1), custom_call_target="tpu_custom_call" | custom-call | tf_op jit(solution)/shard_map/pallas_call | solution.py:589
  48.5 81.5 %shard_map.229 = (bf16[4,4,2,144,1152]{4,3,2,1,0:T(8,128)(2,1)}, bf16[4,144,1152]{2,1,0:T(8,128)(2,1)}, f32[16,56,128]{2,1,0:T(8,128)}, bf16[4,256,1152]{2,1,0:T(8,128)(2,1)}) custom-call(bf16[2,144,1152]{2,1,0:T(8,128)(2,1)} %get-tuple-element.51.block_ref, f32[2,16,56,128]{3,2,1,0:T(8,128)} %bitcast.93, bf16[4,256,1152]{2,1,0:T(8,128)(2,1)} %bitcast.101), custom_call_target="tpu_custom_call" | custom-call | tf_op jit(solution)/shard_map/pallas_call | solution.py:770
  130.0 1.2 reduce_sum.58
  132.7 2.0 convert_reduce_fusion.1
  135.5 2.4 add_convert_fusion.hidden_ref
  140.0 128.2 %shard_map.230 = (bf16[1024,3456]{1,0:T(8,128)(2,1)}, bf16[1024,1152]{1,0:T(8,128)(2,1)}, f32[16,1,1024]{2,1,0:T(1,128)}, f32[1024,1152]{1,0:T(8,128)}, f32[1024...) custom-call(bf16[1024,1152]{1,0:T(8,128)(2,1)} %add_convert_fusion.h, ...), custom_call_target="tpu_custom_call" | custom-call | tf_op jit(solution)/shard_map/pallas_call | solution.py:1054
  268.9 50.7 %shard_map.231 = (bf16[4,256,1152]{2,1,0:T(8,128)(2,1)}, bf16[1024,1152]{1,0:T(8,128)(2,1)}, bf16[4,1152,1152]{2,1,0:T(8,128)(2,1)}, f32[8,1152]{1,0:T(8,128)}) custom-call(bf16[1024,4608]{1,0:T(8,128)(2,1)} %get-tuple-element.58.active_ref, bf16[4608,1152]{1,0:T(8,128)(2,1)} %bitcast.82, f32[1024,1152]{1,0:T(8,128)} %get-tuple-element.60.middle_ref, ...), custom_call_target="tpu_custom_call" | custom-call | tf_op jit(solution)/shard_map/pallas_call | solution.py:1374
  320.2 92.0 %shard_map.232 = (bf16[4,1152,1152]{2,1,0:T(8,128)(2,1)}, f32[12,1,384]{2,1,0:T(1,128)}, f32[1024,1152]{1,0:T(8,128)}, bf16[1024,1152]{1,0:T(8,128)(2,1)}, bf16[...) custom-call(bf16[1024,1152]{1,0:T(8,128)(2,1)} %get-tuple-element.64.back_ref, ...), custom_call_target="tpu_custom_call" | custom-call | tf_op jit(solution)/shard_map/pallas_call | solution.py:1484
  412.2 89.1 %shard_map.233 = (bf16[1024,3456]{1,0:T(8,128)(2,1)}, f32[144,1152]{1,0:T(8,128)}) custom-call(bf16[1024,3456]{1,0:T(8,128)(2,1)} %get-tuple-element.63.query_ref.key_ref.value_ref, bf16[1024,3456]{1,0:T(8,128)(2,1)} %get-tuple-element.63.query_ref.key_ref.value_ref, bf16[1024,3456]{1,0:T(8,128)(2,1)} %get-tuple-element.63.query_ref.key_ref.value_ref, ...), custom_call_target="tpu_custom_call" | custom-call | tf_op jit(solution)/shard_map/pallas_call | solution.py:1272
  501.4 4.0 convert_reduce_fusion
  507.8 5.8 convolution_convert_fusion.2
  513.7 3.3 convolution_convert_fusion.1
  517.0 3.3 convolution_convert_fusion
  520.3 5.2 pad_maximum_fusion.grad_ref
  525.5 101.4 %shard_map.234 = (f32[144,1152]{1,0:T(8,128)}, bf16[4,256,1152]{2,1,0:T(8,128)(2,1)}, bf16[32,64,128]{2,1,0:T(8,128)(2,1)}, f32[32,8,128]{2,1,0:T(8,128)}, f32[4,40,1152]{2,1,0:T(8,128)}) custom-call(bf16[4,4,2,144,1152]{4,3,2,1,0:T(8,128)(2,1)} %pad_maximum_fusion.grad_ref, bf16[1024,3456]{1,0:T(8,128)(2,1)} %get-tuple-element.74.triple_ref, ...), custom_call_target="tpu_custom_call" | custom-call | tf_op jit(solution)/shard_map/pallas_call | solution.py:1644
  627.0 1.4 copy.41
  629.3 18.9 %shard_map.235 = (f32[32,8,128]{2,1,0:T(8,128)}, f32[4,40,1152]{2,1,0:T(8,128)}) custom-call(f32[8,8,128]{2,1,0:T(8,128)} %pad.25.part_ref, f32[144,1152]{1,0:T(8,128)} %get-tuple-element.83.block_ref), custom_call_target="tpu_custom_call" | custom-call | tf_op jit(solution)/shard_map/pallas_call | solution.py:1689
  648.2 1.9 slice_bitcast_fusion.1
  652.6 2.2 fusion.17
  654.8 2.5 convert.4
  659.4 1.4 convert_reduce_fusion.2
  663.4 1.4 copy.51
  (100 shorter events, 22.4 us)
Async XLA Ops:
  0.6 46.3 %copy-start = (bf16[36,6912]{1,0:T(8,128)(2,1)S(1)}, bf16[36,6912]{1,0:T(8,128)(2,1)}, u32[]{:S(2)}) copy-start(bf16[36,6912]{1,0:T(8,128)(2,1)} %param.16) | copy-start | bytes 1492996
  46.3 0.7 copy-start.8
  130.0 4.7 copy-start.1
  501.4 4.2 copy-start.11
  501.4 4.4 copy-start.12
  507.0 6.6 slice-start
  507.8 5.8 copy-start.10
  507.8 5.9 slice-start.1
  507.8 5.9 copy-start.2
  517.0 3.3 copy-start.3
  627.0 25.0 %copy-start.9 = (bf16[2,2,1152]{2,1,0:T(2,128)(2,1)S(1)}, bf16[2,2,1152]{2,1,0:T(2,128)(2,1)}, u32[]{:S(2)}) copy-start(bf16[2,2,1152]{2,1,0:T(2,128)(2,1)} %param.14) | copy-start | bytes 27652
  628.6 26.2 %copy-start.4 = (bf16[4,256,1152]{2,1,0:T(8,128)(2,1)S(1)}, bf16[4,256,1152]{2,1,0:T(8,128)(2,1)}, u32[]{:S(2)}) copy-start(bf16[4,256,1152]{2,1,0:T(8,128)(2,1)} %get-tuple-element.81) | copy-start | bytes 7077892
  654.8 2.5 copy-start.6
  657.3 6.1 copy-start.5
  661.7 3.1 copy-start.7

commit v4 on v3

--- a/solution.py
+++ b/solution.py
@@ -423,6 +423,7 @@
 ANY = pl.BlockSpec(memory_space=pl.ANY)
 ROWS = 144
 MATMUL_ROWS = 1024
+LOW, HIGH = pl.ds(0, 80), pl.ds(80, 64)
 
 
 class Here:
@@ -540,7 +541,7 @@
 
 
 def introduce_kernel(
-    note_ref, shard_ref, shrink_ref, notes_ref, blocks_ref, quad_ref, landing, wide, buffer,
+    note_ref, shard_ref, shrink_ref, notes_ref, blocks_ref, quad_ref, column_ref, landing, wide, buffer,
     note_sent, note_landed, sent, landed, local,
 ):
     here = Here()
@@ -554,22 +555,31 @@
     for step in range(1, 4):
         place = lax.rem(here.member + step, 4)
         quads.append(wires.copy(step - 1, columns(place), landing.at[here.member], here.at_member(step)))
-    shrinks = [
-        wires.copy(2 + step, shrink_ref, quad_ref.at[here.member], here.at_member(step)) for step in range(1, 4)
+    highs = [
+        wires.copy(2 + step, shrink_ref.at[HIGH], quad_ref.at[here.member], here.at_member(step))
+        for step in range(1, 4)
     ]
-    for copy in quads:
+    lows = [
+        wires.copy(5 + step, shrink_ref.at[LOW], column_ref.at[here.z], here.at_z(step)) for step in range(1, 4)
+    ]
+    for copy in quads + lows:
         copy.start()
-    keep = Bounce(shrink_ref, buffer, quad_ref.at[here.member], local.at[2])
-    keep.start()
+    keeps = [
+        Bounce(shrink_ref.at[LOW], buffer.at[LOW], column_ref.at[here.z], local.at[2]),
+        Bounce(shrink_ref.at[HIGH], buffer.at[HIGH], quad_ref.at[here.member], local.at[3]),
+    ]
+    for keep in keeps:
+        keep.start()
     done = everyone(here, lambda place: note_ref.at[0], notes_ref, note_sent, note_landed)
     own = pltpu.make_async_copy(columns(here.member), landing.at[here.member], local.at[0])
     own.start()
     mine = pltpu.make_async_copy(note_ref.at[0], notes_ref.at[here.index], local.at[1])
     mine.start()
-    for copy in shrinks:
+    for copy in highs:
         copy.start()
     own.wait()
-    keep.go_on()
+    for keep in keeps:
+        keep.go_on()
     for copy in quads:
         copy.wait_recv()
     for part in range(2):
@@ -578,9 +588,8 @@
         blocks_ref[part] = wide[...].astype(BF16)
     for copy in quads:
         copy.wait_send()
-    for copy in shrinks:
+    for copy in highs + lows + keeps:
         copy.wait()
-    keep.wait()
     mine.wait()
     done()
 
@@ -589,11 +598,12 @@
     return pl.pallas_call(
         introduce_kernel,
         in_specs=[ANY, ANY, ANY],
-        out_specs=[ANY, pl.BlockSpec(memory_space=pltpu.VMEM), ANY],
+        out_specs=[ANY, pl.BlockSpec(memory_space=pltpu.VMEM), ANY, ANY],
         out_shape=[
             jax.ShapeDtypeStruct((32,) + note.shape[1:], note.dtype),
             jax.ShapeDtypeStruct((2, ROWS, 1152), BF16),
-            jax.ShapeDtypeStruct((4, ROWS, 1152), BF16),
+            jax.ShapeDtypeStruct((4, HIGH.size, 1152), BF16),
+            jax.ShapeDtypeStruct((4, LOW.size, 1152), BF16),
         ],
         scratch_shapes=[
             pltpu.VMEM((4,) + shard.shape[:2] + (1152,), BF16),
@@ -601,9 +611,9 @@
             pltpu.VMEM((ROWS, 1152), BF16),
             pltpu.SemaphoreType.DMA((32,)),
             pltpu.SemaphoreType.DMA((32,)),
-            pltpu.SemaphoreType.DMA((6,)),
-            pltpu.SemaphoreType.DMA((6,)),
-            pltpu.SemaphoreType.DMA((3,)),
+            pltpu.SemaphoreType.DMA((9,)),
+            pltpu.SemaphoreType.DMA((9,)),
+            pltpu.SemaphoreType.DMA((4,)),
         ],
         compiler_params=pltpu.CompilerParams(collective_id=1, has_side_effects=True),
     )(note, shard, shrink)
@@ -696,9 +706,73 @@
                 self.passed(kind, order).wait_send()
 
 
+class Column:
+    COPIES = 13
+
+    def __init__(self, here, full, quad, sent, landed):
+        self.here, self.full, self.quad = here, full, quad
+        self.wires = Wires(sent, landed)
+
+    def pass_on(self, way, turn):
+        here = self.here
+        target = self.full.at[here.z - way * turn, here.core, :, HIGH]
+        partner = ((here.z + way) * 2 + here.core, here.member)
+        return self.wires.copy(turn + (3 if way < 0 else 0), self.quad if turn == 0 else target, target, partner)
+
+    def came(self, way, turn):
+        here = self.here
+        return self.full.at[here.z - way * (turn + 1), here.core, :, HIGH]
+
+    def arrival(self, way, turn):
+        ref = self.came(way, turn)
+        return self.wires.copy(turn + (3 if way < 0 else 0), ref, ref, self.here.at_core())
+
+    def across(self, way, turn):
+        ref = self.came(way, turn)
+        return self.wires.copy(6 + turn + (3 if way < 0 else 0), ref, ref, self.here.at_core())
+
+    def own_across(self):
+        here = self.here
+        return self.wires.copy(12, self.quad, self.full.at[here.z, here.core, :, HIGH], here.at_core())
+
+    def sends(self, way, turn):
+        z = self.here.z
+        return (z < 3) & (z >= turn) if way > 0 else (z > 0) & (z <= 3 - turn)
+
+    def comes(self, way, turn):
+        z = self.here.z
+        return z >= turn + 1 if way > 0 else z <= 2 - turn
+
+    def each(self, test, turn, action):
+        for way in (1, -1):
+            pl.when(test(way, turn))(lambda way=way: action(way, turn))
+
+    def begin(self):
+        self.each(self.sends, 0, lambda way, turn: self.pass_on(way, turn).start())
+        self.own_across().start()
+
+    def end_first(self):
+        self.each(self.comes, 0, lambda way, turn: self.arrival(way, turn).wait_recv())
+        self.each(self.sends, 0, lambda way, turn: self.pass_on(way, turn).wait_send())
+        self.own_across().wait()
+
+    def step(self, turn):
+        if turn > 1:
+            self.each(self.comes, turn - 1, lambda way, turn: self.arrival(way, turn).wait_recv())
+        if turn < 3:
+            self.each(self.sends, turn, lambda way, turn: self.pass_on(way, turn).start())
+        self.each(self.comes, turn - 1, lambda way, turn: self.across(way, turn).start())
+
+    def end(self):
+        for turn in range(3):
+            self.each(self.comes, turn, lambda way, turn: self.across(way, turn).wait())
+        for turn in range(1, 3):
+            self.each(self.sends, turn, lambda way, turn: self.pass_on(way, turn).wait_send())
+
+
 def open_kernel(
-    block_ref, part_ref, token_ref, full_ref, expand_ref, parts_ref, tokens_ref,
-    part_mine, part_half, block_buffer, token_buffer, part_sent, part_landed, sent, landed, more_sent, more_landed, local,
+    block_ref, quad_ref, part_ref, token_ref, full_ref, expand_ref, shrink_ref, parts_ref, tokens_ref,
+    part_mine, part_half, block_buffer, token_buffer, quad_buffer, part_sent, part_landed, sent, landed, more_sent, more_landed, local,
 ):
     here = Here()
     greet_all(here)
@@ -715,12 +789,14 @@
         landed.at[0],
     )
     second = Gather(here, None, lambda z: expand_ref.at[z], sent.at[1], landed.at[1])
+    third = Column(here, shrink_ref, quad_ref, more_sent.at[pl.ds(4, 13)], more_landed.at[pl.ds(4, 13)])
     first.begin(block_ref.at[0])
     mine = here.z * 4 + here.member
     own = [
         Bounce(block_ref.at[0], block_buffer.at[0], first.own(here.z), local.at[1]),
         Bounce(block_ref.at[1], block_buffer.at[1], second.own(here.z), local.at[2]),
         Bounce(token_ref.at[here.member], token_buffer, tokens_ref.at[here.member], local.at[3]),
+        Bounce(quad_ref, quad_buffer, shrink_ref.at[here.z, here.core, :, HIGH], local.at[5]),
     ]
     for copy in own:
         copy.start()
@@ -749,11 +825,13 @@
         first.along(ARRIVALS[order], block_ref.at[0]).wait_recv()
         first.spread(order)
     second.begin(block_ref.at[1])
+    third.begin()
     for order in range(4):
         first.relay(order)
     for order in range(4):
         first.close(order)
     first.end()
+    third.end_first()
     for step in (1, 3, 2):
         first.along(step, block_ref.at[0]).wait_send()
         second.along(step, block_ref.at[1]).wait()
@@ -765,15 +843,16 @@
     done()
 
 
-def open_up(blocks, parts, tokens):
+def open_up(blocks, quad, parts, tokens):
     column = jax.ShapeDtypeStruct((4, ROWS, 1152), BF16)
     return pl.pallas_call(
         open_kernel,
-        in_specs=[ANY] * 3,
-        out_specs=[ANY] * 4,
+        in_specs=[ANY] * 4,
+        out_specs=[ANY] * 5,
         out_shape=[
             jax.ShapeDtypeStruct((4, 4, 2, ROWS, 1152), BF16),
             column,
+            jax.ShapeDtypeStruct((4, 2, 4, ROWS, 1152), BF16),
             jax.ShapeDtypeStruct(parts.shape[1:], parts.dtype),
             jax.ShapeDtypeStruct(tokens.shape, tokens.dtype),
         ],
@@ -782,84 +861,17 @@
             pltpu.VMEM(parts.shape[1:], F32),
             pltpu.VMEM((2, ROWS, 1152), BF16),
             pltpu.VMEM(tokens.shape[1:], BF16),
+            pltpu.VMEM(quad.shape, BF16),
             pltpu.SemaphoreType.DMA((16,)),
             pltpu.SemaphoreType.DMA((16,)),
             pltpu.SemaphoreType.DMA((2, 31)),
             pltpu.SemaphoreType.DMA((2, 31)),
-            pltpu.SemaphoreType.DMA((7,)),
-            pltpu.SemaphoreType.DMA((7,)),
+            pltpu.SemaphoreType.DMA((17,)),
+            pltpu.SemaphoreType.DMA((17,)),
             pltpu.SemaphoreType.DMA((6,)),
         ],
         compiler_params=pltpu.CompilerParams(collective_id=2, has_side_effects=True),
-    )(blocks, parts, tokens)
-
-
-class Column:
-    COPIES = 13
-
-    def __init__(self, here, full, quad, sent, landed):
-        self.here, self.full, self.quad = here, full, quad
-        self.wires = Wires(sent, landed)
-
-    def pass_on(self, way, turn):
-        here = self.here
-        source = self.quad if turn == 0 else self.full.at[here.z - way * turn, here.core]
-        target = self.full.at[here.z - way * turn, here.core]
-        partner = ((here.z + way) * 2 + here.core, here.member)
-        return self.wires.copy(turn + (3 if way < 0 else 0), source, target, partner)
-
-    def arrival(self, way, turn):
-        here = self.here
-        ref = self.full.at[here.z - way * (turn + 1), here.core]
-        return self.wires.copy(turn + (3 if way < 0 else 0), ref, ref, here.at_core())
-
-    def across(self, way, turn):
-        here = self.here
-        ref = self.full.at[here.z - way * (turn + 1), here.core]
-        return self.wires.copy(6 + turn + (3 if way < 0 else 0), ref, ref, here.at_core())
-
-    def own_across(self):
-        here = self.here
-        return self.wires.copy(12, self.quad, self.full.at[here.z, here.core], here.at_core())
-
-    def sends(self, way, turn):
-        z = self.here.z
-        return (z < 3) & (z >= turn) if way > 0 else (z > 0) & (z <= 3 - turn)
-
-    def comes(self, way, turn):
-        z = self.here.z
-        return z >= turn + 1 if way > 0 else z <= 2 - turn
-
-    def start(self, turn):
-        for way in (1, -1):
-            pl.when(self.sends(way, turn))(lambda way=way: self.pass_on(way, turn).start())
-        if turn == 0:
-            self.own_across().start()
-
-    def take(self, turn):
-        for way in (1, -1):
-
-            @pl.when(self.comes(way, turn))
-            def _():
-                self.arrival(way, turn).wait_recv()
-                self.across(way, turn).start()
-
-    def step(self, turn):
-        for way in (1, -1):
-
-            @pl.when(self.comes(way, turn - 1))
-            def _():
-                self.arrival(way, turn - 1).wait_recv()
-            if turn < 3:
-                pl.when(self.sends(way, turn))(lambda way=way: self.pass_on(way, turn).start())
-            pl.when(self.comes(way, turn - 1))(lambda way=way: self.across(way, turn - 1).start())
-
-    def end(self):
-        self.own_across().wait()
-        for way in (1, -1):
-            for turn in range(3):
-                pl.when(self.comes(way, turn))(lambda way=way, turn=turn: self.across(way, turn).wait())
-                pl.when(self.sends(way, turn))(lambda way=way, turn=turn: self.pass_on(way, turn).wait_send())
+    )(blocks, quad, parts, tokens)
 
 
 MIX_AT = 19
@@ -868,7 +880,7 @@
 
 
 def forward_kernel(
-    hidden_ref, weight_ref, bias_ref, latent_ref, scaling_ref, expand_bias_ref, expand_column, shrink_quad, incoming_ref,
+    hidden_ref, weight_ref, bias_ref, latent_ref, scaling_ref, expand_bias_ref, expand_column, shrink_given, shrink_column, incoming_ref,
     projected_ref, mixed_ref, log_ref, branch_ref, middle_ref, second_ref, pre_ref, active_ref,
     expand_full, shrink_full, incomings_ref,
     chunk, token_buffer, sent, landed, more_sent, more_landed, local, fetch,
@@ -880,15 +892,22 @@
         here,
         lambda member, z, core: expand_full.at[member, z, core],
         lambda z: expand_column.at[z],
-        sent,
-        landed,
-    )
-    third = Column(here, shrink_full, shrink_quad, more_sent.at[pl.ds(0, 13)], more_landed.at[pl.ds(0, 13)])
+        sent.at[0],
+        landed.at[0],
+    )
+    fourth = Gather(
+        here,
+        lambda member, z, core: shrink_full.at[z, core, member, LOW],
+        lambda z: shrink_column.at[z],
+        sent.at[1],
+        landed.at[1],
+    )
+    third = Column(here, shrink_full, None, more_sent.at[pl.ds(0, 13)], more_landed.at[pl.ds(0, 13)])
     more = Wires(more_sent, more_landed)
     own = (
         Bounce(expand_column, chunk.at[0, :, 0], expand_full.at[here.member, :, here.core], local.at[0]),
-        Bounce(shrink_quad, chunk.at[1, :, 0], shrink_full.at[here.z, here.core], local.at[1]),
-        Bounce(incoming_ref.at[here.member], token_buffer, incomings_ref.at[here.member], local.at[2]),
+        Bounce(incoming_ref.at[here.member], token_buffer, incomings_ref.at[here.member], local.at[1]),
+        Bounce(shrink_column, chunk.at[1, :, 0, LOW], shrink_full.at[:, here.core, here.member, LOW], local.at[2]),
     )
 
     def fetch_chunk(part):
@@ -905,7 +924,7 @@
         greet_near(here)
         for order in range(4):
             second.spread(order)
-        third.start(0)
+        third.step(1)
         for copy in own:
             copy.start()
 
@@ -917,6 +936,16 @@
     def relay_expand():
         for order in range(4):
             second.relay(order)
+
+    def spread_shrink():
+        for order in range(4):
+            fourth.spread(order)
+
+    def relay_shrink():
+        for order in range(4):
+            fourth.relay(order)
+
+    def start_moves():
         for number in (2, 1, 3):
             move(number).start()
 
@@ -932,16 +961,21 @@
         fetch_chunk(1).start()
 
     def finish():
-        third.step(3)
+        for order in range(4):
+            fourth.close(order)
         third.end()
+        fourth.end()
         for number in (1, 2, 3):
             move(number).wait()
 
     for turn, action in (
+        (10, functools.partial(third.step, 2)),
         (12, relay_expand),
-        (12, functools.partial(third.step, 1)),
-        (19, close_expand),
-        (EXPAND_AT + 1, functools.partial(third.step, 2)),
+        (14, spread_shrink),
+        (20, functools.partial(third.step, 3)),
+        (21, close_expand),
+        (EXPAND_AT - 1, start_moves),
+        (EXPAND_AT + 1, relay_shrink),
         (EXPAND_AT - 1, finish_expand),
     ):
         pl.when(step == turn)(action)
@@ -1038,7 +1072,7 @@
     )
 
 
-def forward(hidden, weights, biases, latents, scalings, expand_bias, expand_column, shrink_quad, incoming):
+def forward(hidden, weights, biases, latents, scalings, expand_bias, expand_column, shrink, shrink_column, incoming):
     rows, features = hidden.shape
 
     def clip(step, low, high):
@@ -1054,6 +1088,7 @@
     return pl.pallas_call(
         forward_kernel,
         grid=(FORWARD_STEPS,),
+        input_output_aliases={7: 9},
         in_specs=[
             everything((rows, features)),
             pl.BlockSpec((1, features, features), lambda step: (jnp.minimum(step, 3), 0, 0)),
@@ -1061,6 +1096,7 @@
             by_rows,
             everything((3, 1, features)),
             everything((4, 1, features)),
+            ANY,
             ANY,
             ANY,
             ANY,
@@ -1094,8 +1130,8 @@
         scratch_shapes=[
             pltpu.VMEM((2, 4, 2, ROWS, 1152), BF16),
             pltpu.VMEM(incoming.shape[1:], BF16),
-            pltpu.SemaphoreType.DMA((31,)),
-            pltpu.SemaphoreType.DMA((31,)),
+            pltpu.SemaphoreType.DMA((2, 31)),
+            pltpu.SemaphoreType.DMA((2, 31)),
             pltpu.SemaphoreType.DMA((16,)),
             pltpu.SemaphoreType.DMA((16,)),
             pltpu.SemaphoreType.DMA((3,)),
@@ -1104,53 +1140,56 @@
         compiler_params=pltpu.CompilerParams(
             collective_id=5, has_side_effects=True, vmem_limit_bytes=60 * 1024 * 1024
         ),
-    )(hidden, weights, biases, latents, scalings, expand_bias, expand_column, shrink_quad, incoming)
-
-
-class Reduce:
-    SCRATCH = (
-        pltpu.VMEM((4, 4, ROWS, 1152), BF16),
-        pltpu.VMEM((4, 4, ROWS, 1152), BF16),
-        pltpu.VMEM((2, 2, ROWS, 1152), BF16),
-        pltpu.VMEM((2, 4, ROWS, 1152), BF16),
-        pltpu.VMEM((3, ROWS, 1152), BF16),
-        pltpu.SemaphoreType.DMA((13,)),
-        pltpu.SemaphoreType.DMA((13,)),
-        pltpu.SemaphoreType.DMA((4,)),
-    )
-
-    def __init__(self, here, source, total, kept, crossed, relayed, beside, along, sent, landed, local):
-        self.here, self.source, self.total, self.local = here, source, total, local
+    )(hidden, weights, biases, latents, scalings, expand_bias, expand_column, shrink, shrink_column, incoming)
+
+
+class Half:
+    COPIES = 13
+
+    def __init__(self, here, rows, source, total, kept, crossed, relayed, beside, along, sent, landed, local):
+        self.here, self.rows, self.source, self.total, self.local = here, rows, source, total, local
         self.kept, self.crossed, self.relayed, self.beside, self.pieces = kept, crossed, relayed, beside, along
         self.wires = Wires(sent, landed)
         self.order = (here.across, here.across_x, here.across_y, here.member)
 
     def load(self, turn):
         return pltpu.make_async_copy(
-            self.source(self.order[turn], self.here.core), self.kept.at[turn], self.local.at[turn]
+            self.source(self.order[turn], self.here.core).at[:, self.rows],
+            self.kept.at[turn, :, self.rows],
+            self.local.at[turn],
         )
 
     def cross(self, turn):
         here = self.here
         return self.wires.copy(
-            turn, self.source(self.order[turn], 1 - here.core), self.crossed.at[turn], here.at_core()
+            turn,
+            self.source(self.order[turn], 1 - here.core).at[:, self.rows],
+            self.crossed.at[turn, :, self.rows],
+            here.at_core(),
         )
 
     def relay(self, way):
         partner = (self.here.at_x, self.here.at_y)[way]()
         half = pl.ds(2 - 2 * way, 2)
-        return self.wires.copy(4 + way, self.kept.at[0, half], self.relayed.at[way], partner)
+        return self.wires.copy(
+            4 + way, self.kept.at[0, half, self.rows], self.relayed.at[way, :, self.rows], partner
+        )
 
     def side(self, way, part):
         partner = (self.here.at_x, self.here.at_y)[way]()
         half = pl.ds(2 * part, 2)
         return self.wires.copy(
-            6 + 2 * way + part, self.kept.at[1 + way, half], self.beside.at[way, half], partner
+            6 + 2 * way + part,
+            self.kept.at[1 + way, half, self.rows],
+            self.beside.at[way, half, self.rows],
+            partner,
         )
 
     def along(self, step):
         z = lax.rem(self.here.z + step, 4)
-        return self.wires.copy(9 + step, self.kept.at[3, z], self.pieces.at[step - 1], self.here.at_z(step))
+        return self.wires.copy(
+            9 + step, self.kept.at[3, z, self.rows], self.pieces.at[step - 1, self.rows], self.here.at_z(step)
+        )
 
     def begin(self):
         for turn in range(4):
@@ -1162,15 +1201,17 @@
         self.cross(turn).wait_recv()
 
         def add(z, carry):
-            self.kept[turn, z] = (self.kept[turn, z].astype(F32) + self.crossed[turn, z].astype(F32)).astype(BF16)
+            mine = self.kept[turn, z, self.rows, :].astype(F32)
+            self.kept[turn, z, self.rows, :] = (mine + self.crossed[turn, z, self.rows, :].astype(F32)).astype(BF16)
             return carry
 
         lax.fori_loop(0, 4, add, 0)
 
     def add_relayed(self, turn, way, first):
         def add(z, carry):
-            self.kept[turn, first + z] = (
-                self.kept[turn, first + z].astype(F32) + self.relayed[way, z].astype(F32)
+            mine = self.kept[turn, first + z, self.rows, :].astype(F32)
+            self.kept[turn, first + z, self.rows, :] = (
+                mine + self.relayed[way, z, self.rows, :].astype(F32)
             ).astype(BF16)
             return carry
 
@@ -1181,30 +1222,26 @@
         self.relay(1).start()
         self.relay(0).start()
 
-    def direct_x(self):
+    def direct(self):
         self.add_crossed(1)
         self.side(0, 1).start()
-
-    def direct_y(self):
         self.add_crossed(2)
         self.side(1, 0).start()
-
-    def relay_x(self):
+        self.add_crossed(3)
+
+    def relays(self):
         self.relay(1).wait_recv()
         self.add_relayed(1, 1, 0)
         self.side(0, 0).start()
-
-    def relay_y(self):
         self.relay(0).wait_recv()
         self.add_relayed(2, 0, 2)
         self.side(1, 1).start()
 
-    def keep_own(self):
-        self.add_crossed(3)
-
     def three(self, z):
         return (
-            self.kept[3, z].astype(F32) + self.beside[0, z].astype(F32) + self.beside[1, z].astype(F32)
+            self.kept[3, z, self.rows, :].astype(F32)
+            + self.beside[0, z, self.rows, :].astype(F32)
+            + self.beside[1, z, self.rows, :].astype(F32)
         )
 
     def along_z(self):
@@ -1214,14 +1251,15 @@
                 self.side(way, part).wait_recv()
         for step in (2, 1, 3):
             z = lax.rem(here.z + step, 4)
-            self.kept[3, z] = self.three(z).astype(BF16)
+            self.kept[3, z, self.rows, :] = self.three(z).astype(BF16)
             self.along(step).start()
-        self.total[...] = self.three(here.z)
+        self.total[self.rows, :] = self.three(here.z)
 
     def finish(self):
         for step in (1, 3, 2):
             self.along(step).wait_recv()
-        self.total[...] += self.pieces[0].astype(F32) + self.pieces[1].astype(F32) + self.pieces[2].astype(F32)
+        pieces = [self.pieces[step, self.rows, :].astype(F32) for step in range(3)]
+        self.total[self.rows, :] += pieces[0] + pieces[1] + pieces[2]
         for turn in range(4):
             self.cross(turn).wait_send()
         for way in range(2):
@@ -1231,17 +1269,53 @@
         for step in range(1, 4):
             self.along(step).wait_send()
 
+
+class Reduce:
+    SCRATCH = (
+        pltpu.VMEM((4, 4, ROWS, 1152), BF16),
+        pltpu.VMEM((4, 4, ROWS, 1152), BF16),
+        pltpu.VMEM((2, 2, ROWS, 1152), BF16),
+        pltpu.VMEM((2, 4, ROWS, 1152), BF16),
+        pltpu.VMEM((3, ROWS, 1152), BF16),
+        pltpu.SemaphoreType.DMA((26,)),
+        pltpu.SemaphoreType.DMA((26,)),
+        pltpu.SemaphoreType.DMA((8,)),
+    )
+
+    def __init__(self, here, source, total, *scratch):
+        buffers, (sent, landed, local) = scratch[:5], scratch[5:]
+        self.halves = [
+            Half(
+                here,
+                rows,
+                source,
+                total,
+                *buffers,
+                sent.at[pl.ds(13 * part, 13)],
+                landed.at[pl.ds(13 * part, 13)],
+                local.at[pl.ds(4 * part, 4)],
+            )
+            for part, rows in enumerate((pl.ds(0, 80), pl.ds(80, 64)))
+        ]
+
+    def begin(self):
+        for half in self.halves:
+            half.begin()
+
     def steps(self):
+        first, second = self.halves
         return (
-            self.begin,
-            self.diagonal,
-            self.direct_x,
-            self.direct_y,
-            self.keep_own,
-            self.relay_x,
-            self.relay_y,
-            self.along_z,
-            self.finish,
+            (0.0, self.begin),
+            (0.11, first.diagonal),
+            (0.26, first.direct),
+            (0.26, first.relays),
+            (0.27, second.diagonal),
+            (0.56, second.direct),
+            (0.57, second.relays),
+            (0.58, first.along_z),
+            (0.84, second.along_z),
+            (1.0, first.finish),
+            (1.0, second.finish),
         )
 
 
@@ -1258,12 +1332,13 @@
         greet((here.at_x(), here.at_y(), here.at_core(), here.at_z(1), here.at_z(2), here.at_z(3)))
 
     steps = reduce.steps()
-    for step, turn in zip(steps[:-1], (0, 2, 6, 6, 6, 6, 6, 13)):
-        pl.when(head == turn)(step)
+    for share, action in steps[:-2]:
+        pl.when(head == round(share * HEADS))(action)
     attend_backward_kernel(
         query_ref, key_ref, value_ref, incoming_ref, log_ref, grad_ref, key_total, value_total
     )
-    pl.when(head == HEADS - 1)(steps[-1])
+    for _, action in steps[-2:]:
+        pl.when(head == HEADS - 1)(action)
 
 
 def attend_backward_reduce(projected, incoming, log_total, source):
@@ -1295,65 +1370,29 @@
 
 
 def turn_kernel(
-    active_ref, shrink_ref, middle_ref, incoming_ref, gate_ref, bias_ref,
-    tokens_ref, back_ref, grads_ref, sums_ref, total, token, sent, landed, local,
+    active_ref, shrink_ref, middle_ref, incoming_ref, gate_ref, bias_ref, token_ref, back_ref, grads_ref, sums_ref, total
 ):
     step = pl.program_id(0)
-    here = Here()
-    wires = Wires(sent, landed)
-
-    def move(number):
-        place = lax.rem(here.member + number, 4)
-        return wires.copy(number - 1, token.at[place], tokens_ref.at[here.member], here.at_member(number))
-
-    own = pltpu.make_async_copy(token.at[here.member], tokens_ref.at[here.member], local.at[0])
 
     @pl.when(step == 0)
     def _():
-        greet([here.at_member(number) for number in range(1, 4)])
         sums_ref[...] = jnp.zeros_like(sums_ref)
-
-    def blocks(body):
-        def one(block, carry):
-            body(pl.ds(pl.multiple_of(block * MATMUL_ROWS, MATMUL_ROWS), MATMUL_ROWS))
-            return carry
-
-        lax.fori_loop(0, total.shape[0] // MATMUL_ROWS, one, 0)
-
-    @pl.when(step == 0)
-    def _():
-        def first(rows):
-            total[rows, :] = dot_nn(active_ref[rows, :], shrink_ref[...])
-
-        blocks(first)
+        total[...] = dot_nn(active_ref[...], shrink_ref[...])
 
     @pl.when((step > 0) & (step < 4))
     def _():
-        def more(rows):
-            total[rows, :] += dot_nn(active_ref[rows, :], shrink_ref[...])
-
-        blocks(more)
+        total[...] += dot_nn(active_ref[...], shrink_ref[...])
 
     @pl.when((step >= 4) & (step < 8))
     def _():
         rows = pl.ds(pl.multiple_of((step - 4) * 256, 256), 256)
         branch = total[rows, :] + bias_ref[...]
         incoming = incoming_ref[0].astype(F32)
-        token[step - 4] = (middle_ref[...] + gate_ref[...] * branch).astype(BF16)
+        token_ref[0] = (middle_ref[...] + gate_ref[...] * branch).astype(BF16)
         back = (gate_ref[...] * incoming).astype(BF16)
         back_ref[rows, :] = back
         sums_ref[0:1, :] += jnp.sum(incoming * branch, axis=0, keepdims=True)
         sums_ref[1:2, :] += jnp.sum(back.astype(F32), axis=0, keepdims=True)
-
-    for number in range(1, 4):
-
-        @pl.when(step - 4 == lax.rem(here.member + number, 4))
-        def _():
-            move(number).start()
-
-    @pl.when(step - 4 == here.member)
-    def _():
-        own.start()
 
     @pl.when(step >= 8)
     def _():
@@ -1362,15 +1401,10 @@
             columns = slice(part * width, (part + 1) * width)
             grads_ref[0, columns, :] = dot_tn(active_ref[:, columns], back_ref[...]).astype(BF16)
 
-    @pl.when(step == 11)
-    def _():
-        for number in range(1, 4):
-            move(number).wait()
-        own.wait()
-
 
 def turn(active, shrink, middle, incoming, gate, bias):
     rows, features = middle.shape
+    by_member = pl.BlockSpec((1, 256, features), lambda step: (clipped(step, 4, 3), 0, 0))
     return pl.pallas_call(
         turn_kernel,
         grid=(12,),
@@ -1378,12 +1412,12 @@
             pl.BlockSpec((rows, features), lambda step: (0, jnp.where(step < 8, jnp.minimum(step, 3), step - 8))),
             pl.BlockSpec((features, features), lambda step: (jnp.minimum(step, 3), 0)),
             pl.BlockSpec((256, features), lambda step: (clipped(step, 4, 3), 0)),
-            pl.BlockSpec((1, 256, features), lambda step: (clipped(step, 4, 3), 0, 0)),
+            by_member,
             everything((1, features)),
             everything((1, features)),
         ],
         out_specs=[
-            ANY,
+            by_member,
             everything((rows, features)),
             pl.BlockSpec((1, features, features), lambda step: (clipped(step, 8, 3), 0, 0)),
             everything((8, features)),
@@ -1394,41 +1428,53 @@
             jax.ShapeDtypeStruct((4, features, features), BF16),
             jax.ShapeDtypeStruct((8, features), F32),
         ],
-        scratch_shapes=[
-            pltpu.VMEM((rows, features), F32),
-            pltpu.VMEM(incoming.shape, BF16),
-            pltpu.SemaphoreType.DMA((3,)),
-            pltpu.SemaphoreType.DMA((3,)),
-            pltpu.SemaphoreType.DMA((1,)),
-        ],
-        compiler_params=pltpu.CompilerParams(
-            collective_id=7, has_side_effects=True, vmem_limit_bytes=56 * 1024 * 1024
-        ),
+        scratch_shapes=[pltpu.VMEM((rows, features), F32)],
+        compiler_params=pltpu.CompilerParams(vmem_limit_bytes=56 * 1024 * 1024),
     )(active, shrink, middle, incoming, gate, bias)
 
 
 NORM_AT = 12
 BACK_STEPS = NORM_AT + 5
+BACK_SHARE = 13
 
 
 def back_kernel(
     back_ref, second_ref, pre_ref, shrink_ref, expand_ref, middle_ref, branch_ref, incoming_ref, mixed_ref, weight_ref,
-    scaling_ref, source_ref, expand_grad_ref, expand_sum_ref, middle_grad_ref, mixed_grad_ref, output_grad_ref, sums_ref,
-    block_ref, total, slope, branch_back, *scratch
+    scaling_ref, source_ref, token_ref,
+    expand_grad_ref, expand_sum_ref, middle_grad_ref, mixed_grad_ref, output_grad_ref, sums_ref, block_ref, tokens_ref,
+    total, slope, branch_back, buffer, sent, landed, local, *scratch
 ):
     step = pl.program_id(0)
     here = Here()
     reduce = Reduce(here, lambda member, core: source_ref.at[:, core, member], block_ref, *scratch)
 
+    wires = Wires(sent, landed)
+
+    def move(number):
+        place = lax.rem(here.member + number, 4)
+        return wires.copy(number - 1, token_ref.at[place], tokens_ref.at[here.member], here.at_member(number))
+
+    own = Bounce(token_ref.at[here.member], buffer, tokens_ref.at[here.member], local.at[0])
+
     @pl.when(step == 0)
     def _():
-        greet((here.at_x(), here.at_y(), here.at_core(), here.at_z(1), here.at_z(2), here.at_z(3)))
+        greet_near(here)
+        own.start()
         sums_ref[...] = jnp.zeros_like(sums_ref)
+
+    @pl.when(step == 9)
+    def _():
+        own.go_on()
+        for number in (2, 1, 3):
+            move(number).start()
+
+    @pl.when(step == 0)
+    def _():
         total[...] = jnp.zeros_like(total)
 
     steps = reduce.steps()
-    for action, turn in zip(steps[:-1], (0, 2, 5, 5, 5, 5, 5, 11)):
-        pl.when(step == turn)(action)
+    for share, action in steps[:-2]:
+        pl.when(step == round(share * BACK_SHARE))(action)
 
     @pl.when(step < NORM_AT)
     def _():
@@ -1467,12 +1513,19 @@
         width = mixed_ref.shape[1] // 3
         for part in range(3):
             columns = slice(part * width, (part + 1) * width)
-            output_grad_ref[columns, :] = dot_tn(mixed_ref[:, columns], branch_back[...]).astype(BF16)
-
-    pl.when(step == BACK_STEPS - 1)(steps[-1])
-
-
-def back(back_rows, second, pre, shrink, expand, middle, branch, incoming, mixed, weights, scalings, source):
+            output_grad_ref[0, columns, :] = dot_tn(mixed_ref[:, columns], branch_back[...]).astype(BF16)
+
+    for _, action in steps[-2:]:
+        pl.when(step == BACK_STEPS - 1)(action)
+
+    @pl.when(step == BACK_STEPS - 1)
+    def _():
+        for number in range(1, 4):
+            move(number).wait()
+        own.wait()
+
+
+def back(back_rows, second, pre, shrink, expand, middle, branch, incoming, mixed, weights, scalings, source, token):
     rows, features = middle.shape
     third = features // 3
     by_rows = pl.BlockSpec((256, features), lambda step: (clipped(step, NORM_AT, 3), 0))
@@ -1497,35 +1550,69 @@
             pl.BlockSpec((1, features, features), lambda step: (3, 0, 0), pipeline_mode=pl.Buffered(1)),
             everything((2, 1, features)),
             ANY,
+            ANY,
         ],
         out_specs=[
             pl.BlockSpec((1, features, third), lambda step: (piece(step) // 3, 0, piece(step) % 3)),
             pl.BlockSpec((1, 1, third), lambda step: (piece(step), 0, 0)),
             by_rows,
             by_rows,
-            everything((features, features)),
+            pl.BlockSpec((1, features, features), lambda step: (3, 0, 0), pipeline_mode=pl.Buffered(1)),
             everything((8, features)),
             everything((ROWS, features)),
+            ANY,
         ],
         out_shape=[
             jax.ShapeDtypeStruct((4, features, features), BF16),
             jax.ShapeDtypeStruct((NORM_AT, 1, third), F32),
             wide,
             jax.ShapeDtypeStruct((rows, features), BF16),
-            jax.ShapeDtypeStruct((features, features), BF16),
+            jax.ShapeDtypeStruct((4, features, features), BF16),
             jax.ShapeDtypeStruct((8, features), F32),
             jax.ShapeDtypeStruct((ROWS, features), F32),
+            jax.ShapeDtypeStruct(token.shape, BF16),
         ],
         scratch_shapes=[
             pltpu.VMEM((rows, features), F32),
             pltpu.VMEM((rows, third), BF16),
             pltpu.VMEM((rows, features), BF16),
+            pltpu.VMEM(token.shape[1:], BF16),
+            pltpu.SemaphoreType.DMA((3,)),
+            pltpu.SemaphoreType.DMA((3,)),
+            pltpu.SemaphoreType.DMA((1,)),
             *Reduce.SCRATCH,
         ],
         compiler_params=pltpu.CompilerParams(
             collective_id=8, has_side_effects=True, vmem_limit_bytes=60 * 1024 * 1024
         ),
-    )(back_rows, second, pre, shrink, expand, middle, branch, incoming, mixed, weights, scalings, source)
+    )(back_rows, second, pre, shrink, expand, middle, branch, incoming, mixed, weights, scalings, source, token)
+
+
+def triple_kernel(given_ref, hidden_ref, triple_ref, grad_ref, sums_ref):
+    width = hidden_ref.shape[1] // 3
+    for part in range(3):
+        columns = slice(part * width, (part + 1) * width)
+        grad_ref[0, columns, :] = dot_tn(hidden_ref[:, columns], triple_ref[...]).astype(BF16)
+    sums_ref[0] = jnp.sum(triple_ref[...].astype(F32), axis=0, keepdims=True)
+
+
+def triple_gradient(given, hidden, triple):
+    rows, features = hidden.shape
+    return pl.pallas_call(
+        triple_kernel,
+        grid=(3,),
+        in_specs=[ANY, everything((rows, features)), pl.BlockSpec((rows, features), lambda step: (0, step))],
+        out_specs=[
+            pl.BlockSpec((1, features, features), lambda step: (step, 0, 0)),
+            pl.BlockSpec((1, 1, features), lambda step: (step, 0, 0)),
+        ],
+        out_shape=[
+            jax.ShapeDtypeStruct(given.shape, BF16),
+            jax.ShapeDtypeStruct((3, 1, features), F32),
+        ],
+        input_output_aliases={0: 0},
+        compiler_params=pltpu.CompilerParams(vmem_limit_bytes=56 * 1024 * 1024),
+    )(given, hidden, triple)
 
 
 class Shares:
@@ -1602,16 +1689,18 @@
 
     for copy in loads:
         copy.wait()
+    first, second = reduce.halves
     sums = [compute(2)]
-    reduce.diagonal()
+    first.diagonal()
     sums.append(compute(1))
-    reduce.direct_x()
-    reduce.direct_y()
-    reduce.keep_own()
-    reduce.relay_x()
-    reduce.relay_y()
+    first.direct()
+    first.relays()
+    second.diagonal()
     sums.append(compute(3))
     sums.append(compute(0))
+    second.direct()
+    second.relays()
+    first.along_z()
     own = pltpu.make_async_copy(token.at[here.member], tokens_ref.at[here.member], local.at[5])
     own.start()
     wide[...] = vector_ref[...]
@@ -1624,10 +1713,11 @@
     rows_done = everyone(here, lambda place: row, rows_ref, row_sent, row_landed)
     own_row = pltpu.make_async_copy(row, rows_ref.at[here.index], local.at[6])
     own_row.start()
-    reduce.along_z()
+    second.along_z()
     for step in (2, 1, 3):
         move(step).start()
-    reduce.finish()
+    first.finish()
+    second.finish()
     shares.wait()
     for step in range(1, 4):
         move(step).wait()
@@ -1735,7 +1825,7 @@
     biases = (modulate_bias, triple_bias, output_bias, expand_bias, shrink_bias)
     note = jnp.concatenate([own_cond, *biases]).astype(F32)
     note = jnp.pad(note, (0, 1664 - note.shape[0])).reshape(1, 1, 1664)
-    notes, blocks, shrink_quad = introduce(note, shard, shrink_weight)
+    notes, blocks, shrink_quad, shrink_column = introduce(note, shard, shrink_weight)
     notes = notes.reshape(32, 1664)
     cond_act = jax.nn.silu(notes[:, :features]).astype(BF16)
     cuts = []
@@ -1748,8 +1838,8 @@
     act_owned = lax.dynamic_slice_in_dim(cond_act, me * owned, owned, axis=1)
     parts = pad_lanes(dot_nn(act_owned, modulate_weight), 56 * LANES).reshape(4, 2, 4, 56, LANES)
     parts = jnp.swapaxes(parts, 0, 1).reshape(2, 16, 56, LANES)
-    first_full, expand_column, parts, token_rows = open_up(
-        blocks, parts, latents.reshape(4, tokens, features)
+    first_full, expand_column, shrink_full, parts, token_rows = open_up(
+        blocks, shrink_quad, parts, latents.reshape(4, tokens, features)
     )
     first_full = first_full.reshape(4, features, features)
     modulation = jnp.sum(parts, axis=0).reshape(-1)[: 6 * features] + modulate_offset
@@ -1784,15 +1874,16 @@
         jnp.stack([gate_one, shift_two, scale_two]),
         expand_offset.reshape(4, 1, features),
         expand_column,
-        shrink_quad,
+        shrink_full,
+        shrink_column,
         cotangent.reshape(4, tokens, features),
     )
     expand_full = expand_full.reshape(4, features, features)
     shrink_full = shrink_full.reshape(hidden, features)
-    output, back_rows, shrink_grad, turn_sums = turn(
+    output_rows, back_rows, shrink_grad, turn_sums = turn(
         activated, shrink_full, middle, incoming, gate_two, shrink_offset[None]
     )
-    expand_grad, expand_offset_grad, middle_grad, mixed_grad, output_grad, back_sums, shrink_total = back(
+    expand_grad, expand_offset_grad, middle_grad, mixed_grad, first_grad, back_sums, shrink_total, output = back(
         back_rows,
         hidden_two,
         pre_act,
@@ -1805,17 +1896,15 @@
         first_full,
         jnp.stack([gate_one, scale_two]),
         shrink_grad.reshape(4, 2, 4, ROWS, features),
+        output_rows,
     )
     expand_grad = expand_grad.reshape(4, 4, 2, ROWS, features)
     gate_two_grad, shrink_offset_grad = turn_sums[0], turn_sums[1]
     gate_one_grad, output_offset_grad = back_sums[0], back_sums[3]
     triple_rows, expand_block = attend_backward_reduce(projected, mixed_grad, log_total, expand_grad)
-    column_sums = jnp.sum(triple_rows.astype(F32), axis=0)
-    triple_offset_grad = jnp.concatenate([column_sums[:features], column_sums[2 * features :]])
-    first_grad = jnp.stack(
-        [dot_tn(hidden_one, triple_rows[:, part * features : (part + 1) * features]).astype(BF16) for part in range(3)]
-        + [output_grad]
-    ).reshape(4, 4, 2, ROWS, features)
+    first_grad, column_sums = triple_gradient(first_grad, hidden_one, triple_rows)
+    first_grad = first_grad.reshape(4, 4, 2, ROWS, features)
+    triple_offset_grad = jnp.concatenate([column_sums[0, 0], column_sums[2, 0]])
     vectors = jnp.concatenate(
         [
             jnp.zeros((2 * features,), F32),

time: 671 us -> 629 us (0.937)
  Pallas kernels: 599 us -> 572 us
  matrix products: 15.2 us -> 2.77 us
  other arithmetic: 27.1 us -> 17.9 us
    pallas_call x1, Pallas kernels: 89.1 us -> 71.4 us  [attend_backward_reduce(): pl.pallas_call(backward_reduce_kernel, grid=(HEADS,), in_specs=[whole_blo...]
    pallas_call x2 -> x3, Pallas kernels: 210 us -> 224 us  [the longest x1 124 us: forward(): pl.pallas_call(forward_kernel, grid=(FORWARD_STEPS,), input_output_aliase...]
    dot_general x4 -> x1, matrix products: 14.6 us -> 2.17 us  [dot_tn(): lax.dot_general(left, right, (((0,), (0,)), ((), ())), preferred_element_...]
    pallas_call x1, Pallas kernels: 50.7 us -> 38.6 us  [turn(): pl.pallas_call(turn_kernel, grid=(12,), in_specs=[pl.BlockSpec((rows, fea...]
    pallas_call x1, Pallas kernels: 36.7 us -> 28.9 us  [introduce(): pl.pallas_call(introduce_kernel, in_specs=[ANY, ANY, ANY], out_specs=[ANY...]
where the time goes in v4:
time: 629 us; the launch traced here: 619 us
  Pallas kernels  572 us (91%)
  local copies, waits for them, and re-layouts  25.1 us (4%)
  other arithmetic  17.9 us (3%)
    pallas_call x1, Pallas kernels, forward(): pl.pallas_call(forward_kernel, grid=(FORWARD_STEPS,), input_output_aliase...  124 us
    pallas_call x1, Pallas kernels, close_down(): pl.pallas_call(close_kernel, in_specs=[ANY] * 5 + [whole, whole, ANY, who...  98.5 us
    pallas_call x1, Pallas kernels, back(): pl.pallas_call(back_kernel, grid=(BACK_STEPS,), in_specs=[everything((row...  93.6 us
    pallas_call x1, Pallas kernels, open_up(): pl.pallas_call(open_kernel, in_specs=[ANY] * 4, out_specs=[ANY] * 5, out_...  85.1 us
    pallas_call x1, Pallas kernels, attend_backward_reduce(): pl.pallas_call(backward_reduce_kernel, grid=(HEADS,), in_specs=[whole_blo...  71.4 us
    pallas_call x1, Pallas kernels, turn(): pl.pallas_call(turn_kernel, grid=(12,), in_specs=[pl.BlockSpec((rows, fea...  38.6 us
    pallas_call x1, Pallas kernels, introduce(): pl.pallas_call(introduce_kernel, in_specs=[ANY, ANY, ANY], out_specs=[ANY...  28.9 us
    pallas_call x1, Pallas kernels, swap(): pl.pallas_call(swap_kernel, in_specs=[ANY, pl.BlockSpec(memory_space=pltp...  17 us

profile of v4, /device:TPU:0, one launch (start us, length us, event | category | flops | bytes accessed | tf_op | source)
XLA Modules:
  0.0 619.1 jit_solution(7166672752902446067)
XLA Ops:
  1.5 3.4 concatenate.23
  5.5 1.0 maximum_bitcast_fusion
  6.6 2.0 fusion.4.shard_ref
  8.5 28.9 %shard_map.228 = (f32[32,1,1664]{2,1,0:T(1,128)}, bf16[2,144,1152]{2,1,0:T(8,128)(2,1)}, bf16[4,64,1152]{2,1,0:T(8,128)(2,1)}, bf16[4,80,1152]{2,1,0:T(8,128)(2,1)}) custom-call(f32[1,1,1664]{2,1,0:T(1,128)} %reshape.192.note_ref, bf16[2,48,4608]{2,1,0:T(8,128)(2,1)} %fusion.4.shard_ref, bf16[144,1152]{1,0:T(8,128)(2,1)} %shrink_ref.1), custom_call_target="tpu_custom_call" | custom-call | tf_op jit(solution)/shard_map/pallas_call | solution.py:598
  37.4 0.9 copy.44
  39.7 1.0 copy.29
  40.7 85.1 %shard_map.229 = (bf16[4,4,2,144,1152]{4,3,2,1,0:T(8,128)(2,1)}, bf16[4,144,1152]{2,1,0:T(8,128)(2,1)}, bf16[4,2,4,144,1152]{4,3,2,1,0:T(8,128)(2,1)}, f32[16,56,128]{2,1,0:T(8,128)}, bf16[4,256,1152]{2,1,0:T(8,128)(2,1)}) custom-call(bf16[2,144,1152]{2,1,0:T(8,128)(2,1)} %get-tuple-element.56.block_ref, bf16[4,64,1152]{2,1,0:T(8,128)(2,1)} %get-tuple-element.57.quad_ref, ...), custom_call_target="tpu_custom_call" | custom-call | tf_op jit(solution)/shard_map/pallas_call | solution.py:848
  125.8 1.2 reduce_sum.49
  128.4 2.0 convert_reduce_fusion
  131.3 2.4 add_convert_fusion.hidden_ref
  135.7 124.5 %shard_map.230 = (bf16[1024,3456]{1,0:T(8,128)(2,1)}, bf16[1024,1152]{1,0:T(8,128)(2,1)}, f32[16,1,1024]{2,1,0:T(1,128)}, f32[1024,1152]{1,0:T(8,128)}, f32[1024...) custom-call(bf16[1024,1152]{1,0:T(8,128)(2,1)} %add_convert_fusion.h, ...), custom_call_target="tpu_custom_call", output_to_operand_aliasing={{9}: (7, {})} | custom-call | tf_op jit(solution)/shard_map/pallas_call | solution.py:1088
  260.9 38.6 %shard_map.231 = (bf16[4,256,1152]{2,1,0:T(8,128)(2,1)}, bf16[1024,1152]{1,0:T(8,128)(2,1)}, bf16[4,1152,1152]{2,1,0:T(8,128)(2,1)}, f32[8,1152]{1,0:T(8,128)}) custom-call(bf16[1024,4608]{1,0:T(8,128)(2,1)} %get-tuple-element.65.active_ref, bf16[4608,1152]{1,0:T(8,128)(2,1)} %bitcast.74, f32[1024,1152]{1,0:T(8,128)} %get-tuple-element.67.middle_ref, ...), custom_call_target="tpu_custom_call" | custom-call | tf_op jit(solution)/shard_map/pallas_call | solution.py:1408
  300.1 93.6 %shard_map.232 = (bf16[4,1152,1152]{2,1,0:T(8,128)(2,1)}, f32[12,1,384]{2,1,0:T(1,128)}, f32[1024,1152]{1,0:T(8,128)}, bf16[1024,1152]{1,0:T(8,128)(2,1)}, bf16[...) custom-call(bf16[1024,1152]{1,0:T(8,128)(2,1)} %get-tuple-element.69.back_re, ...), custom_call_target="tpu_custom_call" | custom-call | tf_op jit(solution)/shard_map/pallas_call | solution.py:1537
  393.7 71.4 %shard_map.233 = (bf16[1024,3456]{1,0:T(8,128)(2,1)}, f32[144,1152]{1,0:T(8,128)}) custom-call(bf16[1024,3456]{1,0:T(8,128)(2,1)} %get-tuple-element.79.query_ref.key_ref.value_ref, bf16[1024,3456]{1,0:T(8,128)(2,1)} %get-tuple-element.79.query_ref.key_ref.value_ref, bf16[1024,3456]{1,0:T(8,128)(2,1)} %get-tuple-element.79.query_ref.key_ref.value_ref, ...), custom_call_target="tpu_custom_call" | custom-call | tf_op jit(solution)/shard_map/pallas_call | solution.py:1347
  465.2 14.5 %shard_map.234 = (bf16[4,1152,1152]{2,1,0:T(8,128)(2,1)}, f32[3,1,1152]{2,1,0:T(1,128)}) custom-call(bf16[4,1152,1152]{2,1,0:T(8,128)(2,1)} %get-tuple-element.78.given_ref, bf16[1024,1152]{1,0:T(8,128)(2,1)} %add_convert_fusion.hidden_ref, bf16[1024,3456]{1,0:T(8,128)(2,1)} %get-tuple-element.83.triple_ref), custom_call_target="tpu_custom_call", output_to_operand_aliasing={{0}: (0, {})} | custom-call | tf_op jit(solution)/shard_map/pallas_call | solution.py:1601
  483.3 98.5 %shard_map.235 = (f32[144,1152]{1,0:T(8,128)}, bf16[4,256,1152]{2,1,0:T(8,128)(2,1)}, bf16[32,64,128]{2,1,0:T(8,128)(2,1)}, f32[32,8,128]{2,1,0:T(8,128)}, f32[4,40,1152]{2,1,0:T(8,128)}) custom-call(bf16[4,4,2,144,1152]{4,3,2,1,0:T(8,128)(2,1)} %bitcast.78, bf16[1024,3456]{1,0:T(8,128)(2,1)} %get-tuple-element.83.triple_ref, ...), custom_call_target="tpu_custom_call" | custom-call | tf_op jit(solution)/shard_map/pallas_call | solution.py:1734
  581.9 1.5 copy.43
  584.3 17.0 %shard_map.236 = (f32[32,8,128]{2,1,0:T(8,128)}, f32[4,40,1152]{2,1,0:T(8,128)}) custom-call(f32[8,8,128]{2,1,0:T(8,128)} %pad.25.part_ref, f32[144,1152]{1,0:T(8,128)} %get-tuple-element.93.block_ref), custom_call_target="tpu_custom_call" | custom-call | tf_op jit(solution)/shard_map/pallas_call | solution.py:1779
  601.3 1.9 slice_bitcast_fusion.1
  605.8 2.2 fusion.14
  608.0 2.5 convert.4
  612.5 1.4 convert_reduce_fusion.1
  613.9 0.9 reduce_sum.51
  616.6 1.4 copy.55
  (87 shorter events, 19.8 us)
Async XLA Ops:
  0.6 38.4 %copy-start = (bf16[36,6912]{1,0:T(8,128)(2,1)S(1)}, bf16[36,6912]{1,0:T(8,128)(2,1)}, u32[]{:S(2)}) copy-start(bf16[36,6912]{1,0:T(8,128)(2,1)} %param.16) | copy-start | bytes 1492996
  38.4 0.7 copy-start.6
  125.8 4.7 copy-start.1
  465.1 15.4 %copy-start.9 = (f32[12,1,384]{2,1,0:T(1,128)S(1)}, f32[12,1,384]{2,1,0:T(1,128)}, u32[]{:S(2)}) copy-start(f32[12,1,384]{2,1,0:T(1,128)} %get-tuple-element.89) | copy-start | bytes 55300
  465.2 15.5 %copy-start.10 = (f32[8,1152]{1,0:T(8,128)S(1)}, f32[8,1152]{1,0:T(8,128)}, u32[]{:S(2)}) copy-start(f32[8,1152]{1,0:T(8,128)} %get-tuple-element.86) | copy-start | bytes 110596
  482.7 0.6 copy-start.8
  581.9 23.3 %copy-start.7 = (bf16[2,2,1152]{2,1,0:T(2,128)(2,1)S(1)}, bf16[2,2,1152]{2,1,0:T(2,128)(2,1)}, u32[]{:S(2)}) copy-start(bf16[2,2,1152]{2,1,0:T(2,128)(2,1)} %param.14) | copy-start | bytes 27652
  581.9 26.1 %copy-start.2 = (bf16[4,256,1152]{2,1,0:T(8,128)(2,1)S(1)}, bf16[4,256,1152]{2,1,0:T(8,128)(2,1)}, u32[]{:S(2)}) copy-start(bf16[4,256,1152]{2,1,0:T(8,128)(2,1)} %get-tuple-element.91) | copy-start | bytes 7077892
  605.1 5.3 copy-start.4
  610.5 6.1 copy-start.3
  614.9 3.1 copy-start.5

commit v5 on v4

--- a/solution.py
+++ b/solution.py
@@ -970,12 +970,12 @@
 
     for turn, action in (
         (10, functools.partial(third.step, 2)),
-        (12, relay_expand),
-        (14, spread_shrink),
+        (13, relay_expand),
+        (19, spread_shrink),
         (20, functools.partial(third.step, 3)),
         (21, close_expand),
-        (EXPAND_AT - 1, start_moves),
-        (EXPAND_AT + 1, relay_shrink),
+        (1, start_moves),
+        (EXPAND_AT + 2, relay_shrink),
         (EXPAND_AT - 1, finish_expand),
     ):
         pl.when(step == turn)(action)

time: 629 us -> 624 us (level)
  no operation moved by 1% of the time
where the time goes in v5:
time: 624 us; the launch traced here: 614 us
  Pallas kernels  567 us (91%)
  local copies, waits for them, and re-layouts  25.1 us (4%)
  other arithmetic  17.9 us (3%)
    pallas_call x1, Pallas kernels, forward(): pl.pallas_call(forward_kernel, grid=(FORWARD_STEPS,), input_output_aliase...  119 us
    pallas_call x1, Pallas kernels, close_down(): pl.pallas_call(close_kernel, in_specs=[ANY] * 5 + [whole, whole, ANY, who...  95 us
    pallas_call x1, Pallas kernels, back(): pl.pallas_call(back_kernel, grid=(BACK_STEPS,), in_specs=[everything((row...  93.4 us
    pallas_call x1, Pallas kernels, open_up(): pl.pallas_call(open_kernel, in_specs=[ANY] * 4, out_specs=[ANY] * 5, out_...  85.1 us
    pallas_call x1, Pallas kernels, attend_backward_reduce(): pl.pallas_call(backward_reduce_kernel, grid=(HEADS,), in_specs=[whole_blo...  75.6 us
    pallas_call x1, Pallas kernels, turn(): pl.pallas_call(turn_kernel, grid=(12,), in_specs=[pl.BlockSpec((rows, fea...  38.6 us
    pallas_call x1, Pallas kernels, introduce(): pl.pallas_call(introduce_kernel, in_specs=[ANY, ANY, ANY], out_specs=[ANY...  28.9 us
    pallas_call x1, Pallas kernels, swap(): pl.pallas_call(swap_kernel, in_specs=[ANY, pl.BlockSpec(memory_space=pltp...  17.1 us

profile of v5, /device:TPU:0, one launch (start us, length us, event | category | flops | bytes accessed | tf_op | source)
XLA Modules:
  0.0 614.3 jit_solution(12451440707649273487)
XLA Ops:
  1.5 3.4 concatenate.23
  5.5 1.0 maximum_bitcast_fusion
  6.6 2.0 fusion.4.shard_ref
  8.5 28.9 %shard_map.228 = (f32[32,1,1664]{2,1,0:T(1,128)}, bf16[2,144,1152]{2,1,0:T(8,128)(2,1)}, bf16[4,64,1152]{2,1,0:T(8,128)(2,1)}, bf16[4,80,1152]{2,1,0:T(8,128)(2,1)}) custom-call(f32[1,1,1664]{2,1,0:T(1,128)} %reshape.192.note_ref, bf16[2,48,4608]{2,1,0:T(8,128)(2,1)} %fusion.4.shard_ref, bf16[144,1152]{1,0:T(8,128)(2,1)} %shrink_ref.1), custom_call_target="tpu_custom_call" | custom-call | tf_op jit(solution)/shard_map/pallas_call | solution.py:598
  37.4 0.9 copy.44
  39.7 1.0 copy.29
  40.7 85.1 %shard_map.229 = (bf16[4,4,2,144,1152]{4,3,2,1,0:T(8,128)(2,1)}, bf16[4,144,1152]{2,1,0:T(8,128)(2,1)}, bf16[4,2,4,144,1152]{4,3,2,1,0:T(8,128)(2,1)}, f32[16,56,128]{2,1,0:T(8,128)}, bf16[4,256,1152]{2,1,0:T(8,128)(2,1)}) custom-call(bf16[2,144,1152]{2,1,0:T(8,128)(2,1)} %get-tuple-element.56.block_ref, bf16[4,64,1152]{2,1,0:T(8,128)(2,1)} %get-tuple-element.57.quad_ref, ...), custom_call_target="tpu_custom_call" | custom-call | tf_op jit(solution)/shard_map/pallas_call | solution.py:848
  125.8 1.2 reduce_sum.49
  128.4 2.0 convert_reduce_fusion
  131.3 2.4 add_convert_fusion.hidden_ref
  135.7 119.1 %shard_map.230 = (bf16[1024,3456]{1,0:T(8,128)(2,1)}, bf16[1024,1152]{1,0:T(8,128)(2,1)}, f32[16,1,1024]{2,1,0:T(1,128)}, f32[1024,1152]{1,0:T(8,128)}, f32[1024...) custom-call(bf16[1024,1152]{1,0:T(8,128)(2,1)} %add_convert_fusion.h, ...), custom_call_target="tpu_custom_call", output_to_operand_aliasing={{9}: (7, {})} | custom-call | tf_op jit(solution)/shard_map/pallas_call | solution.py:1088
  255.5 38.6 %shard_map.231 = (bf16[4,256,1152]{2,1,0:T(8,128)(2,1)}, bf16[1024,1152]{1,0:T(8,128)(2,1)}, bf16[4,1152,1152]{2,1,0:T(8,128)(2,1)}, f32[8,1152]{1,0:T(8,128)}) custom-call(bf16[1024,4608]{1,0:T(8,128)(2,1)} %get-tuple-element.65.active_ref, bf16[4608,1152]{1,0:T(8,128)(2,1)} %bitcast.74, f32[1024,1152]{1,0:T(8,128)} %get-tuple-element.67.middle_ref, ...), custom_call_target="tpu_custom_call" | custom-call | tf_op jit(solution)/shard_map/pallas_call | solution.py:1408
  294.7 93.4 %shard_map.232 = (bf16[4,1152,1152]{2,1,0:T(8,128)(2,1)}, f32[12,1,384]{2,1,0:T(1,128)}, f32[1024,1152]{1,0:T(8,128)}, bf16[1024,1152]{1,0:T(8,128)(2,1)}, bf16[...) custom-call(bf16[1024,1152]{1,0:T(8,128)(2,1)} %get-tuple-element.69.back_re, ...), custom_call_target="tpu_custom_call" | custom-call | tf_op jit(solution)/shard_map/pallas_call | solution.py:1537
  388.1 75.6 %shard_map.233 = (bf16[1024,3456]{1,0:T(8,128)(2,1)}, f32[144,1152]{1,0:T(8,128)}) custom-call(bf16[1024,3456]{1,0:T(8,128)(2,1)} %get-tuple-element.79.query_ref.key_ref.value_ref, bf16[1024,3456]{1,0:T(8,128)(2,1)} %get-tuple-element.79.query_ref.key_ref.value_ref, bf16[1024,3456]{1,0:T(8,128)(2,1)} %get-tuple-element.79.query_ref.key_ref.value_ref, ...), custom_call_target="tpu_custom_call" | custom-call | tf_op jit(solution)/shard_map/pallas_call | solution.py:1347
  463.8 14.5 %shard_map.234 = (bf16[4,1152,1152]{2,1,0:T(8,128)(2,1)}, f32[3,1,1152]{2,1,0:T(1,128)}) custom-call(bf16[4,1152,1152]{2,1,0:T(8,128)(2,1)} %get-tuple-element.78.given_ref, bf16[1024,1152]{1,0:T(8,128)(2,1)} %add_convert_fusion.hidden_ref, bf16[1024,3456]{1,0:T(8,128)(2,1)} %get-tuple-element.83.triple_ref), custom_call_target="tpu_custom_call", output_to_operand_aliasing={{0}: (0, {})} | custom-call | tf_op jit(solution)/shard_map/pallas_call | solution.py:1601
  481.9 95.0 %shard_map.235 = (f32[144,1152]{1,0:T(8,128)}, bf16[4,256,1152]{2,1,0:T(8,128)(2,1)}, bf16[32,64,128]{2,1,0:T(8,128)(2,1)}, f32[32,8,128]{2,1,0:T(8,128)}, f32[4,40,1152]{2,1,0:T(8,128)}) custom-call(bf16[4,4,2,144,1152]{4,3,2,1,0:T(8,128)(2,1)} %bitcast.78, bf16[1024,3456]{1,0:T(8,128)(2,1)} %get-tuple-element.83.triple_ref, ...), custom_call_target="tpu_custom_call" | custom-call | tf_op jit(solution)/shard_map/pallas_call | solution.py:1734
  577.0 1.5 copy.43
  579.4 17.1 %shard_map.236 = (f32[32,8,128]{2,1,0:T(8,128)}, f32[4,40,1152]{2,1,0:T(8,128)}) custom-call(f32[8,8,128]{2,1,0:T(8,128)} %pad.25.part_ref, f32[144,1152]{1,0:T(8,128)} %get-tuple-element.93.block_ref), custom_call_target="tpu_custom_call" | custom-call | tf_op jit(solution)/shard_map/pallas_call | solution.py:1779
  596.6 1.9 slice_bitcast_fusion.1
  601.0 2.2 fusion.14
  603.2 2.5 convert.4
  607.8 1.4 convert_reduce_fusion.1
  609.2 0.9 reduce_sum.51
  611.8 1.4 copy.55
  (87 shorter events, 19.8 us)
Async XLA Ops:
  0.6 38.4 %copy-start = (bf16[36,6912]{1,0:T(8,128)(2,1)S(1)}, bf16[36,6912]{1,0:T(8,128)(2,1)}, u32[]{:S(2)}) copy-start(bf16[36,6912]{1,0:T(8,128)(2,1)} %param.16) | copy-start | bytes 1492996
  38.4 0.7 copy-start.6
  125.8 4.7 copy-start.1
  463.7 15.4 %copy-start.9 = (f32[12,1,384]{2,1,0:T(1,128)S(1)}, f32[12,1,384]{2,1,0:T(1,128)}, u32[]{:S(2)}) copy-start(f32[12,1,384]{2,1,0:T(1,128)} %get-tuple-element.89) | copy-start | bytes 55300
  463.8 15.5 %copy-start.10 = (f32[8,1152]{1,0:T(8,128)S(1)}, f32[8,1152]{1,0:T(8,128)}, u32[]{:S(2)}) copy-start(f32[8,1152]{1,0:T(8,128)} %get-tuple-element.86) | copy-start | bytes 110596
  481.3 0.6 copy-start.8
  576.9 23.4 %copy-start.7 = (bf16[2,2,1152]{2,1,0:T(2,128)(2,1)S(1)}, bf16[2,2,1152]{2,1,0:T(2,128)(2,1)}, u32[]{:S(2)}) copy-start(bf16[2,2,1152]{2,1,0:T(2,128)(2,1)} %param.14) | copy-start | bytes 27652
  577.0 26.2 %copy-start.2 = (bf16[4,256,1152]{2,1,0:T(8,128)(2,1)S(1)}, bf16[4,256,1152]{2,1,0:T(8,128)(2,1)}, u32[]{:S(2)}) copy-start(bf16[4,256,1152]{2,1,0:T(8,128)(2,1)} %get-tuple-element.91) | copy-start | bytes 7077892
  600.4 5.3 copy-start.4
  605.7 6.1 %copy-start.3 = (bf16[4,256,1152]{2,1,0:T(8,128)(2,1)S(1)}, bf16[4,256,1152]{2,1,0:T(8,128)(2,1)}, u32[]{:S(2)}) copy-start(bf16[4,256,1152]{2,1,0:T(8,128)(2,1)} %get-tuple-element.77) | copy-start | bytes 7077892
  610.1 3.1 copy-start.5
